TPU v7x, 256 devices: a whole 4x4x8 slice. The times are simulated.
256 devices in a mesh: dap: 64 (over z, y, core), grp: 4 (over x).
Axes of the slice: x: 4, y: 4, z: 8, core: 2. Of those that a mesh axis runs over, the one named last changes fastest.
Arguments:
- homolog_stack: bfloat16 [256, 768, 256], P(None, 'dap'), may hold values from -6 to 6
- couple_embedding: bfloat16 [768, 768, 128], P('dap', 'grp'), may hold values from -3 to 3
- dyad_entry_matrix: bfloat16 [256, 64], replicated, may hold values from -0.375 to 0.375
- dyad_final_matrix: bfloat16 [1024, 128], replicated, may hold values from -0.75 to 0.75
- query_key_gate_matrix: bfloat16 [128, 512], replicated, may hold values from -0.5 to 0.5
- couple_offset_matrix: float32 [128, 4], replicated, may hold values from -24 to 24
- softmax_final_matrix: bfloat16 [128, 128], replicated, may hold values from -2 to 2
- strand_couple_filter: int32 [6, 6], replicated, may hold values from 0 to 1, as said below
Outputs:
- pair_mid: bfloat16 [768, 768, 128], P('dap', 'grp')
- tri_update: bfloat16 [768, 768, 128], P('dap', 'grp')
Inputs may be any that keep to these rules, and one draw needn't show every extreme that they name: `strand_couple_filter`: Symmetric, with every diagonal tile 1.
All inputs are finite; a program needn't handle non-finite values.
Results may differ from a plain program's by a relative error of at most 0.025.
Values may be sent and summed in bfloat16 or wider, within the bound.
No kernel may reach another device: no remote copies, remote signals or barrier semaphores. Data moves between devices by JAX's collectives and lax.ppermute only.
A program may use at most 128 MiB of HBM per device.

v0:
```python
import jax
import jax.numpy as jnp
from jax import lax
from jax.experimental import pallas as pl
from jax.experimental.pallas import tpu as pltpu
from jax.sharding import PartitionSpec as P

BF = jnp.bfloat16
F32 = jnp.float32
NT = (((1,), (1,)), ((), ()))
NN = (((1,), (0,)), ((), ()))

ROWS, COLS, CH, HEADS, HD = 12, 192, 128, 4, 32
MSA, PF = 256, 32
BLK = ROWS * PF
LANES = 128
HALF = COLS - LANES
PAY = HEADS * ROWS
LOG2E = 1.4426950408889634
TILES, TILE = 6, 128


def ring(n, k):
    return [(i, (i + k) % n) for i in range(n)]


def dot(a, b, dims):
    return lax.dot_general(a, b, dims, preferred_element_type=F32)


PIECES = [
    (z, y, c) for c in range(2) for (z, y) in ((0, 0), (1, 0), (0, 1), (0, 3), (0, 2), (1, 1), (1, 3), (1, 2))
]


def by_channel(res, lhs, t):
    low = lax.broadcasted_iota(jnp.int32, (PF // 2, 8, LANES), 1) < 4
    for q in range(3):
        part = res[:, q * LANES : (q + 1) * LANES]
        tiles = []
        for k in range(2):
            a, b = [], []
            for c in range(2):
                base = (2 * k + c) * BLK
                a.append(part[base : base + 8 * PF].reshape(PF, 8, LANES))
                b.append(part[base + 8 * PF : base + BLK].reshape(PF // 2, 8, LANES))
            even = jnp.where(low, b[0], jnp.roll(b[1], 4, axis=1))
            odd = jnp.where(low, jnp.roll(b[0], 4, axis=1), b[1])
            tiles.append((a[0], a[1], (even, odd)))
        rows = pl.multiple_of(q * COLS + t * 4 * ROWS, 16)
        for ch in range(PF):
            six = []
            for a0, a1, eo in tiles:
                six += [a0[ch], a1[ch], eo[ch % 2][ch // 2]]
            lhs[pl.ds(rows, 4 * ROWS), ch * LANES : (ch + 1) * LANES] = jnp.concatenate(six, axis=0).astype(BF)


def natural(acc):
    n = acc.shape[1]
    p = acc.reshape(8, 3, 8, n)
    low = lax.broadcasted_iota(jnp.int32, (8, 8, n), 1) < 4
    r = jnp.roll(p[:, 1], 4, axis=1)
    mid = jnp.where(low, p[:, 2], r)
    last = jnp.where(low, r, p[:, 2])
    return jnp.concatenate([p[:, 0:1], mid[:, None], last[:, None]], axis=1).reshape(COLS, n)


def opm_kernel(pos_ref, lt_ref, *refs):
    pieces = refs[: len(PIECES)]
    (w_ref, emb_ref, off_ref, mid_ref, norm_ref, bias_ref) = refs[len(PIECES) : len(PIECES) + 6]
    (right, lhs, wblk, brow, sems) = refs[len(PIECES) + 6 :]
    zl, y, c = pos_ref[0], pos_ref[1], pos_ref[2]
    copies = []
    for n, (dz, dy, dc) in enumerate(PIECES):
        src_z = lax.rem(zl + dz, 2)
        src_y = lax.rem(y + 4 - dy, 4)
        src_c = lax.rem(c + dc, 2)
        start = (src_z * 8 + src_y * 2 + src_c) * BLK
        cp = pltpu.make_async_copy(
            pieces[n], right.at[pl.ds(pl.multiple_of(start, 128), BLK)], sems.at[n]
        )
        cp.start()
        copies.append(cp)

    def build(ch, carry):
        base = pl.multiple_of(ch * LANES, LANES)
        wy = w_ref[ch]
        zero = jnp.zeros((PF, CH), BF)
        for r in range(4):
            for t in range(4):
                wblk[pl.ds(base + r * PF, PF), t * CH : (t + 1) * CH] = wy if r == t else zero
        return carry

    lax.fori_loop(0, PF, build, 0)
    for cp in copies:
        cp.wait()

    def first(t, carry):
        rows = pl.multiple_of(t * 4 * BLK, 4 * BLK)
        by_channel(dot(right[pl.ds(rows, 4 * BLK), :], lt_ref[...], NT), lhs, t)
        return carry

    lax.fori_loop(0, 4, first, 0)
    w = off_ref[...]
    w_hi = w.astype(BF)
    rest = w - w_hi.astype(F32)
    w_mid = rest.astype(BF)
    w_lo = (rest - w_mid.astype(F32)).astype(BF)
    w3 = jnp.concatenate([w_hi, w_mid, w_lo], axis=0)
    for q in range(3):
        update = natural(dot(lhs[q * COLS : (q + 1) * COLS, :], wblk[...], NN)) * (1.0 / MSA)
        for r in range(4):
            i = 4 * q + r
            mid = (emb_ref[i].astype(F32) + update[:, r * CH : (r + 1) * CH]).astype(BF)
            mid_ref[i] = mid
            wide = mid.astype(F32)
            cen = wide - jnp.mean(wide, axis=-1, keepdims=True)
            var = jnp.mean(cen * cen, axis=-1, keepdims=True)
            nrm = (cen * lax.rsqrt(var + 1e-05)).astype(BF)
            norm_ref[i] = nrm
            parts = dot(w3, nrm, NT)
            brow[i] = parts[0:8] + parts[8:16] + parts[16:24]
    for h in range(HEADS):
        b = brow[:, h, :]
        done = []
        tops = []
        for g in range(3):
            part = b[:, g * HALF : (g + 1) * HALF]
            top = jnp.max(part, axis=-1, keepdims=True).astype(BF).astype(F32)
            done.append(part - top)
            tops.append(top)
        lane = lax.broadcasted_iota(jnp.int32, (ROWS, HALF), 1)
        tail = jnp.where(lane == 0, tops[0], jnp.where(lane == 1, tops[1], tops[2]))
        bias_ref[h * ROWS : (h + 1) * ROWS, :] = jnp.concatenate(done + [tail], axis=1).astype(BF)


VMEM = pl.BlockSpec(memory_space=pltpu.VMEM)
SMEM = pl.BlockSpec(memory_space=pltpu.SMEM)
ANY = pl.BlockSpec(memory_space=pl.ANY)
PARAMS = pltpu.CompilerParams(vmem_limit_bytes=56 * 1024 * 1024)


def opm(pos, left, pieces, w, emb, off):
    return pl.pallas_call(
        opm_kernel,
        out_shape=(
            jax.ShapeDtypeStruct((ROWS, COLS, CH), BF),
            jax.ShapeDtypeStruct((ROWS, COLS, CH), BF),
            jax.ShapeDtypeStruct((PAY, 2 * LANES), BF),
        ),
        in_specs=[SMEM, VMEM] + [ANY] * len(PIECES) + [VMEM] * 3,
        out_specs=[VMEM] * 3,
        scratch_shapes=[
            pltpu.VMEM((16 * BLK, MSA), BF),
            pltpu.VMEM((3 * COLS, PF * LANES), BF),
            pltpu.VMEM((PF * LANES, 4 * CH), BF),
            pltpu.VMEM((ROWS, 8, COLS), F32),
            pltpu.SemaphoreType.DMA((len(PIECES),)),
        ],
        compiler_params=PARAMS,
        cost_estimate=pl.CostEstimate(flops=6 * 10**9, bytes_accessed=10**7, transcendentals=0),
        name="opm",
    )(pos, left, *pieces, w, emb, off)


def attend_kernel(
    pos_ref, filt_ref, own_ref, prev_ref, next_ref, far_ref, pay0_ref, pay1_ref,
    wqg_ref, wkv_ref, wo_ref, out_ref, bias,
):
    i = pl.program_id(0)
    z, y, c, x = pos_ref[0], pos_ref[1], pos_ref[2], pos_ref[3]

    @pl.when(i == 0)
    def _():
        first_lane = lax.broadcasted_iota(jnp.int32, (PAY, LANES), 1) < HALF

        def place(pair, carry):
            row0 = pl.multiple_of(pair * 2 * ROWS, 8)
            src_z = pair // 4
            src_y = lax.rem(pair, 4)
            dy = lax.rem(y + 4 - src_y, 4)
            tails = []
            for rel, shift in enumerate((0, 3, 1, 2)):
                zh = lax.rem(x + shift, 4)
                dz = lax.rem(z + 8 - zh * 2 - src_z, 8)
                at = dy * 8 + dz
                p0 = pay0_ref[at].astype(F32) * LOG2E
                p1 = pay1_ref[at].astype(F32) * LOG2E
                heads = []
                for p in (jnp.where(c == 0, p0, p1), jnp.where(c == 0, p1, p0)):
                    m = COLS
                    heads.append(
                        p[:, :LANES] + jnp.where(first_lane, p[:, m : m + 1], p[:, m + 1 : m + 2])
                    )
                    tails.append(p[:, LANES:COLS] + p[:, m + 2 : m + 3])
                for h in range(HEADS):
                    cut = slice(h * ROWS, (h + 1) * ROWS)
                    bias[h, pl.ds(row0, 2 * ROWS), rel * LANES : (rel + 1) * LANES] = jnp.concatenate(
                        [heads[0][cut], heads[1][cut]], axis=0
                    )
            for half in range(2):
                t = tails[4 * half : 4 * half + 4]
                both = [jnp.concatenate([t[0], t[2]], axis=1), jnp.concatenate([t[1], t[3]], axis=1)]
                lane = (4 + half) * LANES
                for h in range(HEADS):
                    cut = slice(h * ROWS, (h + 1) * ROWS)
                    bias[h, pl.ds(row0, 2 * ROWS), lane : lane + LANES] = jnp.concatenate(
                        [both[0][cut], both[1][cut]], axis=0
                    )
            return carry

        lax.fori_loop(0, 8, place, 0)

    own = own_ref[0]
    four = (own, prev_ref[0], next_ref[0], far_ref[0])
    keys_in = jnp.concatenate([f[:LANES] for f in four] + [f[LANES:] for f in four], axis=0)
    qg = dot(own, wqg_ref[...], NN)
    q = (qg[:, :CH] * (HD ** (-0.5) * LOG2E)).astype(BF)
    gate = jax.nn.sigmoid(qg[:, CH:])
    kv = dot(keys_in, wkv_ref[...], NN).astype(BF)
    k = kv[:, :CH]
    v1 = jnp.concatenate([kv[:, CH:], jnp.ones((4 * COLS, CH), BF)], axis=1)
    row_tile = (pos_ref[4] + i) // TILE
    run = lax.broadcasted_iota(jnp.int32, (1, 4 * COLS), 1) // HALF
    pen = jnp.zeros((1, 4 * COLS), F32)
    for rel, shift in enumerate((0, 3, 1, 2)):
        col = lax.rem(x + shift, 4) * COLS
        for slot, start in ((2 * rel, 0), (2 * rel + 1, HALF), (8 + rel, LANES)):
            keep = filt_ref[row_tile * TILES + (col + start) // TILE]
            pen = jnp.where(run == slot, (keep.astype(F32) - 1.0) * 1000000000.0, pen)
    lane_head = lax.broadcasted_iota(jnp.int32, (COLS, CH), 1) // HD
    att = jnp.zeros((COLS, CH), F32)
    for h in range(HEADS):
        mine = lane_head == h
        qh = jnp.where(mine, q, jnp.zeros_like(q))
        s = dot(qh, k, NT) + bias[h] + pen
        p = jnp.exp2(s - jnp.max(s, axis=-1, keepdims=True)).astype(BF)
        o = dot(p, v1, NN)
        att = jnp.where(mine, o[:, :CH] / o[:, CH:], att)
    gated = (gate * att).astype(BF)
    out_ref[0] = dot(gated, wo_ref[...], NN).astype(BF)


def attend(pos, filt, own, prev, nxt, far, pay0, pay1, wqg, wkv, wo):
    row = pl.BlockSpec((1, COLS, CH), lambda i: (i, 0, 0))
    return pl.pallas_call(
        attend_kernel,
        grid=(ROWS,),
        out_shape=jax.ShapeDtypeStruct((ROWS, COLS, CH), BF),
        in_specs=[SMEM, SMEM] + [row] * 4 + [VMEM] * 5,
        out_specs=row,
        scratch_shapes=[pltpu.VMEM((HEADS, COLS, 4 * COLS), F32)],
        compiler_params=PARAMS,
        cost_estimate=pl.CostEstimate(flops=8 * 10**9, bytes_accessed=10**7, transcendentals=7 * 10**6),
        name="attend",
    )(pos, filt, own, prev, nxt, far, pay0, pay1, wqg, wkv, wo)


def standardise_features(values):
    widened = values.astype(F32)
    centered = widened - jnp.mean(widened, axis=-1, keepdims=True)
    spread = jnp.mean(centered * centered, axis=-1, keepdims=True)
    return centered * lax.rsqrt(spread + 1e-05)


ALL = ("zh", "zl", "y", "c", "x")
SWAP = [
    ((a * 16 + r) * 4 + b, (b * 16 + r) * 4 + a) for a in range(4) for r in range(16) for b in range(4)
]


def gather_right(own):
    pp = lax.ppermute
    z = pp(own, "zl", ring(2, 1))
    up, down, far = [pp(own, "y", ring(4, k)) for k in (1, 3, 2)]
    zup, zdown = pp(z, "y", ring(4, 1)), pp(z, "y", ring(4, 3))
    zfar = pp(far, "zl", ring(2, 1))
    mine = [own, z, up, down, far, zup, zdown, zfar]
    return mine + [pp(m, "c", ring(2, 1)) for m in mine]


def gather_bias_z(own):
    pp = lax.ppermute
    zz = ("zh", "zl")
    up, down = pp(own, zz, ring(8, 1)), pp(own, zz, ring(8, 7))
    ahead = pp(jnp.stack([down, own, up]), zz, ring(8, 3))
    behind = pp(jnp.stack([down, own, up][1:]), zz, ring(8, 5))
    return jnp.concatenate([own[None], up[None], ahead, behind, down[None]], axis=0)


def gather_bias_y(col):
    up, down, far = [lax.ppermute(col, "y", ring(4, k)) for k in (1, 3, 2)]
    return jnp.concatenate([col, up, far, down], axis=0)


def body(stack, emb, entry, final, qkg, offset, out_proj, filt):
    pp = lax.ppermute
    zh, zl = lax.axis_index("zh"), lax.axis_index("zl")
    y, c, x = lax.axis_index("y"), lax.axis_index("c"), lax.axis_index("x")
    normed = standardise_features(stack).astype(BF)
    proj = jnp.einsum("sjc,cx->jxs", normed, entry, preferred_element_type=F32).astype(BF)
    left = proj[:, :PF].reshape(BLK, MSA)
    right = proj[:, PF:].transpose(1, 0, 2)
    right = jnp.concatenate([right[:, :8].reshape(8 * PF, MSA), right[:, 8:].reshape(4 * PF, MSA)], axis=0)
    pieces = gather_right(pp(right, ALL, SWAP))
    w = final.reshape(PF, PF, CH).transpose(1, 0, 2)
    off = jnp.pad(offset.T, ((0, 4), (0, 0)))
    pos_a = jnp.stack([zl, y, c]).astype(jnp.int32)
    mid, norm, bias = opm(pos_a, left, pieces, w, emb, off)
    prev, nxt, far = [pp(norm, "x", ring(4, k)) for k in (1, 3, 2)]
    col = gather_bias_z(pp(bias, ALL, SWAP))
    wqg = jnp.concatenate([qkg[:, :CH], qkg[:, 3 * CH :]], axis=1)
    pay0 = gather_bias_y(col)
    prev, nxt, far, pay0 = lax.optimization_barrier((prev, nxt, far, pay0))
    pay1 = pp(pay0, "c", ring(2, 1))

    row0 = (zh * 16 + zl * 8 + y * 2 + c) * ROWS
    pos_b = jnp.stack([zh * 2 + zl, y, c, x, row0]).astype(jnp.int32)
    wkv = qkg[:, CH : 3 * CH]
    update = attend(pos_b, filt.reshape(-1), norm, prev, nxt, far, pay0, pay1, wqg, wkv, out_proj)
    return mid, update


def solution(mesh):
    fine = jax.sharding.Mesh(mesh.devices.reshape(4, 2, 4, 2, 4), ALL)
    dap = ("zh", "zl", "y", "c")
    in_specs = (P(None, dap, None), P(dap, "x", None), P(), P(), P(), P(), P(), P())
    out_specs = (P(dap, "x", None), P(dap, "x", None))
    return jax.shard_map(body, mesh=fine, in_specs=in_specs, out_specs=out_specs, check_vma=False)
```

profile of v0, /device:TPU:1, one launch (start us, length us, event | category | flops | bytes accessed | tf_op | source)
XLA Modules:
  0.0 137.0 jit_solution(15273379183386381823)
XLA Ops:
  0.7 2.0 %convert_reduce_fusion = f32[256,12]{0,1:T(8,128)S(1)} fusion(bf16[256,12,256]{2,0,1:T(8,128)(2,1)} %param.8), kind=kLoop, calls=%fused_computation.1 | loop fusion | flops 1569792 | bytes 1585152 | tf_op jit(solution)/shard_map/reduce_sum | solution.py:261
  2.7 0.9 fusion.2
  3.6 1.3 fusion.11
  6.6 3.8 %collective-permute-start.4 = (bf16[384,256]{1,0:T(8,128)(2,1)S(1)}, bf16[384,256]{1,0:T(8,128)(2,1)S(1)}, u32[]{:S(2)}, u32[]{:S(2)}) collective-permute-start(bf16[384,256]{1,0:T(8,128)(2,1)S(1)} %collective-permute-done.refs_0_), channel_id=1, source_target_pairs={{0,16},{8,24},{16,0},{24,8},{1,17},{9,25},{17,1},{25,9},{2,18},{10... | collective-permute-start | bytes 589832 | tf_op jit(solution)/shard_map/ppermute | solution.py:275
  10.4 1.0 collective-permute-start.8
  11.4 0.8 collective-permute-start.3
  12.2 1.6 %collective-permute-start.1 = (bf16[384,256]{1,0:T(8,128)(2,1)S(1)}, bf16[384,256]{1,0:T(8,128)(2,1)S(1)}, u32[]{:S(2)}, u32[]{:S(2)}) collective-permute-start(bf16[384,256]{1,0:T(8,128)(2,1)S(1)} %collective-permute-done.refs_0_), channel_id=1, source_target_pairs={{0,32},{32,0},{1,33},{33,1},{2,34},{34,2},{3,35},{35,3},{4,36},{36... | collective-permute-start | bytes 589832 | tf_op jit(solution)/shard_map/ppermute | solution.py:274
  14.5 2.8 %collective-permute-start.12 = (bf16[384,256]{1,0:T(8,128)(2,1)S(1)}, bf16[384,256]{1,0:T(8,128)(2,1)S(1)}, u32[]{:S(2)}, u32[]{:S(2)}) collective-permute-start(bf16[384,256]{1,0:T(8,128)(2,1)S(1)} %collective-permute-done.4.refs_4_), channel_id=1, source_target_pairs={{0,4},{4,0},{1,5},{5,1},{2,6},{6,2},{3,7},{7,3},{8,12},{12,8},{9,1... | collective-permute-start | bytes 589832 | tf_op jit(solution)/shard_map/ppermute | solution.py:279
  17.3 1.1 collective-permute-start.7
  18.3 1.1 collective-permute-done.3.refs_3_
  19.4 1.5 %collective-permute-start.11 = (bf16[384,256]{1,0:T(8,128)(2,1)S(1)}, bf16[384,256]{1,0:T(8,128)(2,1)S(1)}, u32[]{:S(2)}, u32[]{:S(2)}) collective-permute-start(bf16[384,256]{1,0:T(8,128)(2,1)S(1)} %collective-permute-done.3.refs_3_), channel_id=1, source_target_pairs={{0,4},{4,0},{1,5},{5,1},{2,6},{6,2},{3,7},{7,3},{8,12},{12,8},{9,1... | collective-permute-start | bytes 589832 | tf_op jit(solution)/shard_map/ppermute | solution.py:279
  20.9 2.4 %collective-permute-start.6 = (bf16[384,256]{1,0:T(8,128)(2,1)S(1)}, bf16[384,256]{1,0:T(8,128)(2,1)S(1)}, u32[]{:S(2)}, u32[]{:S(2)}) collective-permute-start(bf16[384,256]{1,0:T(8,128)(2,1)S(1)} %collective-permute-done.1.refs_1_), channel_id=1, source_target_pairs={{0,24},{8,0},{16,8},{24,16},{1,25},{9,1},{17,9},{25,17},{2,26},{10... | collective-permute-start | bytes 589832 | tf_op jit(solution)/shard_map/ppermute | solution.py:276
  23.8 2.5 %collective-permute-done.7.refs_7_ = bf16[384,256]{1,0:T(8,128)(2,1)S(1)} collective-permute-done((bf16[384,256]{1,0:T(8,128)(2,1)S(1)}, bf16[384,256]{1,0:T(8,128)(2,1)S(1)}, u32[]{:S(2)}, u32[]{:S(2)}) %collective-permute-start.7) | collective-permute-done | bytes 196640 | tf_op jit(solution)/shard_map/ppermute | solution.py:277
  26.3 0.9 collective-permute-start.10
  27.6 0.9 collective-permute-start.14
  28.4 2.2 %collective-permute-done.5.refs_5_ = bf16[384,256]{1,0:T(8,128)(2,1)S(1)} collective-permute-done((bf16[384,256]{1,0:T(8,128)(2,1)S(1)}, bf16[384,256]{1,0:T(8,128)(2,1)S(1)}, u32[]{:S(2)}, u32[]{:S(2)}) %collective-permute-start.5) | collective-permute-done | bytes 196640 | tf_op jit(solution)/shard_map/ppermute | solution.py:276
  30.6 1.2 collective-permute-start.13
  31.8 0.8 copy.17
  34.8 11.0 %opm.1 = (bf16[12,192,128]{2,1,0:T(8,128)(2,1)}, bf16[12,192,128]{2,1,0:T(8,128)(2,1)}, bf16[48,256]{1,0:T(8,128)(2,1)}) custom-call(s32[3]{0:T(128)} %pad_add_fusion.pos_ref, bf16[384,256]{1,0:T(8,128)(2,1)} %bitcast.38, bf16[384,256]{1,0:T(8,128)(2,1)} %copy-done.11, bf16[384,256]{1,0:T(8,128)(2,1)} %copy-done.15, bf16[384,256]{1,0:T(8,128)(2,1)} %copy-done.16, ...), custom_call_target="tpu_custom_call" | custom-call | flops 6000000000 | bytes 10000000 | tf_op jit(solution)/shard_map/opm/pallas_call | solution.py:144
  45.8 1.5 %collective-permute-start.19 = (bf16[48,256]{1,0:T(8,128)(2,1)}, bf16[48,256]{1,0:T(8,128)(2,1)S(1)}, u32[]{:S(2)}, u32[]{:S(2)}) collective-permute-start(bf16[48,256]{1,0:T(8,128)(2,1)} %get-tuple-element.11), channel_id=1, source_target_pairs={{0,0},{1,64},{2,128},{3,192},{4,4},{5,68},{6,132},{7,196},{8,8},{9... | collective-permute-start | bytes 73736 | tf_op jit(solution)/shard_map/ppermute | solution.py:311
  47.4 23.4 %collective-permute-start.18 = (bf16[12,192,128]{2,1,0:T(8,128)(2,1)}, bf16[12,192,128]{2,1,0:T(8,128)(2,1)S(1)}, u32[]{:S(2)}, u32[]{:S(2)}) collective-permute-start(bf16[12,192,128]{2,1,0:T(8,128)(2,1)} %get-tuple-element.10.own_ref), channel_id=1, source_target_pairs={{0,2},{1,3},{2,0},{3,1},{4,6},{5,7},{6,4},{7,5},{8,10},{9,11},{10,... | collective-permute-start | bytes 1769480 | tf_op jit(solution)/shard_map/ppermute | solution.py:310
  70.8 5.8 %collective-permute-start.17 = (bf16[12,192,128]{2,1,0:T(8,128)(2,1)}, bf16[12,192,128]{2,1,0:T(8,128)(2,1)S(1)}, u32[]{:S(2)}, u32[]{:S(2)}) collective-permute-start(bf16[12,192,128]{2,1,0:T(8,128)(2,1)} %get-tuple-element.10.own_ref), channel_id=1, source_target_pairs={{0,3},{1,0},{2,1},{3,2},{4,7},{5,4},{6,5},{7,6},{8,11},{9,8},{10,9... | collective-permute-start | bytes 1769480 | tf_op jit(solution)/shard_map/ppermute | solution.py:310
  77.1 2.3 %collective-permute-start.21 = (bf16[48,256]{1,0:T(8,128)(2,1)S(1)}, bf16[48,256]{1,0:T(8,128)(2,1)S(1)}, u32[]{:S(2)}, u32[]{:S(2)}) collective-permute-start(bf16[48,256]{1,0:T(8,128)(2,1)S(1)} %collective-permute-done.19), channel_id=1, source_target_pairs={{0,224},{32,0},{64,32},{96,64},{128,96},{160,128},{192,160},{224,1... | collective-permute-start | bytes 73736 | tf_op jit(solution)/shard_map/ppermute | solution.py:285
  79.4 4.2 %collective-permute-done.20 = bf16[48,256]{1,0:T(8,128)(2,1)S(1)} collective-permute-done((bf16[48,256]{1,0:T(8,128)(2,1)S(1)}, bf16[48,256]{1,0:T(8,128)(2,1)S(1)}, u32[]{:S(2)}, u32[]{:S(2)}) %collective-permute-start.20) | collective-permute-done | bytes 24608 | tf_op jit(solution)/shard_map/ppermute | solution.py:285
  83.7 3.3 %collective-permute-start.22 = (bf16[3,48,256]{2,1,0:T(8,128)(2,1)S(1)}, bf16[3,48,256]{2,1,0:T(8,128)(2,1)S(1)}, u32[]{:S(2)}, u32[]{:S(2)}) collective-permute-start(bf16[3,48,256]{2,1,0:T(8,128)(2,1)S(1)} %pad_maximum_fusion.1), channel_id=1, source_target_pairs={{0,96},{32,128},{64,160},{96,192},{128,224},{160,0},{192,32},{224,... | collective-permute-start | bytes 221192 | tf_op jit(solution)/shard_map/ppermute | solution.py:286
  87.0 4.4 %collective-permute-done.22 = bf16[3,48,256]{2,1,0:T(8,128)(2,1)S(1)} collective-permute-done((bf16[3,48,256]{2,1,0:T(8,128)(2,1)S(1)}, bf16[3,48,256]{2,1,0:T(8,128)(2,1)S(1)}, u32[]{:S(2)}, u32[]{:S(2)}) %collective-permute-start.22) | collective-permute-done | bytes 73760 | tf_op jit(solution)/shard_map/ppermute | solution.py:286
  91.5 1.4 %collective-permute-start.25 = (bf16[8,48,256]{2,1,0:T(8,128)(2,1)S(1)}, bf16[8,48,256]{2,1,0:T(8,128)(2,1)S(1)}, u32[]{:S(2)}, u32[]{:S(2)}) collective-permute-start(bf16[8,48,256]{2,1,0:T(8,128)(2,1)S(1)} %get-tuple-element.24), channel_id=1, source_target_pairs={{0,16},{8,24},{16,0},{24,8},{1,17},{9,25},{17,1},{25,9},{2,18},{10... | collective-permute-start | bytes 589832 | tf_op jit(solution)/shard_map/ppermute | solution.py:292
  92.9 6.4 %collective-permute-done.24 = bf16[8,48,256]{2,1,0:T(8,128)(2,1)S(1)} collective-permute-done((bf16[8,48,256]{2,1,0:T(8,128)(2,1)S(1)}, bf16[8,48,256]{2,1,0:T(8,128)(2,1)S(1)}, u32[]{:S(2)}, u32[]{:S(2)}) %collective-permute-start.24) | collective-permute-done | bytes 196640 | tf_op jit(solution)/shard_map/ppermute | solution.py:292
  99.4 5.0 %collective-permute-done.26 = bf16[8,48,256]{2,1,0:T(8,128)(2,1)S(1)} collective-permute-done((bf16[8,48,256]{2,1,0:T(8,128)(2,1)S(1)}, bf16[8,48,256]{2,1,0:T(8,128)(2,1)S(1)}, u32[]{:S(2)}, u32[]{:S(2)}) %collective-permute-start.26) | collective-permute-done | bytes 196640 | tf_op jit(solution)/shard_map/ppermute | solution.py:292
  104.5 5.6 %collective-permute-start.27 = (bf16[32,48,256]{2,1,0:T(8,128)(2,1)S(1)}, bf16[32,48,256]{2,1,0:T(8,128)(2,1)S(1)}, u32[]{:S(2)}, u32[]{:S(2)}) collective-permute-start(bf16[32,48,256]{2,1,0:T(8,128)(2,1)S(1)} %constant_dynamic-update-slice_fusion.5.pay0_ref), channel_id=1, source_target_pairs={{0,4},{4,0},{1,5},{5,1},{2,6},{6,2},{3,7},{7,3},{8,12},{12,8},{9,1... | collective-permute-start | bytes 2359304 | tf_op jit(solution)/shard_map/ppermute | solution.py:315
  112.6 0.9 copy-done.7
  113.5 23.5 %attend.1 = bf16[12,192,128]{2,1,0:T(8,128)(2,1)} custom-call(s32[5]{0:T(128)} %stack.46.pos_ref, s32[36]{0:T(128)} %reshape.35.filt_ref, bf16[12,192,128]{2,1,0:T(8,128)(2,1)} %get-tuple-element.10.own_ref, bf16[12,192,128]{2,1,0:T(8,128)(2,1)} %copy-done.10, bf16[12,192,128]{2,1,0:T(8,128)(2,1)} %copy-done.9, bf16[12,192,128]{2,1,0:T(8,128)(2,1)} %copy-done.8, ...), custom_call_target="tpu_custom_call" | custom-call | flops 8000000000 | bytes 10000000 | tf_op jit(solution)/shard_map/attend/pallas_call | solution.py:246
  (108 shorter events, 8.5 us)
Async XLA Ops:
  5.0 27.7 %copy-start.5 = (f32[128,4]{0,1:T(4,128)S(1)}, f32[128,4]{0,1:T(4,128)}, u32[]{:S(2)}) copy-start(f32[128,4]{0,1:T(4,128)} %param.13) | copy-start | bytes 6148
  5.9 0.7 collective-permute-start
  6.6 27.4 %copy-start.11 = (bf16[384,256]{1,0:T(8,128)(2,1)}, bf16[384,256]{1,0:T(8,128)(2,1)S(1)}, u32[]{:S(2)}) copy-start(bf16[384,256]{1,0:T(8,128)(2,1)S(1)} %collective-permute-done.refs_0_) | copy-start | bytes 589828
  6.6 7.9 %collective-permute-start.4 = (bf16[384,256]{1,0:T(8,128)(2,1)S(1)}, bf16[384,256]{1,0:T(8,128)(2,1)S(1)}, u32[]{:S(2)}, u32[]{:S(2)}) collective-permute-start(bf16[384,256]{1,0:T(8,128)(2,1)S(1)} %collective-permute-done.refs_0_), channel_id=1, source_target_pairs={{0,16},{8,24},{16,0},{24,8},{1,17},{9,25},{17,1},{25,9},{2,18},{10... | collective-permute-start | bytes 589832 | tf_op jit(solution)/shard_map/ppermute | solution.py:275
  10.4 6.9 %collective-permute-start.8 = (bf16[384,256]{1,0:T(8,128)(2,1)S(1)}, bf16[384,256]{1,0:T(8,128)(2,1)S(1)}, u32[]{:S(2)}, u32[]{:S(2)}) collective-permute-start(bf16[384,256]{1,0:T(8,128)(2,1)S(1)} %collective-permute-done.refs_0_), channel_id=1, source_target_pairs={{0,4},{4,0},{1,5},{5,1},{2,6},{6,2},{3,7},{7,3},{8,12},{12,8},{9,1... | collective-permute-start | bytes 589832 | tf_op jit(solution)/shard_map/ppermute | solution.py:279
  11.4 8.0 %collective-permute-start.3 = (bf16[384,256]{1,0:T(8,128)(2,1)S(1)}, bf16[384,256]{1,0:T(8,128)(2,1)S(1)}, u32[]{:S(2)}, u32[]{:S(2)}) collective-permute-start(bf16[384,256]{1,0:T(8,128)(2,1)S(1)} %collective-permute-done.refs_0_), channel_id=1, source_target_pairs={{0,24},{8,0},{16,8},{24,16},{1,25},{9,1},{17,9},{25,17},{2,26},{10... | collective-permute-start | bytes 589832 | tf_op jit(solution)/shard_map/ppermute | solution.py:275
  12.2 8.7 %collective-permute-start.1 = (bf16[384,256]{1,0:T(8,128)(2,1)S(1)}, bf16[384,256]{1,0:T(8,128)(2,1)S(1)}, u32[]{:S(2)}, u32[]{:S(2)}) collective-permute-start(bf16[384,256]{1,0:T(8,128)(2,1)S(1)} %collective-permute-done.refs_0_), channel_id=1, source_target_pairs={{0,32},{32,0},{1,33},{33,1},{2,34},{34,2},{3,35},{35,3},{4,36},{36... | collective-permute-start | bytes 589832 | tf_op jit(solution)/shard_map/ppermute | solution.py:274
  13.8 9.5 %collective-permute-start.2 = (bf16[384,256]{1,0:T(8,128)(2,1)S(1)}, bf16[384,256]{1,0:T(8,128)(2,1)S(1)}, u32[]{:S(2)}, u32[]{:S(2)}) collective-permute-start(bf16[384,256]{1,0:T(8,128)(2,1)S(1)} %collective-permute-done.refs_0_), channel_id=1, source_target_pairs={{0,8},{8,16},{16,24},{24,0},{1,9},{9,17},{17,25},{25,1},{2,10},{10... | collective-permute-start | bytes 589832 | tf_op jit(solution)/shard_map/ppermute | solution.py:275
  14.5 8.8 %collective-permute-start.12 = (bf16[384,256]{1,0:T(8,128)(2,1)S(1)}, bf16[384,256]{1,0:T(8,128)(2,1)S(1)}, u32[]{:S(2)}, u32[]{:S(2)}) collective-permute-start(bf16[384,256]{1,0:T(8,128)(2,1)S(1)} %collective-permute-done.4.refs_4_), channel_id=1, source_target_pairs={{0,4},{4,0},{1,5},{5,1},{2,6},{6,2},{3,7},{7,3},{8,12},{12,8},{9,1... | collective-permute-start | bytes 589832 | tf_op jit(solution)/shard_map/ppermute | solution.py:279
  17.3 9.0 %collective-permute-start.7 = (bf16[384,256]{1,0:T(8,128)(2,1)S(1)}, bf16[384,256]{1,0:T(8,128)(2,1)S(1)}, u32[]{:S(2)}, u32[]{:S(2)}) collective-permute-start(bf16[384,256]{1,0:T(8,128)(2,1)S(1)} %collective-permute-done.4.refs_4_), channel_id=1, source_target_pairs={{0,32},{32,0},{1,33},{33,1},{2,34},{34,2},{3,35},{35,3},{4,36},{36... | collective-permute-start | bytes 589832 | tf_op jit(solution)/shard_map/ppermute | solution.py:277
  19.4 7.7 %collective-permute-start.11 = (bf16[384,256]{1,0:T(8,128)(2,1)S(1)}, bf16[384,256]{1,0:T(8,128)(2,1)S(1)}, u32[]{:S(2)}, u32[]{:S(2)}) collective-permute-start(bf16[384,256]{1,0:T(8,128)(2,1)S(1)} %collective-permute-done.3.refs_3_), channel_id=1, source_target_pairs={{0,4},{4,0},{1,5},{5,1},{2,6},{6,2},{3,7},{7,3},{8,12},{12,8},{9,1... | collective-permute-start | bytes 589832 | tf_op jit(solution)/shard_map/ppermute | solution.py:279
  20.9 6.7 %collective-permute-start.6 = (bf16[384,256]{1,0:T(8,128)(2,1)S(1)}, bf16[384,256]{1,0:T(8,128)(2,1)S(1)}, u32[]{:S(2)}, u32[]{:S(2)}) collective-permute-start(bf16[384,256]{1,0:T(8,128)(2,1)S(1)} %collective-permute-done.1.refs_1_), channel_id=1, source_target_pairs={{0,24},{8,0},{16,8},{24,16},{1,25},{9,1},{17,9},{25,17},{2,26},{10... | collective-permute-start | bytes 589832 | tf_op jit(solution)/shard_map/ppermute | solution.py:276
  23.3 7.3 %collective-permute-start.5 = (bf16[384,256]{1,0:T(8,128)(2,1)S(1)}, bf16[384,256]{1,0:T(8,128)(2,1)S(1)}, u32[]{:S(2)}, u32[]{:S(2)}) collective-permute-start(bf16[384,256]{1,0:T(8,128)(2,1)S(1)} %collective-permute-done.1.refs_1_), channel_id=1, source_target_pairs={{0,8},{8,16},{16,24},{24,0},{1,9},{9,17},{17,25},{25,1},{2,10},{10... | collective-permute-start | bytes 589832 | tf_op jit(solution)/shard_map/ppermute | solution.py:276
  23.3 10.6 %collective-permute-start.9 = (bf16[384,256]{1,0:T(8,128)(2,1)S(1)}, bf16[384,256]{1,0:T(8,128)(2,1)S(1)}, u32[]{:S(2)}, u32[]{:S(2)}) collective-permute-start(bf16[384,256]{1,0:T(8,128)(2,1)S(1)} %collective-permute-done.1.refs_1_), channel_id=1, source_target_pairs={{0,4},{4,0},{1,5},{5,1},{2,6},{6,2},{3,7},{7,3},{8,12},{12,8},{9,1... | collective-permute-start | bytes 589832 | tf_op jit(solution)/shard_map/ppermute | solution.py:279
  26.3 7.6 %collective-permute-start.10 = (bf16[384,256]{1,0:T(8,128)(2,1)S(1)}, bf16[384,256]{1,0:T(8,128)(2,1)S(1)}, u32[]{:S(2)}, u32[]{:S(2)}) collective-permute-start(bf16[384,256]{1,0:T(8,128)(2,1)S(1)} %collective-permute-done.2.refs_2_), channel_id=1, source_target_pairs={{0,4},{4,0},{1,5},{5,1},{2,6},{6,2},{3,7},{7,3},{8,12},{12,8},{9,1... | collective-permute-start | bytes 589832 | tf_op jit(solution)/shard_map/ppermute | solution.py:279
  27.2 6.8 %collective-permute-start.15 = (bf16[384,256]{1,0:T(8,128)(2,1)S(1)}, bf16[384,256]{1,0:T(8,128)(2,1)S(1)}, u32[]{:S(2)}, u32[]{:S(2)}) collective-permute-start(bf16[384,256]{1,0:T(8,128)(2,1)S(1)} %collective-permute-done.7.refs_7_), channel_id=1, source_target_pairs={{0,4},{4,0},{1,5},{5,1},{2,6},{6,2},{3,7},{7,3},{8,12},{12,8},{9,1... | collective-permute-start | bytes 589832 | tf_op jit(solution)/shard_map/ppermute | solution.py:279
  27.6 6.4 %collective-permute-start.14 = (bf16[384,256]{1,0:T(8,128)(2,1)S(1)}, bf16[384,256]{1,0:T(8,128)(2,1)S(1)}, u32[]{:S(2)}, u32[]{:S(2)}) collective-permute-start(bf16[384,256]{1,0:T(8,128)(2,1)S(1)} %collective-permute-done.6.refs_6_), channel_id=1, source_target_pairs={{0,4},{4,0},{1,5},{5,1},{2,6},{6,2},{3,7},{7,3},{8,12},{12,8},{9,1... | collective-permute-start | bytes 589832 | tf_op jit(solution)/shard_map/ppermute | solution.py:279
  30.6 3.3 %collective-permute-start.13 = (bf16[384,256]{1,0:T(8,128)(2,1)S(1)}, bf16[384,256]{1,0:T(8,128)(2,1)}, u32[]{:S(2)}, u32[]{:S(2)}) collective-permute-start(bf16[384,256]{1,0:T(8,128)(2,1)S(1)} %collective-permute-done.5.refs_5_), channel_id=1, source_target_pairs={{0,4},{4,0},{1,5},{5,1},{2,6},{6,2},{3,7},{7,3},{8,12},{12,8},{9,1... | collective-permute-start | bytes 589832 | tf_op jit(solution)/shard_map/ppermute | solution.py:279
  45.8 64.3 %copy-start.4 = (s32[6,6]{1,0:T(8,128)S(1)}, s32[6,6]{1,0:T(8,128)}, u32[]{:S(2)}) copy-start(s32[6,6]{1,0:T(8,128)} %param.15) | copy-start | bytes 436
  45.8 64.9 %copy-start.3 = (bf16[128,512]{1,0:T(8,128)(2,1)S(1)}, bf16[128,512]{1,0:T(8,128)(2,1)}, u32[]{:S(2)}) copy-start(bf16[128,512]{1,0:T(8,128)(2,1)} %param.12) | copy-start | bytes 393220
  45.8 31.3 %collective-permute-start.19 = (bf16[48,256]{1,0:T(8,128)(2,1)}, bf16[48,256]{1,0:T(8,128)(2,1)S(1)}, u32[]{:S(2)}, u32[]{:S(2)}) collective-permute-start(bf16[48,256]{1,0:T(8,128)(2,1)} %get-tuple-element.11), channel_id=1, source_target_pairs={{0,0},{1,64},{2,128},{3,192},{4,4},{5,68},{6,132},{7,196},{8,8},{9... | collective-permute-start | bytes 73736 | tf_op jit(solution)/shard_map/ppermute | solution.py:311
  47.4 57.1 %collective-permute-start.18 = (bf16[12,192,128]{2,1,0:T(8,128)(2,1)}, bf16[12,192,128]{2,1,0:T(8,128)(2,1)S(1)}, u32[]{:S(2)}, u32[]{:S(2)}) collective-permute-start(bf16[12,192,128]{2,1,0:T(8,128)(2,1)} %get-tuple-element.10.own_ref), channel_id=1, source_target_pairs={{0,2},{1,3},{2,0},{3,1},{4,6},{5,7},{6,4},{7,5},{8,10},{9,11},{10,... | collective-permute-start | bytes 1769480 | tf_op jit(solution)/shard_map/ppermute | solution.py:310
  70.8 33.6 %collective-permute-start.17 = (bf16[12,192,128]{2,1,0:T(8,128)(2,1)}, bf16[12,192,128]{2,1,0:T(8,128)(2,1)S(1)}, u32[]{:S(2)}, u32[]{:S(2)}) collective-permute-start(bf16[12,192,128]{2,1,0:T(8,128)(2,1)} %get-tuple-element.10.own_ref), channel_id=1, source_target_pairs={{0,3},{1,0},{2,1},{3,2},{4,7},{5,4},{6,5},{7,6},{8,11},{9,8},{10,9... | collective-permute-start | bytes 1769480 | tf_op jit(solution)/shard_map/ppermute | solution.py:310
  76.6 27.8 %collective-permute-start.16 = (bf16[12,192,128]{2,1,0:T(8,128)(2,1)}, bf16[12,192,128]{2,1,0:T(8,128)(2,1)S(1)}, u32[]{:S(2)}, u32[]{:S(2)}) collective-permute-start(bf16[12,192,128]{2,1,0:T(8,128)(2,1)} %get-tuple-element.10.own_ref), channel_id=1, source_target_pairs={{0,1},{1,2},{2,3},{3,0},{4,5},{5,6},{6,7},{7,4},{8,9},{9,10},{10,1... | collective-permute-start | bytes 1769480 | tf_op jit(solution)/shard_map/ppermute | solution.py:310
  77.1 6.5 %collective-permute-start.21 = (bf16[48,256]{1,0:T(8,128)(2,1)S(1)}, bf16[48,256]{1,0:T(8,128)(2,1)S(1)}, u32[]{:S(2)}, u32[]{:S(2)}) collective-permute-start(bf16[48,256]{1,0:T(8,128)(2,1)S(1)} %collective-permute-done.19), channel_id=1, source_target_pairs={{0,224},{32,0},{64,32},{96,64},{128,96},{160,128},{192,160},{224,1... | collective-permute-start | bytes 73736 | tf_op jit(solution)/shard_map/ppermute | solution.py:285
  79.4 4.2 %collective-permute-start.20 = (bf16[48,256]{1,0:T(8,128)(2,1)S(1)}, bf16[48,256]{1,0:T(8,128)(2,1)S(1)}, u32[]{:S(2)}, u32[]{:S(2)}) collective-permute-start(bf16[48,256]{1,0:T(8,128)(2,1)S(1)} %collective-permute-done.19), channel_id=1, source_target_pairs={{0,32},{32,64},{64,96},{96,128},{128,160},{160,192},{192,224},{224... | collective-permute-start | bytes 73736 | tf_op jit(solution)/shard_map/ppermute | solution.py:285
  83.6 7.8 %collective-permute-start.23 = (bf16[2,48,256]{2,1,0:T(8,128)(2,1)S(1)}, bf16[2,48,256]{2,1,0:T(8,128)(2,1)S(1)}, u32[]{:S(2)}, u32[]{:S(2)}) collective-permute-start(bf16[2,48,256]{2,1,0:T(8,128)(2,1)S(1)} %pad_maximum_fusion.3), channel_id=1, source_target_pairs={{0,160},{32,192},{64,224},{96,0},{128,32},{160,64},{192,96},{224,1... | collective-permute-start | bytes 147464 | tf_op jit(solution)/shard_map/ppermute | solution.py:287
  83.7 7.7 %collective-permute-start.22 = (bf16[3,48,256]{2,1,0:T(8,128)(2,1)S(1)}, bf16[3,48,256]{2,1,0:T(8,128)(2,1)S(1)}, u32[]{:S(2)}, u32[]{:S(2)}) collective-permute-start(bf16[3,48,256]{2,1,0:T(8,128)(2,1)S(1)} %pad_maximum_fusion.1), channel_id=1, source_target_pairs={{0,96},{32,128},{64,160},{96,192},{128,224},{160,0},{192,32},{224,... | collective-permute-start | bytes 221192 | tf_op jit(solution)/shard_map/ppermute | solution.py:286
  91.4 7.9 %collective-permute-start.24 = (bf16[8,48,256]{2,1,0:T(8,128)(2,1)S(1)}, bf16[8,48,256]{2,1,0:T(8,128)(2,1)S(1)}, u32[]{:S(2)}, u32[]{:S(2)}) collective-permute-start(bf16[8,48,256]{2,1,0:T(8,128)(2,1)S(1)} %get-tuple-element.24), channel_id=1, source_target_pairs={{0,8},{8,16},{16,24},{24,0},{1,9},{9,17},{17,25},{25,1},{2,10},{10... | collective-permute-start | bytes 589832 | tf_op jit(solution)/shard_map/ppermute | solution.py:292
  91.5 7.8 %collective-permute-start.25 = (bf16[8,48,256]{2,1,0:T(8,128)(2,1)S(1)}, bf16[8,48,256]{2,1,0:T(8,128)(2,1)S(1)}, u32[]{:S(2)}, u32[]{:S(2)}) collective-permute-start(bf16[8,48,256]{2,1,0:T(8,128)(2,1)S(1)} %get-tuple-element.24), channel_id=1, source_target_pairs={{0,16},{8,24},{16,0},{24,8},{1,17},{9,25},{17,1},{25,9},{2,18},{10... | collective-permute-start | bytes 589832 | tf_op jit(solution)/shard_map/ppermute | solution.py:292
  99.3 5.1 %collective-permute-start.26 = (bf16[8,48,256]{2,1,0:T(8,128)(2,1)S(1)}, bf16[8,48,256]{2,1,0:T(8,128)(2,1)S(1)}, u32[]{:S(2)}, u32[]{:S(2)}) collective-permute-start(bf16[8,48,256]{2,1,0:T(8,128)(2,1)S(1)} %get-tuple-element.24), channel_id=1, source_target_pairs={{0,24},{8,0},{16,8},{24,16},{1,25},{9,1},{17,9},{25,17},{2,26},{10... | collective-permute-start | bytes 589832 | tf_op jit(solution)/shard_map/ppermute | solution.py:292
  104.5 8.1 %collective-permute-start.27 = (bf16[32,48,256]{2,1,0:T(8,128)(2,1)S(1)}, bf16[32,48,256]{2,1,0:T(8,128)(2,1)S(1)}, u32[]{:S(2)}, u32[]{:S(2)}) collective-permute-start(bf16[32,48,256]{2,1,0:T(8,128)(2,1)S(1)} %constant_dynamic-update-slice_fusion.5.pay0_ref), channel_id=1, source_target_pairs={{0,4},{4,0},{1,5},{5,1},{2,6},{6,2},{3,7},{7,3},{8,12},{12,8},{9,1... | collective-permute-start | bytes 2359304 | tf_op jit(solution)/shard_map/ppermute | solution.py:315
  (22 other events, 178.5 us)
where the time goes:
time: 137 us
  starting transfers between devices  63.8 us (47%)
  Pallas kernels  34.5 us (25%)
  waiting for transfers between devices  26.1 us (19%)
  local copies, waits for them, and re-layouts  5.95 us (4%)
  other arithmetic  4.25 us (3%)
    ppermute x3, starting transfers between devices, body(): prev, nxt, far = [pp(norm, 'x', ring(4, k)) for k in (1, 3, 2)]  29.7 us
    pallas_call x1, Pallas kernels, attend(): pl.pallas_call(attend_kernel, grid=(ROWS,), out_shape=jax.ShapeDtypeStruc...  23.5 us
    ppermute x3, waiting for transfers between devices, gather_bias_y(): up, down, far = [lax.ppermute(col, 'y', ring(4, k)) for k in (1, 3, 2)]  11.4 us
    pallas_call x1, Pallas kernels, opm(): pl.pallas_call(opm_kernel, out_shape=(jax.ShapeDtypeStruct((ROWS, COLS, C...  11 us
    ppermute x8, starting transfers between devices, gather_right(): return mine + [pp(m, 'c', ring(2, 1)) for m in mine]  8.67 us
    ppermute x1, starting transfers between devices, body(): pay1 = pp(pay0, 'c', ring(2, 1))  5.6 us
    ppermute x3, starting transfers between devices, gather_right(): up, down, far = [pp(own, 'y', ring(4, k)) for k in (1, 3, 2)]  5.29 us
    ppermute x1, waiting for transfers between devices, gather_bias_z(): ahead = pp(jnp.stack([down, own, up]), zz, ring(8, 3))  4.38 us
  transfers between devices with their start and end apart: 28, of which 8 were waited for; matrix products, arithmetic and copies ran while one was open for 3% of the time, Pallas kernels for 0%

commit v1 on v0

--- a/solution.py
+++ b/solution.py
@@ -17,7 +17,7 @@
 HALF = COLS - LANES
 PAY = HEADS * ROWS
 LOG2E = 1.4426950408889634
-TILES, TILE = 6, 128
+TILE = 128
 
 
 def ring(n, k):
@@ -163,12 +163,38 @@
     )(pos, left, *pieces, w, emb, off)
 
 
+def project_kernel(own_ref, prev_ref, next_ref, far_ref, qkg_ref, q_ref, gate_ref, kv_ref):
+    own = own_ref[0]
+    four = (own, prev_ref[0], next_ref[0], far_ref[0])
+    keys_in = jnp.concatenate([f[:LANES] for f in four] + [f[LANES:] for f in four], axis=0)
+    q_ref[0] = (dot(own, qkg_ref[:, :CH], NN) * (HD ** (-0.5) * LOG2E)).astype(BF)
+    gate_ref[0] = jax.nn.sigmoid(dot(own, qkg_ref[:, 3 * CH :], NN))
+    kv_ref[0] = dot(keys_in, qkg_ref[:, CH : 3 * CH], NN).astype(BF)
+
+
+def project(own, prev, nxt, far, qkg):
+    row = pl.BlockSpec((1, COLS, CH), lambda i: (i, 0, 0))
+    return pl.pallas_call(
+        project_kernel,
+        grid=(ROWS,),
+        out_shape=(
+            jax.ShapeDtypeStruct((ROWS, COLS, CH), BF),
+            jax.ShapeDtypeStruct((ROWS, COLS, CH), F32),
+            jax.ShapeDtypeStruct((ROWS, 4 * COLS, 2 * CH), BF),
+        ),
+        in_specs=[row] * 4 + [VMEM],
+        out_specs=[row, row, pl.BlockSpec((1, 4 * COLS, 2 * CH), lambda i: (i, 0, 0))],
+        compiler_params=PARAMS,
+        cost_estimate=pl.CostEstimate(flops=10**10, bytes_accessed=2 * 10**7, transcendentals=10**5),
+        name="project",
+    )(own, prev, nxt, far, qkg)
+
+
 def attend_kernel(
-    pos_ref, filt_ref, own_ref, prev_ref, next_ref, far_ref, pay0_ref, pay1_ref,
-    wqg_ref, wkv_ref, wo_ref, out_ref, bias,
+    pos_ref, filt_ref, q_ref, gate_ref, kv_ref, pay0_ref, pay1_ref, wo_ref, out_ref, bias,
 ):
     i = pl.program_id(0)
-    z, y, c, x = pos_ref[0], pos_ref[1], pos_ref[2], pos_ref[3]
+    c, zh, x = pos_ref[2], pos_ref[3], pos_ref[4]
 
     @pl.when(i == 0)
     def _():
@@ -176,16 +202,11 @@
 
         def place(pair, carry):
             row0 = pl.multiple_of(pair * 2 * ROWS, 8)
-            src_z = pair // 4
-            src_y = lax.rem(pair, 4)
-            dy = lax.rem(y + 4 - src_y, 4)
             tails = []
             for rel, shift in enumerate((0, 3, 1, 2)):
-                zh = lax.rem(x + shift, 4)
-                dz = lax.rem(z + 8 - zh * 2 - src_z, 8)
-                at = dy * 8 + dz
-                p0 = pay0_ref[at].astype(F32) * LOG2E
-                p1 = pay1_ref[at].astype(F32) * LOG2E
+                at = lax.rem(zh + 8 - x - shift, 4)
+                p0 = pay0_ref[pair, at].astype(F32) * LOG2E
+                p1 = pay1_ref[pair, at].astype(F32) * LOG2E
                 heads = []
                 for p in (jnp.where(c == 0, p0, p1), jnp.where(c == 0, p1, p0)):
                     m = COLS
@@ -211,22 +232,16 @@
 
         lax.fori_loop(0, 8, place, 0)
 
-    own = own_ref[0]
-    four = (own, prev_ref[0], next_ref[0], far_ref[0])
-    keys_in = jnp.concatenate([f[:LANES] for f in four] + [f[LANES:] for f in four], axis=0)
-    qg = dot(own, wqg_ref[...], NN)
-    q = (qg[:, :CH] * (HD ** (-0.5) * LOG2E)).astype(BF)
-    gate = jax.nn.sigmoid(qg[:, CH:])
-    kv = dot(keys_in, wkv_ref[...], NN).astype(BF)
+    q, gate, kv = q_ref[0], gate_ref[0], kv_ref[0]
     k = kv[:, :CH]
     v1 = jnp.concatenate([kv[:, CH:], jnp.ones((4 * COLS, CH), BF)], axis=1)
-    row_tile = (pos_ref[4] + i) // TILE
+    row_tile = (pos_ref[5] + i) // TILE
     run = lax.broadcasted_iota(jnp.int32, (1, 4 * COLS), 1) // HALF
     pen = jnp.zeros((1, 4 * COLS), F32)
     for rel, shift in enumerate((0, 3, 1, 2)):
         col = lax.rem(x + shift, 4) * COLS
         for slot, start in ((2 * rel, 0), (2 * rel + 1, HALF), (8 + rel, LANES)):
-            keep = filt_ref[row_tile * TILES + (col + start) // TILE]
+            keep = filt_ref[row_tile, (col + start) // TILE]
             pen = jnp.where(run == slot, (keep.astype(F32) - 1.0) * 1000000000.0, pen)
     lane_head = lax.broadcasted_iota(jnp.int32, (COLS, CH), 1) // HD
     att = jnp.zeros((COLS, CH), F32)
@@ -241,19 +256,19 @@
     out_ref[0] = dot(gated, wo_ref[...], NN).astype(BF)
 
 
-def attend(pos, filt, own, prev, nxt, far, pay0, pay1, wqg, wkv, wo):
+def attend(pos, filt, q, gate, kv, pay0, pay1, wo):
     row = pl.BlockSpec((1, COLS, CH), lambda i: (i, 0, 0))
     return pl.pallas_call(
         attend_kernel,
         grid=(ROWS,),
         out_shape=jax.ShapeDtypeStruct((ROWS, COLS, CH), BF),
-        in_specs=[SMEM, SMEM] + [row] * 4 + [VMEM] * 5,
+        in_specs=[SMEM, SMEM, row, row, pl.BlockSpec((1, 4 * COLS, 2 * CH), lambda i: (i, 0, 0))] + [VMEM] * 3,
         out_specs=row,
         scratch_shapes=[pltpu.VMEM((HEADS, COLS, 4 * COLS), F32)],
         compiler_params=PARAMS,
         cost_estimate=pl.CostEstimate(flops=8 * 10**9, bytes_accessed=10**7, transcendentals=7 * 10**6),
         name="attend",
-    )(pos, filt, own, prev, nxt, far, pay0, pay1, wqg, wkv, wo)
+    )(pos, filt, q, gate, kv, pay0, pay1, wo)
 
 
 def standardise_features(values):
@@ -266,6 +281,12 @@
 ALL = ("zh", "zl", "y", "c", "x")
 SWAP = [
     ((a * 16 + r) * 4 + b, (b * 16 + r) * 4 + a) for a in range(4) for r in range(16) for b in range(4)
+]
+
+
+SPREAD = [
+    ((a * 16 + r) * 4 + (2 * a - b + 2) % 4, (b * 16 + r) * 4 + a)
+    for a in range(4) for r in range(16) for b in range(4)
 ]
 
 
@@ -280,17 +301,11 @@
 
 
 def gather_bias_z(own):
-    pp = lax.ppermute
-    zz = ("zh", "zl")
-    up, down = pp(own, zz, ring(8, 1)), pp(own, zz, ring(8, 7))
-    ahead = pp(jnp.stack([down, own, up]), zz, ring(8, 3))
-    behind = pp(jnp.stack([down, own, up][1:]), zz, ring(8, 5))
-    return jnp.concatenate([own[None], up[None], ahead, behind, down[None]], axis=0)
-
-
-def gather_bias_y(col):
-    up, down, far = [lax.ppermute(col, "y", ring(4, k)) for k in (1, 3, 2)]
-    return jnp.concatenate([col, up, far, down], axis=0)
+    return jnp.stack([own] + [lax.ppermute(own, "zh", ring(4, k)) for k in (1, 2, 3)])
+
+
+def gather_bias_near(col):
+    return lax.all_to_all(jnp.broadcast_to(col[None], (8,) + col.shape), ("zl", "y"), 0, 0, tiled=True)
 
 
 def body(stack, emb, entry, final, qkg, offset, out_proj, filt):
@@ -302,22 +317,23 @@
     left = proj[:, :PF].reshape(BLK, MSA)
     right = proj[:, PF:].transpose(1, 0, 2)
     right = jnp.concatenate([right[:, :8].reshape(8 * PF, MSA), right[:, 8:].reshape(4 * PF, MSA)], axis=0)
-    pieces = gather_right(pp(right, ALL, SWAP))
-    w = final.reshape(PF, PF, CH).transpose(1, 0, 2)
-    off = jnp.pad(offset.T, ((0, 4), (0, 0)))
-    pos_a = jnp.stack([zl, y, c]).astype(jnp.int32)
-    mid, norm, bias = opm(pos_a, left, pieces, w, emb, off)
+    row0 = (zh * 16 + zl * 8 + y * 2 + c) * ROWS
+    prepared = (
+        final.reshape(PF, PF, CH).transpose(1, 0, 2),
+        jnp.pad(offset.T, ((0, 4), (0, 0))),
+        jnp.stack([zl, y, c, zh, x, row0]).astype(jnp.int32),
+    )
+    right, w, off, pos = lax.optimization_barrier((pp(right, ALL, SPREAD), *prepared))
+    mid, norm, bias = opm(pos, left, gather_right(right), w, emb, off)
+
     prev, nxt, far = [pp(norm, "x", ring(4, k)) for k in (1, 3, 2)]
     col = gather_bias_z(pp(bias, ALL, SWAP))
-    wqg = jnp.concatenate([qkg[:, :CH], qkg[:, 3 * CH :]], axis=1)
-    pay0 = gather_bias_y(col)
-    prev, nxt, far, pay0 = lax.optimization_barrier((prev, nxt, far, pay0))
+    prev, nxt, far, col = lax.optimization_barrier((prev, nxt, far, col))
+    q, gate, kv = project(norm, prev, nxt, far, qkg)
+    pay0 = gather_bias_near(col)
+    q, gate, kv, pay0 = lax.optimization_barrier((q, gate, kv, pay0))
     pay1 = pp(pay0, "c", ring(2, 1))
-
-    row0 = (zh * 16 + zl * 8 + y * 2 + c) * ROWS
-    pos_b = jnp.stack([zh * 2 + zl, y, c, x, row0]).astype(jnp.int32)
-    wkv = qkg[:, CH : 3 * CH]
-    update = attend(pos_b, filt.reshape(-1), norm, prev, nxt, far, pay0, pay1, wqg, wkv, out_proj)
+    update = attend(pos, filt, q, gate, kv, pay0, pay1, out_proj)
     return mid, update
 
 

time: 137 us -> 130 us (0.949)
  waiting for transfers between devices: 26.1 us -> 15.2 us
  Pallas kernels: 34.5 us -> 39.7 us
  starting transfers between devices: 63.8 us -> 61.9 us
    ppermute x3, starting transfers between devices: 29.7 us -> 5.65 us  [body(): prev, nxt, far = [pp(norm, 'x', ring(4, k)) for k in (1, 3, 2)]]
    ppermute x8 -> x4, starting transfers between devices: 7.84 us -> 24.4 us  [the longest x3 16.6 us: gather_bias_z(): lax.ppermute(own, 'zh', ring(4, k))]
    ppermute x8 -> x4, waiting for transfers between devices: 20 us -> 4.32 us  [the longest x3 2.72 us: gather_bias_z(): lax.ppermute(own, 'zh', ring(4, k))]
    pallas_call x0 -> x1, Pallas kernels: none -> 9.36 us  [project(): pl.pallas_call(project_kernel, grid=(ROWS,), out_shape=(jax.ShapeDtypeStr...]
    ppermute x3, waiting for transfers between devices: 0.01 us -> 5.3 us  [body(): prev, nxt, far = [pp(norm, 'x', ring(4, k)) for k in (1, 3, 2)]]
    pallas_call x1, Pallas kernels: 23.5 us -> 19.4 us  [attend(): pl.pallas_call(attend_kernel, grid=(ROWS,), out_shape=jax.ShapeDtypeStruc...]
    all_to_all x0 -> x1, starting transfers between devices: none -> 3.55 us  [gather_bias_near(): lax.all_to_all(jnp.broadcast_to(col[None], (8,) + col.shape), ('zl', 'y')...]
    ppermute x1, starting transfers between devices: 5.6 us -> 2.22 us  [body(): pay1 = pp(pay0, 'c', ring(2, 1))]
  transfers between devices with their start and end apart: 28 -> 25, of which waited for: 8 -> 11; matrix products, arithmetic and copies ran while one was open for 3% -> 2% of each run, Pallas kernels for 0% -> 7%
where the time goes in v1:
time: 130 us; the launch traced here: 129 us
  starting transfers between devices  61.9 us (48%)
  Pallas kernels  39.7 us (31%)
  waiting for transfers between devices  15.2 us (12%)
  local copies, waits for them, and re-layouts  5.49 us (4%)
  other arithmetic  4.42 us (3%)
  matrix products  1.31 us (1%)
    pallas_call x1, Pallas kernels, attend(): pl.pallas_call(attend_kernel, grid=(ROWS,), out_shape=jax.ShapeDtypeStruc...  19.4 us
    ppermute x3, starting transfers between devices, gather_bias_z(): lax.ppermute(own, 'zh', ring(4, k))  16.6 us
    ppermute x8, starting transfers between devices, gather_right(): return mine + [pp(m, 'c', ring(2, 1)) for m in mine]  11.8 us
    pallas_call x1, Pallas kernels, opm(): pl.pallas_call(opm_kernel, out_shape=(jax.ShapeDtypeStruct((ROWS, COLS, C...  11 us
    pallas_call x1, Pallas kernels, project(): pl.pallas_call(project_kernel, grid=(ROWS,), out_shape=(jax.ShapeDtypeStr...  9.36 us
    ppermute x1, starting transfers between devices, body(): pp(right, ALL, SPREAD)  7.81 us
    ppermute x3, starting transfers between devices, body(): prev, nxt, far = [pp(norm, 'x', ring(4, k)) for k in (1, 3, 2)]  5.65 us
    ppermute x3, waiting for transfers between devices, body(): prev, nxt, far = [pp(norm, 'x', ring(4, k)) for k in (1, 3, 2)]  5.3 us
  transfers between devices with their start and end apart: 25, of which 11 were waited for; matrix products, arithmetic and copies ran while one was open for 2% of the time, Pallas kernels for 7%

profile of v1, /device:TPU:1, one launch (start us, length us, event | category | flops | bytes accessed | tf_op | source)
XLA Modules:
  0.0 128.9 jit_solution(5155035373577967134)
XLA Ops:
  0.7 2.0 %convert_reduce_fusion = f32[256,12]{0,1:T(8,128)S(1)} fusion(bf16[256,12,256]{2,0,1:T(8,128)(2,1)} %param.8), kind=kLoop, calls=%fused_computation.1 | loop fusion | flops 1569792 | bytes 1585152 | tf_op jit(solution)/shard_map/reduce_sum | solution.py:276
  2.7 2.4 %fusion.2 = f32[256,12]{0,1:T(8,128)S(1)} fusion(bf16[256,12,256]{2,0,1:T(8,128)(2,1)} %param.8, f32[256,12]{0,1:T(8,128)S(1)} %broadcast_multiply_fusion), kind=kLoop, calls=%fused_computation.4 | loop fusion | flops 3142656 | bytes 1597440 | tf_op jit(solution)/shard_map/reduce_sum | solution.py:277
  5.1 1.3 %fusion.11 = bf16[12,64,256]{2,1,0:T(8,128)(2,1)S(1)} fusion(bf16[256,12,256]{2,0,1:T(8,128)(2,1)S(1)} %copy-done.1, f32[256,12]{0,1:T(8,128)S(1)} %add_rsqrt_fusion, f32[256,12]{0,1:T(8,128)S(1)} %broadcast_multiply_fusion, bf16[256,64]{0,1:T(8,128)(2,1)S(1)} %copy-done), kind=kOutput, calls=%fused_computation.10 | convolution fusion | flops 104005632 | bytes 2023424 | tf_op jit(solution)/shard_map/sjc,cx->jxs/dot_general | solution.py:316
  7.3 7.8 %collective-permute-start = (bf16[384,256]{1,0:T(8,128)(2,1)S(1)}, bf16[384,256]{1,0:T(8,128)(2,1)S(1)}, u32[]{:S(2)}, u32[]{:S(2)}) collective-permute-start(bf16[384,256]{1,0:T(8,128)(2,1)S(1)} %pad_maximum_fusion), channel_id=1, source_target_pairs={{2,0},{1,64},{0,128},{3,192},{6,4},{5,68},{4,132},{7,196},{10,8},{... | collective-permute-start | bytes 589832 | tf_op jit(solution)/shard_map/ppermute | solution.py:326
  17.1 1.6 %collective-permute-done.refs_0_ = bf16[384,256]{1,0:T(8,128)(2,1)S(1)} collective-permute-done((bf16[384,256]{1,0:T(8,128)(2,1)S(1)}, bf16[384,256]{1,0:T(8,128)(2,1)S(1)}, u32[]{:S(2)}, u32[]{:S(2)}) %collective-permute-start) | collective-permute-done | bytes 196640 | tf_op jit(solution)/shard_map/ppermute | solution.py:326
  18.7 3.5 %collective-permute-start.1 = (bf16[384,256]{1,0:T(8,128)(2,1)S(1)}, bf16[384,256]{1,0:T(8,128)(2,1)S(1)}, u32[]{:S(2)}, u32[]{:S(2)}) collective-permute-start(bf16[384,256]{1,0:T(8,128)(2,1)S(1)} %collective-permute-done.refs_0_), channel_id=1, source_target_pairs={{0,32},{32,0},{1,33},{33,1},{2,34},{34,2},{3,35},{35,3},{4,36},{36... | collective-permute-start | bytes 589832 | tf_op jit(solution)/shard_map/ppermute | solution.py:295
  22.2 1.3 %collective-permute-start.2 = (bf16[384,256]{1,0:T(8,128)(2,1)S(1)}, bf16[384,256]{1,0:T(8,128)(2,1)S(1)}, u32[]{:S(2)}, u32[]{:S(2)}) collective-permute-start(bf16[384,256]{1,0:T(8,128)(2,1)S(1)} %collective-permute-done.refs_0_), channel_id=1, source_target_pairs={{0,8},{8,16},{16,24},{24,0},{1,9},{9,17},{17,25},{25,1},{2,10},{10... | collective-permute-start | bytes 589832 | tf_op jit(solution)/shard_map/ppermute | solution.py:296
  23.5 2.6 %collective-permute-start.4 = (bf16[384,256]{1,0:T(8,128)(2,1)S(1)}, bf16[384,256]{1,0:T(8,128)(2,1)S(1)}, u32[]{:S(2)}, u32[]{:S(2)}) collective-permute-start(bf16[384,256]{1,0:T(8,128)(2,1)S(1)} %collective-permute-done.refs_0_), channel_id=1, source_target_pairs={{0,16},{8,24},{16,0},{24,8},{1,17},{9,25},{17,1},{25,9},{2,18},{10... | collective-permute-start | bytes 589832 | tf_op jit(solution)/shard_map/ppermute | solution.py:296
  26.2 1.1 collective-permute-start.3
  27.2 3.9 %collective-permute-start.8 = (bf16[384,256]{1,0:T(8,128)(2,1)S(1)}, bf16[384,256]{1,0:T(8,128)(2,1)S(1)}, u32[]{:S(2)}, u32[]{:S(2)}) collective-permute-start(bf16[384,256]{1,0:T(8,128)(2,1)S(1)} %collective-permute-done.refs_0_), channel_id=1, source_target_pairs={{0,4},{4,0},{1,5},{5,1},{2,6},{6,2},{3,7},{7,3},{8,12},{12,8},{9,1... | collective-permute-start | bytes 589832 | tf_op jit(solution)/shard_map/ppermute | solution.py:300
  31.6 2.3 %collective-permute-start.6 = (bf16[384,256]{1,0:T(8,128)(2,1)S(1)}, bf16[384,256]{1,0:T(8,128)(2,1)S(1)}, u32[]{:S(2)}, u32[]{:S(2)}) collective-permute-start(bf16[384,256]{1,0:T(8,128)(2,1)S(1)} %collective-permute-done.1.refs_1_), channel_id=1, source_target_pairs={{0,24},{8,0},{16,8},{24,16},{1,25},{9,1},{17,9},{25,17},{2,26},{10... | collective-permute-start | bytes 589832 | tf_op jit(solution)/shard_map/ppermute | solution.py:297
  33.9 1.7 %collective-permute-start.7 = (bf16[384,256]{1,0:T(8,128)(2,1)S(1)}, bf16[384,256]{1,0:T(8,128)(2,1)S(1)}, u32[]{:S(2)}, u32[]{:S(2)}) collective-permute-start(bf16[384,256]{1,0:T(8,128)(2,1)S(1)} %collective-permute-done.4.refs_4_), channel_id=1, source_target_pairs={{0,32},{32,0},{1,33},{33,1},{2,34},{34,2},{3,35},{35,3},{4,36},{36... | collective-permute-start | bytes 589832 | tf_op jit(solution)/shard_map/ppermute | solution.py:298
  35.6 3.8 %collective-permute-start.9 = (bf16[384,256]{1,0:T(8,128)(2,1)S(1)}, bf16[384,256]{1,0:T(8,128)(2,1)S(1)}, u32[]{:S(2)}, u32[]{:S(2)}) collective-permute-start(bf16[384,256]{1,0:T(8,128)(2,1)S(1)} %collective-permute-done.1.refs_1_), channel_id=1, source_target_pairs={{0,4},{4,0},{1,5},{5,1},{2,6},{6,2},{3,7},{7,3},{8,12},{12,8},{9,1... | collective-permute-start | bytes 589832 | tf_op jit(solution)/shard_map/ppermute | solution.py:300
  39.5 1.2 collective-permute-done.5.refs_5_
  41.4 2.7 %collective-permute-start.13 = (bf16[384,256]{1,0:T(8,128)(2,1)S(1)}, bf16[384,256]{1,0:T(8,128)(2,1)S(1)}, u32[]{:S(2)}, u32[]{:S(2)}) collective-permute-start(bf16[384,256]{1,0:T(8,128)(2,1)S(1)} %collective-permute-done.5.refs_5_), channel_id=1, source_target_pairs={{0,4},{4,0},{1,5},{5,1},{2,6},{6,2},{3,7},{7,3},{8,12},{12,8},{9,1... | collective-permute-start | bytes 589832 | tf_op jit(solution)/shard_map/ppermute | solution.py:300
  46.5 11.0 %opm.1 = (bf16[12,192,128]{2,1,0:T(8,128)(2,1)}, bf16[12,192,128]{2,1,0:T(8,128)(2,1)}, bf16[48,256]{1,0:T(8,128)(2,1)}) custom-call(s32[6]{0:T(128)} %stack.42.pos_ref, bf16[384,256]{1,0:T(8,128)(2,1)} %bitcast.29, bf16[384,256]{1,0:T(8,128)(2,1)} %copy-done.9, bf16[384,256]{1,0:T(8,128)(2,1)} %copy-done.10, bf16[384,256]{1,0:T(8,128)(2,1)} %copy-done.11, ...), custom_call_target="tpu_custom_call" | custom-call | flops 6000000000 | bytes 10000000 | tf_op jit(solution)/shard_map/opm/pallas_call | solution.py:144
  57.6 4.5 %collective-permute-start.17 = (bf16[12,192,128]{2,1,0:T(8,128)(2,1)}, bf16[12,192,128]{2,1,0:T(8,128)(2,1)S(1)}, u32[]{:S(2)}, u32[]{:S(2)}) collective-permute-start(bf16[12,192,128]{2,1,0:T(8,128)(2,1)} %get-tuple-element.25.own_ref), channel_id=1, source_target_pairs={{0,3},{1,0},{2,1},{3,2},{4,7},{5,4},{6,5},{7,6},{8,11},{9,8},{10,9... | collective-permute-start | bytes 1769480 | tf_op jit(solution)/shard_map/ppermute | solution.py:329
  62.1 1.1 collective-permute-start.18
  63.2 1.4 %collective-permute-start.19 = (bf16[48,256]{1,0:T(8,128)(2,1)}, bf16[48,256]{1,0:T(8,128)(2,1)S(1)}, u32[]{:S(2)}, u32[]{:S(2)}) collective-permute-start(bf16[48,256]{1,0:T(8,128)(2,1)} %get-tuple-element.26), channel_id=1, source_target_pairs={{0,0},{1,64},{2,128},{3,192},{4,4},{5,68},{6,132},{7,196},{8,8},{9... | collective-permute-start | bytes 73736 | tf_op jit(solution)/shard_map/ppermute | solution.py:330
  64.5 11.1 %collective-permute-start.22 = (bf16[48,256]{1,0:T(8,128)(2,1)S(1)}, bf16[48,256]{1,0:T(8,128)(2,1)S(1)}, u32[]{:S(2)}, u32[]{:S(2)}) collective-permute-start(bf16[48,256]{1,0:T(8,128)(2,1)S(1)} %collective-permute-done.19), channel_id=1, source_target_pairs={{0,192},{64,0},{128,64},{192,128},{1,193},{65,1},{129,65},{193,129... | collective-permute-start | bytes 73736 | tf_op jit(solution)/shard_map/ppermute | solution.py:304
  75.7 3.1 %collective-permute-start.21 = (bf16[48,256]{1,0:T(8,128)(2,1)S(1)}, bf16[48,256]{1,0:T(8,128)(2,1)S(1)}, u32[]{:S(2)}, u32[]{:S(2)}) collective-permute-start(bf16[48,256]{1,0:T(8,128)(2,1)S(1)} %collective-permute-done.19), channel_id=1, source_target_pairs={{0,128},{64,192},{128,0},{192,64},{1,129},{65,193},{129,1},{193,65... | collective-permute-start | bytes 73736 | tf_op jit(solution)/shard_map/ppermute | solution.py:304
  78.8 2.4 %collective-permute-start.20 = (bf16[48,256]{1,0:T(8,128)(2,1)S(1)}, bf16[48,256]{1,0:T(8,128)(2,1)S(1)}, u32[]{:S(2)}, u32[]{:S(2)}) collective-permute-start(bf16[48,256]{1,0:T(8,128)(2,1)S(1)} %collective-permute-done.19), channel_id=1, source_target_pairs={{0,64},{64,128},{128,192},{192,0},{1,65},{65,129},{129,193},{193,1... | collective-permute-start | bytes 73736 | tf_op jit(solution)/shard_map/ppermute | solution.py:304
  81.1 1.1 collective-permute-done.21
  82.3 1.6 %collective-permute-done.20 = bf16[48,256]{1,0:T(8,128)(2,1)S(1)} collective-permute-done((bf16[48,256]{1,0:T(8,128)(2,1)S(1)}, bf16[48,256]{1,0:T(8,128)(2,1)S(1)}, u32[]{:S(2)}, u32[]{:S(2)}) %collective-permute-start.20) | collective-permute-done | bytes 24608 | tf_op jit(solution)/shard_map/ppermute | solution.py:304
  83.9 4.1 %collective-permute-done.17.next_ref = bf16[12,192,128]{2,1,0:T(8,128)(2,1)S(1)} collective-permute-done((bf16[12,192,128]{2,1,0:T(8,128)(2,1)}, bf16[12,192,128]{2,1,0:T(8,128)(2,1)S(1)}, u32[]{:S(2)}, u32[]{:S(2)}) %collective-permute-start.17) | collective-permute-done | bytes 589856 | tf_op jit(solution)/shard_map/ppermute | solution.py:329
  88.0 1.2 collective-permute-done.18.far_ref
  90.2 3.5 %all-to-all-start = ((bf16[8,4,48,256]{3,2,1,0:T(8,128)(2,1)}), bf16[8,4,48,256]{3,2,1,0:T(8,128)(2,1)S(1)}, u32[]{:S(2)}, u32[]{:S(2)}) async-start(bf16[8,4,48,256]{3,2,1,0:T(8,128)(2,1)} %broadcast_in_dim.2), calls=%async_computation | async-start | bytes 1572864 | tf_op jit(solution)/shard_map/all_to_all | solution.py:308
  93.8 9.4 %project.1 = (bf16[12,192,128]{2,1,0:T(8,128)(2,1)}, f32[12,192,128]{2,1,0:T(8,128)}, bf16[12,768,256]{2,1,0:T(8,128)(2,1)}) custom-call(bf16[12,192,128]{2,1,0:T(8,128)(2,1)} %get-tuple-element.25.own_ref, bf16[12,192,128]{2,1,0:T(8,128)(2,1)} %copy-done.6, bf16[12,192,128]{2,1,0:T(8,128)(2,1)} %copy-done.7, bf16[12,192,128]{2,1,0:T(8,128)(2,1)} %copy-done.8, ...), custom_call_target="tpu_custom_call" | custom-call | flops 10000000000 | bytes 20000000 | tf_op jit(solution)/shard_map/project/pallas_call | solution.py:177
  103.2 1.2 all-to-all-done.pay0_ref
  104.4 2.2 %collective-permute-start.23 = (bf16[8,4,48,256]{3,2,1,0:T(8,128)(2,1)S(1)}, bf16[8,4,48,256]{3,2,1,0:T(8,128)(2,1)S(1)}, u32[]{:S(2)}, u32[]{:S(2)}) collective-permute-start(bf16[8,4,48,256]{3,2,1,0:T(8,128)(2,1)S(1)} %all-to-all-done.pay0_ref), channel_id=1, source_target_pairs={{0,4},{4,0},{1,5},{5,1},{2,6},{6,2},{3,7},{7,3},{8,12},{12,8},{9,1... | collective-permute-start | bytes 2359304 | tf_op jit(solution)/shard_map/ppermute | solution.py:335
  106.6 1.9 %collective-permute-done.23.pay1_ref = bf16[8,4,48,256]{3,2,1,0:T(8,128)(2,1)S(1)} collective-permute-done((bf16[8,4,48,256]{3,2,1,0:T(8,128)(2,1)S(1)}, bf16[8,4,48,256]{3,2,1,0:T(8,128)(2,1)S(1)}, u32[]{:S(2)}, u32[]{:S(2)}) %collective-permute-start.23) | collective-permute-done | bytes 786464 | tf_op jit(solution)/shard_map/ppermute | solution.py:335
  109.5 19.4 %attend.1 = bf16[12,192,128]{2,1,0:T(8,128)(2,1)} custom-call(s32[6]{0:T(128)} %stack.42.pos_ref, s32[6,6]{1,0:T(8,128)} %filt_ref.1, bf16[12,192,128]{2,1,0:T(8,128)(2,1)} %get-tuple-element.34.q_ref, f32[12,192,128]{2,1,0:T(8,128)} %get-tuple-element.35.gate_ref, bf16[12,768,256]{2,1,0:T(8,128)(2,1)} %get-tuple-element.36.kv_ref, ...), custom_call_target="tpu_custom_call" | custom-call | flops 8000000000 | bytes 10000000 | tf_op jit(solution)/shard_map/attend/pallas_call | solution.py:261
  (88 shorter events, 8.6 us)
Async XLA Ops:
  2.7 12.5 %copy-start.3 = (bf16[1024,128]{1,0:T(8,128)(2,1)S(1)}, bf16[1024,128]{1,0:T(8,128)(2,1)}, u32[]{:S(2)}) copy-start(bf16[1024,128]{1,0:T(8,128)(2,1)} %param.11) | copy-start | bytes 786436
  5.1 10.9 %copy-start.4 = (f32[128,4]{0,1:T(4,128)S(1)}, f32[128,4]{0,1:T(4,128)}, u32[]{:S(2)}) copy-start(f32[128,4]{0,1:T(4,128)} %param.13) | copy-start | bytes 6148
  7.3 11.4 %collective-permute-start = (bf16[384,256]{1,0:T(8,128)(2,1)S(1)}, bf16[384,256]{1,0:T(8,128)(2,1)S(1)}, u32[]{:S(2)}, u32[]{:S(2)}) collective-permute-start(bf16[384,256]{1,0:T(8,128)(2,1)S(1)} %pad_maximum_fusion), channel_id=1, source_target_pairs={{2,0},{1,64},{0,128},{3,192},{6,4},{5,68},{4,132},{7,196},{10,8},{... | collective-permute-start | bytes 589832 | tf_op jit(solution)/shard_map/ppermute | solution.py:326
  18.7 27.1 %copy-start.9 = (bf16[384,256]{1,0:T(8,128)(2,1)}, bf16[384,256]{1,0:T(8,128)(2,1)S(1)}, u32[]{:S(2)}) copy-start(bf16[384,256]{1,0:T(8,128)(2,1)S(1)} %collective-permute-done.refs_0_) | copy-start | bytes 589828
  18.7 12.4 %collective-permute-start.1 = (bf16[384,256]{1,0:T(8,128)(2,1)S(1)}, bf16[384,256]{1,0:T(8,128)(2,1)S(1)}, u32[]{:S(2)}, u32[]{:S(2)}) collective-permute-start(bf16[384,256]{1,0:T(8,128)(2,1)S(1)} %collective-permute-done.refs_0_), channel_id=1, source_target_pairs={{0,32},{32,0},{1,33},{33,1},{2,34},{34,2},{3,35},{35,3},{4,36},{36... | collective-permute-start | bytes 589832 | tf_op jit(solution)/shard_map/ppermute | solution.py:295
  22.2 9.3 %collective-permute-start.2 = (bf16[384,256]{1,0:T(8,128)(2,1)S(1)}, bf16[384,256]{1,0:T(8,128)(2,1)S(1)}, u32[]{:S(2)}, u32[]{:S(2)}) collective-permute-start(bf16[384,256]{1,0:T(8,128)(2,1)S(1)} %collective-permute-done.refs_0_), channel_id=1, source_target_pairs={{0,8},{8,16},{16,24},{24,0},{1,9},{9,17},{17,25},{25,1},{2,10},{10... | collective-permute-start | bytes 589832 | tf_op jit(solution)/shard_map/ppermute | solution.py:296
  23.5 10.3 %collective-permute-start.4 = (bf16[384,256]{1,0:T(8,128)(2,1)S(1)}, bf16[384,256]{1,0:T(8,128)(2,1)S(1)}, u32[]{:S(2)}, u32[]{:S(2)}) collective-permute-start(bf16[384,256]{1,0:T(8,128)(2,1)S(1)} %collective-permute-done.refs_0_), channel_id=1, source_target_pairs={{0,16},{8,24},{16,0},{24,8},{1,17},{9,25},{17,1},{25,9},{2,18},{10... | collective-permute-start | bytes 589832 | tf_op jit(solution)/shard_map/ppermute | solution.py:296
  26.2 9.4 %collective-permute-start.3 = (bf16[384,256]{1,0:T(8,128)(2,1)S(1)}, bf16[384,256]{1,0:T(8,128)(2,1)S(1)}, u32[]{:S(2)}, u32[]{:S(2)}) collective-permute-start(bf16[384,256]{1,0:T(8,128)(2,1)S(1)} %collective-permute-done.refs_0_), channel_id=1, source_target_pairs={{0,24},{8,0},{16,8},{24,16},{1,25},{9,1},{17,9},{25,17},{2,26},{10... | collective-permute-start | bytes 589832 | tf_op jit(solution)/shard_map/ppermute | solution.py:296
  27.2 12.1 %collective-permute-start.8 = (bf16[384,256]{1,0:T(8,128)(2,1)S(1)}, bf16[384,256]{1,0:T(8,128)(2,1)S(1)}, u32[]{:S(2)}, u32[]{:S(2)}) collective-permute-start(bf16[384,256]{1,0:T(8,128)(2,1)S(1)} %collective-permute-done.refs_0_), channel_id=1, source_target_pairs={{0,4},{4,0},{1,5},{5,1},{2,6},{6,2},{3,7},{7,3},{8,12},{12,8},{9,1... | collective-permute-start | bytes 589832 | tf_op jit(solution)/shard_map/ppermute | solution.py:300
  31.1 14.7 %copy-start.10 = (bf16[384,256]{1,0:T(8,128)(2,1)}, bf16[384,256]{1,0:T(8,128)(2,1)S(1)}, u32[]{:S(2)}) copy-start(bf16[384,256]{1,0:T(8,128)(2,1)S(1)} %collective-permute-done.1.refs_1_) | copy-start | bytes 589828
  31.2 9.5 %collective-permute-start.5 = (bf16[384,256]{1,0:T(8,128)(2,1)S(1)}, bf16[384,256]{1,0:T(8,128)(2,1)S(1)}, u32[]{:S(2)}, u32[]{:S(2)}) collective-permute-start(bf16[384,256]{1,0:T(8,128)(2,1)S(1)} %collective-permute-done.1.refs_1_), channel_id=1, source_target_pairs={{0,8},{8,16},{16,24},{24,0},{1,9},{9,17},{17,25},{25,1},{2,10},{10... | collective-permute-start | bytes 589832 | tf_op jit(solution)/shard_map/ppermute | solution.py:297
  31.6 14.3 %copy-start.11 = (bf16[384,256]{1,0:T(8,128)(2,1)}, bf16[384,256]{1,0:T(8,128)(2,1)S(1)}, u32[]{:S(2)}) copy-start(bf16[384,256]{1,0:T(8,128)(2,1)S(1)} %collective-permute-done.2.refs_2_) | copy-start | bytes 589828
  31.6 9.7 %collective-permute-start.6 = (bf16[384,256]{1,0:T(8,128)(2,1)S(1)}, bf16[384,256]{1,0:T(8,128)(2,1)S(1)}, u32[]{:S(2)}, u32[]{:S(2)}) collective-permute-start(bf16[384,256]{1,0:T(8,128)(2,1)S(1)} %collective-permute-done.1.refs_1_), channel_id=1, source_target_pairs={{0,24},{8,0},{16,8},{24,16},{1,25},{9,1},{17,9},{25,17},{2,26},{10... | collective-permute-start | bytes 589832 | tf_op jit(solution)/shard_map/ppermute | solution.py:297
  33.9 12.0 %copy-start.12 = (bf16[384,256]{1,0:T(8,128)(2,1)}, bf16[384,256]{1,0:T(8,128)(2,1)S(1)}, u32[]{:S(2)}) copy-start(bf16[384,256]{1,0:T(8,128)(2,1)S(1)} %collective-permute-done.4.refs_4_) | copy-start | bytes 589828
  33.9 7.6 %collective-permute-start.7 = (bf16[384,256]{1,0:T(8,128)(2,1)S(1)}, bf16[384,256]{1,0:T(8,128)(2,1)S(1)}, u32[]{:S(2)}, u32[]{:S(2)}) collective-permute-start(bf16[384,256]{1,0:T(8,128)(2,1)S(1)} %collective-permute-done.4.refs_4_), channel_id=1, source_target_pairs={{0,32},{32,0},{1,33},{33,1},{2,34},{34,2},{3,35},{35,3},{4,36},{36... | collective-permute-start | bytes 589832 | tf_op jit(solution)/shard_map/ppermute | solution.py:298
  35.6 10.3 %copy-start.13 = (bf16[384,256]{1,0:T(8,128)(2,1)}, bf16[384,256]{1,0:T(8,128)(2,1)S(1)}, u32[]{:S(2)}) copy-start(bf16[384,256]{1,0:T(8,128)(2,1)S(1)} %collective-permute-done.3.refs_3_) | copy-start | bytes 589828
  35.6 8.5 %collective-permute-start.9 = (bf16[384,256]{1,0:T(8,128)(2,1)S(1)}, bf16[384,256]{1,0:T(8,128)(2,1)S(1)}, u32[]{:S(2)}, u32[]{:S(2)}) collective-permute-start(bf16[384,256]{1,0:T(8,128)(2,1)S(1)} %collective-permute-done.1.refs_1_), channel_id=1, source_target_pairs={{0,4},{4,0},{1,5},{5,1},{2,6},{6,2},{3,7},{7,3},{8,12},{12,8},{9,1... | collective-permute-start | bytes 589832 | tf_op jit(solution)/shard_map/ppermute | solution.py:300
  39.4 4.8 %collective-permute-start.10 = (bf16[384,256]{1,0:T(8,128)(2,1)S(1)}, bf16[384,256]{1,0:T(8,128)(2,1)S(1)}, u32[]{:S(2)}, u32[]{:S(2)}) collective-permute-start(bf16[384,256]{1,0:T(8,128)(2,1)S(1)} %collective-permute-done.2.refs_2_), channel_id=1, source_target_pairs={{0,4},{4,0},{1,5},{5,1},{2,6},{6,2},{3,7},{7,3},{8,12},{12,8},{9,1... | collective-permute-start | bytes 589832 | tf_op jit(solution)/shard_map/ppermute | solution.py:300
  40.6 4.0 %collective-permute-start.12 = (bf16[384,256]{1,0:T(8,128)(2,1)S(1)}, bf16[384,256]{1,0:T(8,128)(2,1)S(1)}, u32[]{:S(2)}, u32[]{:S(2)}) collective-permute-start(bf16[384,256]{1,0:T(8,128)(2,1)S(1)} %collective-permute-done.4.refs_4_), channel_id=1, source_target_pairs={{0,4},{4,0},{1,5},{5,1},{2,6},{6,2},{3,7},{7,3},{8,12},{12,8},{9,1... | collective-permute-start | bytes 589832 | tf_op jit(solution)/shard_map/ppermute | solution.py:300
  41.3 3.3 %collective-permute-start.11 = (bf16[384,256]{1,0:T(8,128)(2,1)S(1)}, bf16[384,256]{1,0:T(8,128)(2,1)S(1)}, u32[]{:S(2)}, u32[]{:S(2)}) collective-permute-start(bf16[384,256]{1,0:T(8,128)(2,1)S(1)} %collective-permute-done.3.refs_3_), channel_id=1, source_target_pairs={{0,4},{4,0},{1,5},{5,1},{2,6},{6,2},{3,7},{7,3},{8,12},{12,8},{9,1... | collective-permute-start | bytes 589832 | tf_op jit(solution)/shard_map/ppermute | solution.py:300
  41.4 3.8 %collective-permute-start.13 = (bf16[384,256]{1,0:T(8,128)(2,1)S(1)}, bf16[384,256]{1,0:T(8,128)(2,1)S(1)}, u32[]{:S(2)}, u32[]{:S(2)}) collective-permute-start(bf16[384,256]{1,0:T(8,128)(2,1)S(1)} %collective-permute-done.5.refs_5_), channel_id=1, source_target_pairs={{0,4},{4,0},{1,5},{5,1},{2,6},{6,2},{3,7},{7,3},{8,12},{12,8},{9,1... | collective-permute-start | bytes 589832 | tf_op jit(solution)/shard_map/ppermute | solution.py:300
  44.1 1.4 %collective-permute-start.14 = (bf16[384,256]{1,0:T(8,128)(2,1)S(1)}, bf16[384,256]{1,0:T(8,128)(2,1)S(1)}, u32[]{:S(2)}, u32[]{:S(2)}) collective-permute-start(bf16[384,256]{1,0:T(8,128)(2,1)S(1)} %collective-permute-done.6.refs_6_), channel_id=1, source_target_pairs={{0,4},{4,0},{1,5},{5,1},{2,6},{6,2},{3,7},{7,3},{8,12},{12,8},{9,1... | collective-permute-start | bytes 589832 | tf_op jit(solution)/shard_map/ppermute | solution.py:300
  44.2 1.6 %collective-permute-start.15 = (bf16[384,256]{1,0:T(8,128)(2,1)S(1)}, bf16[384,256]{1,0:T(8,128)(2,1)S(1)}, u32[]{:S(2)}, u32[]{:S(2)}) collective-permute-start(bf16[384,256]{1,0:T(8,128)(2,1)S(1)} %collective-permute-done.7.refs_7_), channel_id=1, source_target_pairs={{0,4},{4,0},{1,5},{5,1},{2,6},{6,2},{3,7},{7,3},{8,12},{12,8},{9,1... | collective-permute-start | bytes 589832 | tf_op jit(solution)/shard_map/ppermute | solution.py:300
  57.5 26.4 %collective-permute-start.16 = (bf16[12,192,128]{2,1,0:T(8,128)(2,1)}, bf16[12,192,128]{2,1,0:T(8,128)(2,1)S(1)}, u32[]{:S(2)}, u32[]{:S(2)}) collective-permute-start(bf16[12,192,128]{2,1,0:T(8,128)(2,1)} %get-tuple-element.25.own_ref), channel_id=1, source_target_pairs={{0,1},{1,2},{2,3},{3,0},{4,5},{5,6},{6,7},{7,4},{8,9},{9,10},{10,1... | collective-permute-start | bytes 1769480 | tf_op jit(solution)/shard_map/ppermute | solution.py:329
  57.6 30.4 %collective-permute-start.17 = (bf16[12,192,128]{2,1,0:T(8,128)(2,1)}, bf16[12,192,128]{2,1,0:T(8,128)(2,1)S(1)}, u32[]{:S(2)}, u32[]{:S(2)}) collective-permute-start(bf16[12,192,128]{2,1,0:T(8,128)(2,1)} %get-tuple-element.25.own_ref), channel_id=1, source_target_pairs={{0,3},{1,0},{2,1},{3,2},{4,7},{5,4},{6,5},{7,6},{8,11},{9,8},{10,9... | collective-permute-start | bytes 1769480 | tf_op jit(solution)/shard_map/ppermute | solution.py:329
  62.1 27.1 %collective-permute-start.18 = (bf16[12,192,128]{2,1,0:T(8,128)(2,1)}, bf16[12,192,128]{2,1,0:T(8,128)(2,1)S(1)}, u32[]{:S(2)}, u32[]{:S(2)}) collective-permute-start(bf16[12,192,128]{2,1,0:T(8,128)(2,1)} %get-tuple-element.25.own_ref), channel_id=1, source_target_pairs={{0,2},{1,3},{2,0},{3,1},{4,6},{5,7},{6,4},{7,5},{8,10},{9,11},{10,... | collective-permute-start | bytes 1769480 | tf_op jit(solution)/shard_map/ppermute | solution.py:329
  63.2 1.4 %collective-permute-start.19 = (bf16[48,256]{1,0:T(8,128)(2,1)}, bf16[48,256]{1,0:T(8,128)(2,1)S(1)}, u32[]{:S(2)}, u32[]{:S(2)}) collective-permute-start(bf16[48,256]{1,0:T(8,128)(2,1)} %get-tuple-element.26), channel_id=1, source_target_pairs={{0,0},{1,64},{2,128},{3,192},{4,4},{5,68},{6,132},{7,196},{8,8},{9... | collective-permute-start | bytes 73736 | tf_op jit(solution)/shard_map/ppermute | solution.py:330
  64.5 14.2 %collective-permute-start.22 = (bf16[48,256]{1,0:T(8,128)(2,1)S(1)}, bf16[48,256]{1,0:T(8,128)(2,1)S(1)}, u32[]{:S(2)}, u32[]{:S(2)}) collective-permute-start(bf16[48,256]{1,0:T(8,128)(2,1)S(1)} %collective-permute-done.19), channel_id=1, source_target_pairs={{0,192},{64,0},{128,64},{192,128},{1,193},{65,1},{129,65},{193,129... | collective-permute-start | bytes 73736 | tf_op jit(solution)/shard_map/ppermute | solution.py:304
  75.7 6.6 %collective-permute-start.21 = (bf16[48,256]{1,0:T(8,128)(2,1)S(1)}, bf16[48,256]{1,0:T(8,128)(2,1)S(1)}, u32[]{:S(2)}, u32[]{:S(2)}) collective-permute-start(bf16[48,256]{1,0:T(8,128)(2,1)S(1)} %collective-permute-done.19), channel_id=1, source_target_pairs={{0,128},{64,192},{128,0},{192,64},{1,129},{65,193},{129,1},{193,65... | collective-permute-start | bytes 73736 | tf_op jit(solution)/shard_map/ppermute | solution.py:304
  78.8 5.1 %collective-permute-start.20 = (bf16[48,256]{1,0:T(8,128)(2,1)S(1)}, bf16[48,256]{1,0:T(8,128)(2,1)S(1)}, u32[]{:S(2)}, u32[]{:S(2)}) collective-permute-start(bf16[48,256]{1,0:T(8,128)(2,1)S(1)} %collective-permute-done.19), channel_id=1, source_target_pairs={{0,64},{64,128},{128,192},{192,0},{1,65},{65,129},{129,193},{193,1... | collective-permute-start | bytes 73736 | tf_op jit(solution)/shard_map/ppermute | solution.py:304
  90.2 14.2 %all-to-all-start = ((bf16[8,4,48,256]{3,2,1,0:T(8,128)(2,1)}), bf16[8,4,48,256]{3,2,1,0:T(8,128)(2,1)S(1)}, u32[]{:S(2)}, u32[]{:S(2)}) async-start(bf16[8,4,48,256]{3,2,1,0:T(8,128)(2,1)} %broadcast_in_dim.2), calls=%async_computation | async-start | bytes 1572864 | tf_op jit(solution)/shard_map/all_to_all | solution.py:308
  104.4 4.1 %collective-permute-start.23 = (bf16[8,4,48,256]{3,2,1,0:T(8,128)(2,1)S(1)}, bf16[8,4,48,256]{3,2,1,0:T(8,128)(2,1)S(1)}, u32[]{:S(2)}, u32[]{:S(2)}) collective-permute-start(bf16[8,4,48,256]{3,2,1,0:T(8,128)(2,1)S(1)} %all-to-all-done.pay0_ref), channel_id=1, source_target_pairs={{0,4},{4,0},{1,5},{5,1},{2,6},{6,2},{3,7},{7,3},{8,12},{12,8},{9,1... | collective-permute-start | bytes 2359304 | tf_op jit(solution)/shard_map/ppermute | solution.py:335
  (18 other events, 63.5 us)

commit v2 on v1

--- a/solution.py
+++ b/solution.py
@@ -47,12 +47,12 @@
             even = jnp.where(low, b[0], jnp.roll(b[1], 4, axis=1))
             odd = jnp.where(low, jnp.roll(b[0], 4, axis=1), b[1])
             tiles.append((a[0], a[1], (even, odd)))
-        rows = pl.multiple_of(q * COLS + t * 4 * ROWS, 16)
+        rows = q * COLS + t * 4 * ROWS
         for ch in range(PF):
             six = []
             for a0, a1, eo in tiles:
                 six += [a0[ch], a1[ch], eo[ch % 2][ch // 2]]
-            lhs[pl.ds(rows, 4 * ROWS), ch * LANES : (ch + 1) * LANES] = jnp.concatenate(six, axis=0).astype(BF)
+            lhs[rows : rows + 4 * ROWS, ch * LANES : (ch + 1) * LANES] = jnp.concatenate(six, axis=0).astype(BF)
 
 
 def natural(acc):
@@ -95,20 +95,17 @@
     for cp in copies:
         cp.wait()
 
-    def first(t, carry):
-        rows = pl.multiple_of(t * 4 * BLK, 4 * BLK)
-        by_channel(dot(right[pl.ds(rows, 4 * BLK), :], lt_ref[...], NT), lhs, t)
-        return carry
-
-    lax.fori_loop(0, 4, first, 0)
+    for t in range(4):
+        by_channel(dot(right[t * 4 * BLK : (t + 1) * 4 * BLK, :], lt_ref[...], NT), lhs, t)
     w = off_ref[...]
     w_hi = w.astype(BF)
     rest = w - w_hi.astype(F32)
     w_mid = rest.astype(BF)
     w_lo = (rest - w_mid.astype(F32)).astype(BF)
     w3 = jnp.concatenate([w_hi, w_mid, w_lo], axis=0)
+    acc = dot(lhs[...], wblk[...], NN)
     for q in range(3):
-        update = natural(dot(lhs[q * COLS : (q + 1) * COLS, :], wblk[...], NN)) * (1.0 / MSA)
+        update = natural(acc[q * COLS : (q + 1) * COLS]) * (1.0 / MSA)
         for r in range(4):
             i = 4 * q + r
             mid = (emb_ref[i].astype(F32) + update[:, r * CH : (r + 1) * CH]).astype(BF)
@@ -294,18 +291,15 @@
     pp = lax.ppermute
     z = pp(own, "zl", ring(2, 1))
     up, down, far = [pp(own, "y", ring(4, k)) for k in (1, 3, 2)]
-    zup, zdown = pp(z, "y", ring(4, 1)), pp(z, "y", ring(4, 3))
-    zfar = pp(far, "zl", ring(2, 1))
+    zdown = pp(z, "y", ring(4, 3))
+    zup, zfar = pp(up, "zl", ring(2, 1)), pp(far, "zl", ring(2, 1))
     mine = [own, z, up, down, far, zup, zdown, zfar]
     return mine + [pp(m, "c", ring(2, 1)) for m in mine]
 
 
 def gather_bias_z(own):
-    return jnp.stack([own] + [lax.ppermute(own, "zh", ring(4, k)) for k in (1, 2, 3)])
-
-
-def gather_bias_near(col):
-    return lax.all_to_all(jnp.broadcast_to(col[None], (8,) + col.shape), ("zl", "y"), 0, 0, tiled=True)
+    col = jnp.stack([own] + [lax.ppermute(own, "zh", ring(4, k)) for k in (1, 2, 3)])
+    return jnp.broadcast_to(col[None], (8,) + col.shape)
 
 
 def body(stack, emb, entry, final, qkg, offset, out_proj, filt):
@@ -330,7 +324,7 @@
     col = gather_bias_z(pp(bias, ALL, SWAP))
     prev, nxt, far, col = lax.optimization_barrier((prev, nxt, far, col))
     q, gate, kv = project(norm, prev, nxt, far, qkg)
-    pay0 = gather_bias_near(col)
+    pay0 = lax.all_to_all(col, ("zl", "y"), 0, 0, tiled=True)
     q, gate, kv, pay0 = lax.optimization_barrier((q, gate, kv, pay0))
     pay1 = pp(pay0, "c", ring(2, 1))
     update = attend(pos, filt, q, gate, kv, pay0, pay1, out_proj)

time: 130 us -> 129 us (level)
  waiting for transfers between devices: 15.2 us -> 17.5 us
  starting transfers between devices: 61.9 us -> 60 us
  Pallas kernels: 39.7 us -> 37.9 us
    ppermute x1, starting transfers between devices: 3.49 us -> 0.01 us  [gather_right(): z = pp(own, 'zl', ring(2, 1))]
    ppermute x3, waiting for transfers between devices: 0.01 us -> 3.01 us  [gather_right(): up, down, far = [pp(own, 'y', ring(4, k)) for k in (1, 3, 2)]]
    ppermute x8, starting transfers between devices: 11.8 us -> 14.6 us  [gather_right(): return mine + [pp(m, 'c', ring(2, 1)) for m in mine]]
    ppermute x3, starting transfers between devices: 4.44 us -> 2.5 us  [the longest x1 2.5 us: gather_right(): zdown = pp(z, 'y', ring(4, 3))]
    ppermute x3, starting transfers between devices: 5.65 us -> 3.86 us  [body(): prev, nxt, far = [pp(norm, 'x', ring(4, k)) for k in (1, 3, 2)]]
    pallas_call x1, Pallas kernels: 11 us -> 9.21 us  [opm(): pl.pallas_call(opm_kernel, out_shape=(jax.ShapeDtypeStruct((ROWS, COLS, C...]
    all_to_all x1, starting transfers between devices: 3.55 us -> 4.88 us  [body(): pay0 = lax.all_to_all(col, ('zl', 'y'), 0, 0, tiled=True)]
where the time goes in v2:
time: 129 us; the launch traced here: 128 us
  starting transfers between devices  60 us (47%)
  Pallas kernels  37.9 us (29%)
  waiting for transfers between devices  17.5 us (14%)
  local copies, waits for them, and re-layouts  5.51 us (4%)
  other arithmetic  4.42 us (3%)
  matrix products  1.31 us (1%)
    pallas_call x1, Pallas kernels, attend(): pl.pallas_call(attend_kernel, grid=(ROWS,), out_shape=jax.ShapeDtypeStruc...  19.4 us
    ppermute x3, starting transfers between devices, gather_bias_z(): lax.ppermute(own, 'zh', ring(4, k))  17.1 us
    ppermute x8, starting transfers between devices, gather_right(): return mine + [pp(m, 'c', ring(2, 1)) for m in mine]  14.6 us
    pallas_call x1, Pallas kernels, project(): pl.pallas_call(project_kernel, grid=(ROWS,), out_shape=(jax.ShapeDtypeStr...  9.37 us
    pallas_call x1, Pallas kernels, opm(): pl.pallas_call(opm_kernel, out_shape=(jax.ShapeDtypeStruct((ROWS, COLS, C...  9.21 us
    ppermute x1, starting transfers between devices, body(): pp(right, ALL, SPREAD)  7.81 us
    ppermute x3, waiting for transfers between devices, body(): prev, nxt, far = [pp(norm, 'x', ring(4, k)) for k in (1, 3, 2)]  5.25 us
    all_to_all x1, starting transfers between devices, body(): pay0 = lax.all_to_all(col, ('zl', 'y'), 0, 0, tiled=True)  4.88 us
  transfers between devices with their start and end apart: 25, of which 11 were waited for; matrix products, arithmetic and copies ran while one was open for 2% of the time, Pallas kernels for 7%

profile of v2, /device:TPU:1, one launch (start us, length us, event | category | flops | bytes accessed | tf_op | source)
XLA Modules:
  0.0 127.6 jit_solution(4370047636799061936)
XLA Ops:
  0.7 2.0 %convert_reduce_fusion = f32[256,12]{0,1:T(8,128)S(1)} fusion(bf16[256,12,256]{2,0,1:T(8,128)(2,1)} %param.8), kind=kLoop, calls=%fused_computation.1 | loop fusion | flops 1569792 | bytes 1585152 | tf_op jit(solution)/shard_map/reduce_sum | solution.py:273
  2.7 2.4 %fusion.2 = f32[256,12]{0,1:T(8,128)S(1)} fusion(bf16[256,12,256]{2,0,1:T(8,128)(2,1)} %param.8, f32[256,12]{0,1:T(8,128)S(1)} %broadcast_multiply_fusion), kind=kLoop, calls=%fused_computation.4 | loop fusion | flops 3142656 | bytes 1597440 | tf_op jit(solution)/shard_map/reduce_sum | solution.py:274
  5.1 1.3 %fusion.11 = bf16[12,64,256]{2,1,0:T(8,128)(2,1)S(1)} fusion(bf16[256,12,256]{2,0,1:T(8,128)(2,1)S(1)} %copy-done.1, f32[256,12]{0,1:T(8,128)S(1)} %add_rsqrt_fusion, f32[256,12]{0,1:T(8,128)S(1)} %broadcast_multiply_fusion, bf16[256,64]{0,1:T(8,128)(2,1)S(1)} %copy-done), kind=kOutput, calls=%fused_computation.10 | convolution fusion | flops 104005632 | bytes 2023424 | tf_op jit(solution)/shard_map/sjc,cx->jxs/dot_general | solution.py:310
  7.4 7.8 %collective-permute-start = (bf16[384,256]{1,0:T(8,128)(2,1)S(1)}, bf16[384,256]{1,0:T(8,128)(2,1)S(1)}, u32[]{:S(2)}, u32[]{:S(2)}) collective-permute-start(bf16[384,256]{1,0:T(8,128)(2,1)S(1)} %pad_maximum_fusion), channel_id=1, source_target_pairs={{2,0},{1,64},{0,128},{3,192},{6,4},{5,68},{4,132},{7,196},{10,8},{... | collective-permute-start | bytes 589832 | tf_op jit(solution)/shard_map/ppermute | solution.py:320
  15.2 0.8 copy.17
  17.2 1.6 %collective-permute-done.refs_0_ = bf16[384,256]{1,0:T(8,128)(2,1)S(1)} collective-permute-done((bf16[384,256]{1,0:T(8,128)(2,1)S(1)}, bf16[384,256]{1,0:T(8,128)(2,1)S(1)}, u32[]{:S(2)}, u32[]{:S(2)}) %collective-permute-start) | collective-permute-done | bytes 196640 | tf_op jit(solution)/shard_map/ppermute | solution.py:320
  18.7 2.9 %collective-permute-start.4 = (bf16[384,256]{1,0:T(8,128)(2,1)S(1)}, bf16[384,256]{1,0:T(8,128)(2,1)S(1)}, u32[]{:S(2)}, u32[]{:S(2)}) collective-permute-start(bf16[384,256]{1,0:T(8,128)(2,1)S(1)} %collective-permute-done.refs_0_), channel_id=1, source_target_pairs={{0,16},{8,24},{16,0},{24,8},{1,17},{9,25},{17,1},{25,9},{2,18},{10... | collective-permute-start | bytes 589832 | tf_op jit(solution)/shard_map/ppermute | solution.py:293
  21.7 5.9 %collective-permute-start.8 = (bf16[384,256]{1,0:T(8,128)(2,1)S(1)}, bf16[384,256]{1,0:T(8,128)(2,1)S(1)}, u32[]{:S(2)}, u32[]{:S(2)}) collective-permute-start(bf16[384,256]{1,0:T(8,128)(2,1)S(1)} %collective-permute-done.refs_0_), channel_id=1, source_target_pairs={{0,4},{4,0},{1,5},{5,1},{2,6},{6,2},{3,7},{7,3},{8,12},{12,8},{9,1... | collective-permute-start | bytes 589832 | tf_op jit(solution)/shard_map/ppermute | solution.py:297
  27.6 0.8 collective-permute-start.3
  29.1 2.6 %collective-permute-start.12 = (bf16[384,256]{1,0:T(8,128)(2,1)S(1)}, bf16[384,256]{1,0:T(8,128)(2,1)S(1)}, u32[]{:S(2)}, u32[]{:S(2)}) collective-permute-start(bf16[384,256]{1,0:T(8,128)(2,1)S(1)} %collective-permute-done.4.refs_4_), channel_id=1, source_target_pairs={{0,4},{4,0},{1,5},{5,1},{2,6},{6,2},{3,7},{7,3},{8,12},{12,8},{9,1... | collective-permute-start | bytes 589832 | tf_op jit(solution)/shard_map/ppermute | solution.py:297
  31.7 3.0 %collective-permute-done.3.refs_3_ = bf16[384,256]{1,0:T(8,128)(2,1)S(1)} collective-permute-done((bf16[384,256]{1,0:T(8,128)(2,1)S(1)}, bf16[384,256]{1,0:T(8,128)(2,1)S(1)}, u32[]{:S(2)}, u32[]{:S(2)}) %collective-permute-start.3) | collective-permute-done | bytes 196640 | tf_op jit(solution)/shard_map/ppermute | solution.py:293
  34.7 1.5 %collective-permute-start.11 = (bf16[384,256]{1,0:T(8,128)(2,1)S(1)}, bf16[384,256]{1,0:T(8,128)(2,1)S(1)}, u32[]{:S(2)}, u32[]{:S(2)}) collective-permute-start(bf16[384,256]{1,0:T(8,128)(2,1)S(1)} %collective-permute-done.3.refs_3_), channel_id=1, source_target_pairs={{0,4},{4,0},{1,5},{5,1},{2,6},{6,2},{3,7},{7,3},{8,12},{12,8},{9,1... | collective-permute-start | bytes 589832 | tf_op jit(solution)/shard_map/ppermute | solution.py:297
  36.2 2.5 %collective-permute-start.6 = (bf16[384,256]{1,0:T(8,128)(2,1)S(1)}, bf16[384,256]{1,0:T(8,128)(2,1)S(1)}, u32[]{:S(2)}, u32[]{:S(2)}) collective-permute-start(bf16[384,256]{1,0:T(8,128)(2,1)S(1)} %collective-permute-done.1.refs_1_), channel_id=1, source_target_pairs={{0,24},{8,0},{16,8},{24,16},{1,25},{9,1},{17,9},{25,17},{2,26},{10... | collective-permute-start | bytes 589832 | tf_op jit(solution)/shard_map/ppermute | solution.py:294
  39.2 2.4 %collective-permute-start.9 = (bf16[384,256]{1,0:T(8,128)(2,1)S(1)}, bf16[384,256]{1,0:T(8,128)(2,1)S(1)}, u32[]{:S(2)}, u32[]{:S(2)}) collective-permute-start(bf16[384,256]{1,0:T(8,128)(2,1)S(1)} %collective-permute-done.1.refs_1_), channel_id=1, source_target_pairs={{0,4},{4,0},{1,5},{5,1},{2,6},{6,2},{3,7},{7,3},{8,12},{12,8},{9,1... | collective-permute-start | bytes 589832 | tf_op jit(solution)/shard_map/ppermute | solution.py:297
  41.7 1.7 %collective-permute-done.5.refs_5_ = bf16[384,256]{1,0:T(8,128)(2,1)S(1)} collective-permute-done((bf16[384,256]{1,0:T(8,128)(2,1)S(1)}, bf16[384,256]{1,0:T(8,128)(2,1)S(1)}, u32[]{:S(2)}, u32[]{:S(2)}) %collective-permute-start.5) | collective-permute-done | bytes 196640 | tf_op jit(solution)/shard_map/ppermute | solution.py:295
  43.4 1.4 %collective-permute-start.13 = (bf16[384,256]{1,0:T(8,128)(2,1)S(1)}, bf16[384,256]{1,0:T(8,128)(2,1)S(1)}, u32[]{:S(2)}, u32[]{:S(2)}) collective-permute-start(bf16[384,256]{1,0:T(8,128)(2,1)S(1)} %collective-permute-done.5.refs_5_), channel_id=1, source_target_pairs={{0,4},{4,0},{1,5},{5,1},{2,6},{6,2},{3,7},{7,3},{8,12},{12,8},{9,1... | collective-permute-start | bytes 589832 | tf_op jit(solution)/shard_map/ppermute | solution.py:297
  45.1 0.7 collective-permute-done.13.refs_13_
  46.9 9.2 %opm.1 = (bf16[12,192,128]{2,1,0:T(8,128)(2,1)}, bf16[12,192,128]{2,1,0:T(8,128)(2,1)}, bf16[48,256]{1,0:T(8,128)(2,1)}) custom-call(s32[6]{0:T(128)} %stack.42.pos_ref, bf16[384,256]{1,0:T(8,128)(2,1)} %bitcast.29, bf16[384,256]{1,0:T(8,128)(2,1)} %copy-done.9, bf16[384,256]{1,0:T(8,128)(2,1)} %copy-done.14, bf16[384,256]{1,0:T(8,128)(2,1)} %copy-done.13, ...), custom_call_target="tpu_custom_call" | custom-call | flops 6000000000 | bytes 10000000 | tf_op jit(solution)/shard_map/opm/pallas_call | solution.py:141
  56.3 3.3 %collective-permute-start.17 = (bf16[12,192,128]{2,1,0:T(8,128)(2,1)}, bf16[12,192,128]{2,1,0:T(8,128)(2,1)S(1)}, u32[]{:S(2)}, u32[]{:S(2)}) collective-permute-start(bf16[12,192,128]{2,1,0:T(8,128)(2,1)} %get-tuple-element.25.own_ref), channel_id=1, source_target_pairs={{0,3},{1,0},{2,1},{3,2},{4,7},{5,4},{6,5},{7,6},{8,11},{9,8},{10,9... | collective-permute-start | bytes 1769480 | tf_op jit(solution)/shard_map/ppermute | solution.py:323
  60.0 1.4 %collective-permute-start.19 = (bf16[48,256]{1,0:T(8,128)(2,1)}, bf16[48,256]{1,0:T(8,128)(2,1)S(1)}, u32[]{:S(2)}, u32[]{:S(2)}) collective-permute-start(bf16[48,256]{1,0:T(8,128)(2,1)} %get-tuple-element.26), channel_id=1, source_target_pairs={{0,0},{1,64},{2,128},{3,192},{4,4},{5,68},{6,132},{7,196},{8,8},{9... | collective-permute-start | bytes 73736 | tf_op jit(solution)/shard_map/ppermute | solution.py:324
  61.4 13.0 %collective-permute-start.22 = (bf16[48,256]{1,0:T(8,128)(2,1)S(1)}, bf16[48,256]{1,0:T(8,128)(2,1)S(1)}, u32[]{:S(2)}, u32[]{:S(2)}) collective-permute-start(bf16[48,256]{1,0:T(8,128)(2,1)S(1)} %collective-permute-done.19), channel_id=1, source_target_pairs={{0,192},{64,0},{128,64},{192,128},{1,193},{65,1},{129,65},{193,129... | collective-permute-start | bytes 73736 | tf_op jit(solution)/shard_map/ppermute | solution.py:301
  74.4 1.8 %collective-permute-start.21 = (bf16[48,256]{1,0:T(8,128)(2,1)S(1)}, bf16[48,256]{1,0:T(8,128)(2,1)S(1)}, u32[]{:S(2)}, u32[]{:S(2)}) collective-permute-start(bf16[48,256]{1,0:T(8,128)(2,1)S(1)} %collective-permute-done.19), channel_id=1, source_target_pairs={{0,128},{64,192},{128,0},{192,64},{1,129},{65,193},{129,1},{193,65... | collective-permute-start | bytes 73736 | tf_op jit(solution)/shard_map/ppermute | solution.py:301
  76.2 2.4 %collective-permute-start.20 = (bf16[48,256]{1,0:T(8,128)(2,1)S(1)}, bf16[48,256]{1,0:T(8,128)(2,1)S(1)}, u32[]{:S(2)}, u32[]{:S(2)}) collective-permute-start(bf16[48,256]{1,0:T(8,128)(2,1)S(1)} %collective-permute-done.19), channel_id=1, source_target_pairs={{0,64},{64,128},{128,192},{192,0},{1,65},{65,129},{129,193},{193,1... | collective-permute-start | bytes 73736 | tf_op jit(solution)/shard_map/ppermute | solution.py:301
  78.6 2.4 %collective-permute-done.21 = bf16[48,256]{1,0:T(8,128)(2,1)S(1)} collective-permute-done((bf16[48,256]{1,0:T(8,128)(2,1)S(1)}, bf16[48,256]{1,0:T(8,128)(2,1)S(1)}, u32[]{:S(2)}, u32[]{:S(2)}) %collective-permute-start.21) | collective-permute-done | bytes 24608 | tf_op jit(solution)/shard_map/ppermute | solution.py:301
  81.3 5.2 %collective-permute-done.17.next_ref = bf16[12,192,128]{2,1,0:T(8,128)(2,1)S(1)} collective-permute-done((bf16[12,192,128]{2,1,0:T(8,128)(2,1)}, bf16[12,192,128]{2,1,0:T(8,128)(2,1)S(1)}, u32[]{:S(2)}, u32[]{:S(2)}) %collective-permute-start.17) | collective-permute-done | bytes 589856 | tf_op jit(solution)/shard_map/ppermute | solution.py:323
  86.5 1.0 broadcast_in_dim.2
  87.6 4.9 %all-to-all-start = ((bf16[8,4,48,256]{3,2,1,0:T(8,128)(2,1)}), bf16[8,4,48,256]{3,2,1,0:T(8,128)(2,1)S(1)}, u32[]{:S(2)}, u32[]{:S(2)}) async-start(bf16[8,4,48,256]{3,2,1,0:T(8,128)(2,1)} %broadcast_in_dim.2), calls=%async_computation | async-start | bytes 1572864 | tf_op jit(solution)/shard_map/all_to_all | solution.py:327
  92.5 9.4 %project.1 = (bf16[12,192,128]{2,1,0:T(8,128)(2,1)}, f32[12,192,128]{2,1,0:T(8,128)}, bf16[12,768,256]{2,1,0:T(8,128)(2,1)}) custom-call(bf16[12,192,128]{2,1,0:T(8,128)(2,1)} %get-tuple-element.25.own_ref, bf16[12,192,128]{2,1,0:T(8,128)(2,1)} %copy-done.8, bf16[12,192,128]{2,1,0:T(8,128)(2,1)} %copy-done.7, bf16[12,192,128]{2,1,0:T(8,128)(2,1)} %copy-done.6, ...), custom_call_target="tpu_custom_call" | custom-call | flops 10000000000 | bytes 20000000 | tf_op jit(solution)/shard_map/project/pallas_call | solution.py:174
  102.0 3.4 %collective-permute-start.23 = (bf16[8,4,48,256]{3,2,1,0:T(8,128)(2,1)S(1)}, bf16[8,4,48,256]{3,2,1,0:T(8,128)(2,1)S(1)}, u32[]{:S(2)}, u32[]{:S(2)}) collective-permute-start(bf16[8,4,48,256]{3,2,1,0:T(8,128)(2,1)S(1)} %all-to-all-done.pay0_ref), channel_id=1, source_target_pairs={{0,4},{4,0},{1,5},{5,1},{2,6},{6,2},{3,7},{7,3},{8,12},{12,8},{9,1... | collective-permute-start | bytes 2359304 | tf_op jit(solution)/shard_map/ppermute | solution.py:329
  105.4 1.9 %collective-permute-done.23.pay1_ref = bf16[8,4,48,256]{3,2,1,0:T(8,128)(2,1)S(1)} collective-permute-done((bf16[8,4,48,256]{3,2,1,0:T(8,128)(2,1)S(1)}, bf16[8,4,48,256]{3,2,1,0:T(8,128)(2,1)S(1)}, u32[]{:S(2)}, u32[]{:S(2)}) %collective-permute-start.23) | collective-permute-done | bytes 786464 | tf_op jit(solution)/shard_map/ppermute | solution.py:329
  107.3 1.0 copy-done.5
  108.3 19.4 %attend.1 = bf16[12,192,128]{2,1,0:T(8,128)(2,1)} custom-call(s32[6]{0:T(128)} %stack.42.pos_ref, s32[6,6]{1,0:T(8,128)} %filt_ref.1, bf16[12,192,128]{2,1,0:T(8,128)(2,1)} %get-tuple-element.34.q_ref, f32[12,192,128]{2,1,0:T(8,128)} %get-tuple-element.35.gate_ref, bf16[12,768,256]{2,1,0:T(8,128)(2,1)} %get-tuple-element.36.kv_ref, ...), custom_call_target="tpu_custom_call" | custom-call | flops 8000000000 | bytes 10000000 | tf_op jit(solution)/shard_map/attend/pallas_call | solution.py:258
  (88 shorter events, 5.7 us)
Async XLA Ops:
  2.7 12.5 %copy-start.3 = (bf16[1024,128]{1,0:T(8,128)(2,1)S(1)}, bf16[1024,128]{1,0:T(8,128)(2,1)}, u32[]{:S(2)}) copy-start(bf16[1024,128]{1,0:T(8,128)(2,1)} %param.11) | copy-start | bytes 786436
  5.1 10.9 %copy-start.4 = (f32[128,4]{0,1:T(4,128)S(1)}, f32[128,4]{0,1:T(4,128)}, u32[]{:S(2)}) copy-start(f32[128,4]{0,1:T(4,128)} %param.13) | copy-start | bytes 6148
  7.4 11.4 %collective-permute-start = (bf16[384,256]{1,0:T(8,128)(2,1)S(1)}, bf16[384,256]{1,0:T(8,128)(2,1)S(1)}, u32[]{:S(2)}, u32[]{:S(2)}) collective-permute-start(bf16[384,256]{1,0:T(8,128)(2,1)S(1)} %pad_maximum_fusion), channel_id=1, source_target_pairs={{2,0},{1,64},{0,128},{3,192},{6,4},{5,68},{4,132},{7,196},{10,8},{... | collective-permute-start | bytes 589832 | tf_op jit(solution)/shard_map/ppermute | solution.py:320
  18.7 27.5 %copy-start.9 = (bf16[384,256]{1,0:T(8,128)(2,1)}, bf16[384,256]{1,0:T(8,128)(2,1)S(1)}, u32[]{:S(2)}) copy-start(bf16[384,256]{1,0:T(8,128)(2,1)S(1)} %collective-permute-done.refs_0_) | copy-start | bytes 589828
  18.7 10.3 %collective-permute-start.4 = (bf16[384,256]{1,0:T(8,128)(2,1)S(1)}, bf16[384,256]{1,0:T(8,128)(2,1)S(1)}, u32[]{:S(2)}, u32[]{:S(2)}) collective-permute-start(bf16[384,256]{1,0:T(8,128)(2,1)S(1)} %collective-permute-done.refs_0_), channel_id=1, source_target_pairs={{0,16},{8,24},{16,0},{24,8},{1,17},{9,25},{17,1},{25,9},{2,18},{10... | collective-permute-start | bytes 589832 | tf_op jit(solution)/shard_map/ppermute | solution.py:293
  21.7 10.0 %collective-permute-start.8 = (bf16[384,256]{1,0:T(8,128)(2,1)S(1)}, bf16[384,256]{1,0:T(8,128)(2,1)S(1)}, u32[]{:S(2)}, u32[]{:S(2)}) collective-permute-start(bf16[384,256]{1,0:T(8,128)(2,1)S(1)} %collective-permute-done.refs_0_), channel_id=1, source_target_pairs={{0,4},{4,0},{1,5},{5,1},{2,6},{6,2},{3,7},{7,3},{8,12},{12,8},{9,1... | collective-permute-start | bytes 589832 | tf_op jit(solution)/shard_map/ppermute | solution.py:297
  27.6 7.1 %collective-permute-start.3 = (bf16[384,256]{1,0:T(8,128)(2,1)S(1)}, bf16[384,256]{1,0:T(8,128)(2,1)S(1)}, u32[]{:S(2)}, u32[]{:S(2)}) collective-permute-start(bf16[384,256]{1,0:T(8,128)(2,1)S(1)} %collective-permute-done.refs_0_), channel_id=1, source_target_pairs={{0,24},{8,0},{16,8},{24,16},{1,25},{9,1},{17,9},{25,17},{2,26},{10... | collective-permute-start | bytes 589832 | tf_op jit(solution)/shard_map/ppermute | solution.py:293
  28.4 7.8 %collective-permute-start.2 = (bf16[384,256]{1,0:T(8,128)(2,1)S(1)}, bf16[384,256]{1,0:T(8,128)(2,1)S(1)}, u32[]{:S(2)}, u32[]{:S(2)}) collective-permute-start(bf16[384,256]{1,0:T(8,128)(2,1)S(1)} %collective-permute-done.refs_0_), channel_id=1, source_target_pairs={{0,8},{8,16},{16,24},{24,0},{1,9},{9,17},{17,25},{25,1},{2,10},{10... | collective-permute-start | bytes 589832 | tf_op jit(solution)/shard_map/ppermute | solution.py:293
  29.1 7.1 %collective-permute-start.1 = (bf16[384,256]{1,0:T(8,128)(2,1)S(1)}, bf16[384,256]{1,0:T(8,128)(2,1)S(1)}, u32[]{:S(2)}, u32[]{:S(2)}) collective-permute-start(bf16[384,256]{1,0:T(8,128)(2,1)S(1)} %collective-permute-done.refs_0_), channel_id=1, source_target_pairs={{0,32},{32,0},{1,33},{33,1},{2,34},{34,2},{3,35},{35,3},{4,36},{36... | collective-permute-start | bytes 589832 | tf_op jit(solution)/shard_map/ppermute | solution.py:292
  29.1 17.2 %copy-start.10 = (bf16[384,256]{1,0:T(8,128)(2,1)}, bf16[384,256]{1,0:T(8,128)(2,1)S(1)}, u32[]{:S(2)}) copy-start(bf16[384,256]{1,0:T(8,128)(2,1)S(1)} %collective-permute-done.4.refs_4_) | copy-start | bytes 589828
  29.1 9.6 %collective-permute-start.12 = (bf16[384,256]{1,0:T(8,128)(2,1)S(1)}, bf16[384,256]{1,0:T(8,128)(2,1)S(1)}, u32[]{:S(2)}, u32[]{:S(2)}) collective-permute-start(bf16[384,256]{1,0:T(8,128)(2,1)S(1)} %collective-permute-done.4.refs_4_), channel_id=1, source_target_pairs={{0,4},{4,0},{1,5},{5,1},{2,6},{6,2},{3,7},{7,3},{8,12},{12,8},{9,1... | collective-permute-start | bytes 589832 | tf_op jit(solution)/shard_map/ppermute | solution.py:297
  31.7 14.6 %copy-start.11 = (bf16[384,256]{1,0:T(8,128)(2,1)}, bf16[384,256]{1,0:T(8,128)(2,1)S(1)}, u32[]{:S(2)}) copy-start(bf16[384,256]{1,0:T(8,128)(2,1)S(1)} %collective-permute-done.8.refs_8_) | copy-start | bytes 589828
  31.7 7.5 %collective-permute-start.7 = (bf16[384,256]{1,0:T(8,128)(2,1)S(1)}, bf16[384,256]{1,0:T(8,128)(2,1)S(1)}, u32[]{:S(2)}, u32[]{:S(2)}) collective-permute-start(bf16[384,256]{1,0:T(8,128)(2,1)S(1)} %collective-permute-done.4.refs_4_), channel_id=1, source_target_pairs={{0,32},{32,0},{1,33},{33,1},{2,34},{34,2},{3,35},{35,3},{4,36},{36... | collective-permute-start | bytes 589832 | tf_op jit(solution)/shard_map/ppermute | solution.py:295
  34.7 11.6 %copy-start.12 = (bf16[384,256]{1,0:T(8,128)(2,1)}, bf16[384,256]{1,0:T(8,128)(2,1)S(1)}, u32[]{:S(2)}) copy-start(bf16[384,256]{1,0:T(8,128)(2,1)S(1)} %collective-permute-done.3.refs_3_) | copy-start | bytes 589828
  34.7 6.9 %collective-permute-start.11 = (bf16[384,256]{1,0:T(8,128)(2,1)S(1)}, bf16[384,256]{1,0:T(8,128)(2,1)S(1)}, u32[]{:S(2)}, u32[]{:S(2)}) collective-permute-start(bf16[384,256]{1,0:T(8,128)(2,1)S(1)} %collective-permute-done.3.refs_3_), channel_id=1, source_target_pairs={{0,4},{4,0},{1,5},{5,1},{2,6},{6,2},{3,7},{7,3},{8,12},{12,8},{9,1... | collective-permute-start | bytes 589832 | tf_op jit(solution)/shard_map/ppermute | solution.py:297
  36.1 7.2 %collective-permute-start.5 = (bf16[384,256]{1,0:T(8,128)(2,1)S(1)}, bf16[384,256]{1,0:T(8,128)(2,1)S(1)}, u32[]{:S(2)}, u32[]{:S(2)}) collective-permute-start(bf16[384,256]{1,0:T(8,128)(2,1)S(1)} %collective-permute-done.2.refs_2_), channel_id=1, source_target_pairs={{0,32},{32,0},{1,33},{33,1},{2,34},{34,2},{3,35},{35,3},{4,36},{36... | collective-permute-start | bytes 589832 | tf_op jit(solution)/shard_map/ppermute | solution.py:295
  36.2 8.6 %collective-permute-start.6 = (bf16[384,256]{1,0:T(8,128)(2,1)S(1)}, bf16[384,256]{1,0:T(8,128)(2,1)S(1)}, u32[]{:S(2)}, u32[]{:S(2)}) collective-permute-start(bf16[384,256]{1,0:T(8,128)(2,1)S(1)} %collective-permute-done.1.refs_1_), channel_id=1, source_target_pairs={{0,24},{8,0},{16,8},{24,16},{1,25},{9,1},{17,9},{25,17},{2,26},{10... | collective-permute-start | bytes 589832 | tf_op jit(solution)/shard_map/ppermute | solution.py:294
  38.7 6.4 %collective-permute-start.10 = (bf16[384,256]{1,0:T(8,128)(2,1)S(1)}, bf16[384,256]{1,0:T(8,128)(2,1)S(1)}, u32[]{:S(2)}, u32[]{:S(2)}) collective-permute-start(bf16[384,256]{1,0:T(8,128)(2,1)S(1)} %collective-permute-done.2.refs_2_), channel_id=1, source_target_pairs={{0,4},{4,0},{1,5},{5,1},{2,6},{6,2},{3,7},{7,3},{8,12},{12,8},{9,1... | collective-permute-start | bytes 589832 | tf_op jit(solution)/shard_map/ppermute | solution.py:297
  39.2 5.9 %collective-permute-start.9 = (bf16[384,256]{1,0:T(8,128)(2,1)S(1)}, bf16[384,256]{1,0:T(8,128)(2,1)S(1)}, u32[]{:S(2)}, u32[]{:S(2)}) collective-permute-start(bf16[384,256]{1,0:T(8,128)(2,1)S(1)} %collective-permute-done.1.refs_1_), channel_id=1, source_target_pairs={{0,4},{4,0},{1,5},{5,1},{2,6},{6,2},{3,7},{7,3},{8,12},{12,8},{9,1... | collective-permute-start | bytes 589832 | tf_op jit(solution)/shard_map/ppermute | solution.py:297
  41.6 3.5 %collective-permute-start.15 = (bf16[384,256]{1,0:T(8,128)(2,1)S(1)}, bf16[384,256]{1,0:T(8,128)(2,1)S(1)}, u32[]{:S(2)}, u32[]{:S(2)}) collective-permute-start(bf16[384,256]{1,0:T(8,128)(2,1)S(1)} %collective-permute-done.7.refs_7_), channel_id=1, source_target_pairs={{0,4},{4,0},{1,5},{5,1},{2,6},{6,2},{3,7},{7,3},{8,12},{12,8},{9,1... | collective-permute-start | bytes 589832 | tf_op jit(solution)/shard_map/ppermute | solution.py:297
  43.4 2.5 %collective-permute-start.13 = (bf16[384,256]{1,0:T(8,128)(2,1)S(1)}, bf16[384,256]{1,0:T(8,128)(2,1)S(1)}, u32[]{:S(2)}, u32[]{:S(2)}) collective-permute-start(bf16[384,256]{1,0:T(8,128)(2,1)S(1)} %collective-permute-done.5.refs_5_), channel_id=1, source_target_pairs={{0,4},{4,0},{1,5},{5,1},{2,6},{6,2},{3,7},{7,3},{8,12},{12,8},{9,1... | collective-permute-start | bytes 589832 | tf_op jit(solution)/shard_map/ppermute | solution.py:297
  44.8 1.4 %collective-permute-start.14 = (bf16[384,256]{1,0:T(8,128)(2,1)S(1)}, bf16[384,256]{1,0:T(8,128)(2,1)S(1)}, u32[]{:S(2)}, u32[]{:S(2)}) collective-permute-start(bf16[384,256]{1,0:T(8,128)(2,1)S(1)} %collective-permute-done.6.refs_6_), channel_id=1, source_target_pairs={{0,4},{4,0},{1,5},{5,1},{2,6},{6,2},{3,7},{7,3},{8,12},{12,8},{9,1... | collective-permute-start | bytes 589832 | tf_op jit(solution)/shard_map/ppermute | solution.py:297
  56.2 25.1 %collective-permute-start.18 = (bf16[12,192,128]{2,1,0:T(8,128)(2,1)}, bf16[12,192,128]{2,1,0:T(8,128)(2,1)S(1)}, u32[]{:S(2)}, u32[]{:S(2)}) collective-permute-start(bf16[12,192,128]{2,1,0:T(8,128)(2,1)} %get-tuple-element.25.own_ref), channel_id=1, source_target_pairs={{0,2},{1,3},{2,0},{3,1},{4,6},{5,7},{6,4},{7,5},{8,10},{9,11},{10,... | collective-permute-start | bytes 1769480 | tf_op jit(solution)/shard_map/ppermute | solution.py:323
  56.3 30.3 %collective-permute-start.17 = (bf16[12,192,128]{2,1,0:T(8,128)(2,1)}, bf16[12,192,128]{2,1,0:T(8,128)(2,1)S(1)}, u32[]{:S(2)}, u32[]{:S(2)}) collective-permute-start(bf16[12,192,128]{2,1,0:T(8,128)(2,1)} %get-tuple-element.25.own_ref), channel_id=1, source_target_pairs={{0,3},{1,0},{2,1},{3,2},{4,7},{5,4},{6,5},{7,6},{8,11},{9,8},{10,9... | collective-permute-start | bytes 1769480 | tf_op jit(solution)/shard_map/ppermute | solution.py:323
  59.5 27.0 %collective-permute-start.16 = (bf16[12,192,128]{2,1,0:T(8,128)(2,1)}, bf16[12,192,128]{2,1,0:T(8,128)(2,1)S(1)}, u32[]{:S(2)}, u32[]{:S(2)}) collective-permute-start(bf16[12,192,128]{2,1,0:T(8,128)(2,1)} %get-tuple-element.25.own_ref), channel_id=1, source_target_pairs={{0,1},{1,2},{2,3},{3,0},{4,5},{5,6},{6,7},{7,4},{8,9},{9,10},{10,1... | collective-permute-start | bytes 1769480 | tf_op jit(solution)/shard_map/ppermute | solution.py:323
  60.0 1.4 %collective-permute-start.19 = (bf16[48,256]{1,0:T(8,128)(2,1)}, bf16[48,256]{1,0:T(8,128)(2,1)S(1)}, u32[]{:S(2)}, u32[]{:S(2)}) collective-permute-start(bf16[48,256]{1,0:T(8,128)(2,1)} %get-tuple-element.26), channel_id=1, source_target_pairs={{0,0},{1,64},{2,128},{3,192},{4,4},{5,68},{6,132},{7,196},{8,8},{9... | collective-permute-start | bytes 73736 | tf_op jit(solution)/shard_map/ppermute | solution.py:324
  61.4 14.8 %collective-permute-start.22 = (bf16[48,256]{1,0:T(8,128)(2,1)S(1)}, bf16[48,256]{1,0:T(8,128)(2,1)S(1)}, u32[]{:S(2)}, u32[]{:S(2)}) collective-permute-start(bf16[48,256]{1,0:T(8,128)(2,1)S(1)} %collective-permute-done.19), channel_id=1, source_target_pairs={{0,192},{64,0},{128,64},{192,128},{1,193},{65,1},{129,65},{193,129... | collective-permute-start | bytes 73736 | tf_op jit(solution)/shard_map/ppermute | solution.py:301
  74.4 6.6 %collective-permute-start.21 = (bf16[48,256]{1,0:T(8,128)(2,1)S(1)}, bf16[48,256]{1,0:T(8,128)(2,1)S(1)}, u32[]{:S(2)}, u32[]{:S(2)}) collective-permute-start(bf16[48,256]{1,0:T(8,128)(2,1)S(1)} %collective-permute-done.19), channel_id=1, source_target_pairs={{0,128},{64,192},{128,0},{192,64},{1,129},{65,193},{129,1},{193,65... | collective-permute-start | bytes 73736 | tf_op jit(solution)/shard_map/ppermute | solution.py:301
  76.2 5.0 %collective-permute-start.20 = (bf16[48,256]{1,0:T(8,128)(2,1)S(1)}, bf16[48,256]{1,0:T(8,128)(2,1)S(1)}, u32[]{:S(2)}, u32[]{:S(2)}) collective-permute-start(bf16[48,256]{1,0:T(8,128)(2,1)S(1)} %collective-permute-done.19), channel_id=1, source_target_pairs={{0,64},{64,128},{128,192},{192,0},{1,65},{65,129},{129,193},{193,1... | collective-permute-start | bytes 73736 | tf_op jit(solution)/shard_map/ppermute | solution.py:301
  81.3 11.2 %copy-start.6 = (bf16[12,192,128]{2,1,0:T(8,128)(2,1)}, bf16[12,192,128]{2,1,0:T(8,128)(2,1)S(1)}, u32[]{:S(2)}) copy-start(bf16[12,192,128]{2,1,0:T(8,128)(2,1)S(1)} %collective-permute-done.18.far_ref) | copy-start | bytes 1769476
  87.6 14.4 %all-to-all-start = ((bf16[8,4,48,256]{3,2,1,0:T(8,128)(2,1)}), bf16[8,4,48,256]{3,2,1,0:T(8,128)(2,1)S(1)}, u32[]{:S(2)}, u32[]{:S(2)}) async-start(bf16[8,4,48,256]{3,2,1,0:T(8,128)(2,1)} %broadcast_in_dim.2), calls=%async_computation | async-start | bytes 1572864 | tf_op jit(solution)/shard_map/all_to_all | solution.py:327
  102.0 5.3 %collective-permute-start.23 = (bf16[8,4,48,256]{3,2,1,0:T(8,128)(2,1)S(1)}, bf16[8,4,48,256]{3,2,1,0:T(8,128)(2,1)S(1)}, u32[]{:S(2)}, u32[]{:S(2)}) collective-permute-start(bf16[8,4,48,256]{3,2,1,0:T(8,128)(2,1)S(1)} %all-to-all-done.pay0_ref), channel_id=1, source_target_pairs={{0,4},{4,0},{1,5},{5,1},{2,6},{6,2},{3,7},{7,3},{8,12},{12,8},{9,1... | collective-permute-start | bytes 2359304 | tf_op jit(solution)/shard_map/ppermute | solution.py:329
  (18 other events, 76.4 us)

commit v3 on v2

--- a/solution.py
+++ b/solution.py
@@ -11,7 +11,7 @@
 NN = (((1,), (0,)), ((), ()))
 
 ROWS, COLS, CH, HEADS, HD = 12, 192, 128, 4, 32
-MSA, PF = 256, 32
+MSA, MSA_CH, PF = 256, 256, 32
 BLK = ROWS * PF
 LANES = 128
 HALF = COLS - LANES
@@ -26,6 +26,45 @@
 
 def dot(a, b, dims):
     return lax.dot_general(a, b, dims, preferred_element_type=F32)
+
+
+VMEM = pl.BlockSpec(memory_space=pltpu.VMEM)
+SMEM = pl.BlockSpec(memory_space=pltpu.SMEM)
+ANY = pl.BlockSpec(memory_space=pl.ANY)
+PARAMS = pltpu.CompilerParams(vmem_limit_bytes=56 * 1024 * 1024)
+
+
+def msa_kernel(x_ref, w_ref, left_ref, right_ref, near, tail):
+    w = w_ref[...]
+    ones = jnp.ones((MSA_CH, LANES), BF)
+    for j in range(ROWS):
+        mean = dot(x_ref[j], ones, NN) * (1.0 / MSA_CH)
+        cen = x_ref[j].astype(F32) - jnp.concatenate([mean, mean], axis=1)
+        var = jnp.mean(cen * cen, axis=-1, keepdims=True)
+        nrm = (cen * lax.rsqrt(var + 1e-05)).astype(BF)
+        proj = dot(w, nrm, NT)
+        left_ref[j * PF : (j + 1) * PF, :] = proj[:PF].astype(BF)
+        if j < 8:
+            near[:, j, :] = proj[PF:]
+        else:
+            tail[:, j - 8, :] = proj[PF:]
+    right_ref[: 8 * PF, :] = near[...].reshape(8 * PF, MSA).astype(BF)
+    t = tail[...].reshape(PF // 2, 2, 8, MSA)
+    both = jnp.concatenate([t[:, 0, :4], t[:, 1, :4]], axis=1)
+    right_ref[8 * PF :, :] = both.reshape(4 * PF, MSA).astype(BF)
+
+
+def msa_project(x, w):
+    return pl.pallas_call(
+        msa_kernel,
+        out_shape=(jax.ShapeDtypeStruct((BLK, MSA), BF), jax.ShapeDtypeStruct((BLK, MSA), BF)),
+        in_specs=[VMEM, VMEM],
+        out_specs=[VMEM, VMEM],
+        scratch_shapes=[pltpu.VMEM((PF, 8, MSA), F32), pltpu.VMEM((PF, 8, MSA), F32)],
+        compiler_params=PARAMS,
+        cost_estimate=pl.CostEstimate(flops=10**8, bytes_accessed=2 * 10**6, transcendentals=10**4),
+        name="msa",
+    )(x, w)
 
 
 PIECES = [
@@ -131,12 +170,6 @@
         bias_ref[h * ROWS : (h + 1) * ROWS, :] = jnp.concatenate(done + [tail], axis=1).astype(BF)
 
 
-VMEM = pl.BlockSpec(memory_space=pltpu.VMEM)
-SMEM = pl.BlockSpec(memory_space=pltpu.SMEM)
-ANY = pl.BlockSpec(memory_space=pl.ANY)
-PARAMS = pltpu.CompilerParams(vmem_limit_bytes=56 * 1024 * 1024)
-
-
 def opm(pos, left, pieces, w, emb, off):
     return pl.pallas_call(
         opm_kernel,
@@ -160,27 +193,32 @@
     )(pos, left, *pieces, w, emb, off)
 
 
+AT_ROWS = 3
+PR_ROWS = 4
+
+
 def project_kernel(own_ref, prev_ref, next_ref, far_ref, qkg_ref, q_ref, gate_ref, kv_ref):
-    own = own_ref[0]
-    four = (own, prev_ref[0], next_ref[0], far_ref[0])
-    keys_in = jnp.concatenate([f[:LANES] for f in four] + [f[LANES:] for f in four], axis=0)
-    q_ref[0] = (dot(own, qkg_ref[:, :CH], NN) * (HD ** (-0.5) * LOG2E)).astype(BF)
-    gate_ref[0] = jax.nn.sigmoid(dot(own, qkg_ref[:, 3 * CH :], NN))
-    kv_ref[0] = dot(keys_in, qkg_ref[:, CH : 3 * CH], NN).astype(BF)
+    for r in range(PR_ROWS):
+        own = own_ref[r]
+        four = (own, prev_ref[r], next_ref[r], far_ref[r])
+        keys_in = jnp.concatenate([f[:LANES] for f in four] + [f[LANES:] for f in four], axis=0)
+        q_ref[r] = (dot(own, qkg_ref[:, :CH], NN) * (HD ** (-0.5) * LOG2E)).astype(BF)
+        gate_ref[r] = jax.nn.sigmoid(dot(own, qkg_ref[:, 3 * CH :], NN))
+        kv_ref[r] = dot(keys_in, qkg_ref[:, CH : 3 * CH], NN).astype(BF)
 
 
 def project(own, prev, nxt, far, qkg):
-    row = pl.BlockSpec((1, COLS, CH), lambda i: (i, 0, 0))
+    row = pl.BlockSpec((PR_ROWS, COLS, CH), lambda i: (i, 0, 0))
     return pl.pallas_call(
         project_kernel,
-        grid=(ROWS,),
+        grid=(ROWS // PR_ROWS,),
         out_shape=(
             jax.ShapeDtypeStruct((ROWS, COLS, CH), BF),
             jax.ShapeDtypeStruct((ROWS, COLS, CH), F32),
             jax.ShapeDtypeStruct((ROWS, 4 * COLS, 2 * CH), BF),
         ),
         in_specs=[row] * 4 + [VMEM],
-        out_specs=[row, row, pl.BlockSpec((1, 4 * COLS, 2 * CH), lambda i: (i, 0, 0))],
+        out_specs=[row, row, pl.BlockSpec((PR_ROWS, 4 * COLS, 2 * CH), lambda i: (i, 0, 0))],
         compiler_params=PARAMS,
         cost_estimate=pl.CostEstimate(flops=10**10, bytes_accessed=2 * 10**7, transcendentals=10**5),
         name="project",
@@ -229,50 +267,44 @@
 
         lax.fori_loop(0, 8, place, 0)
 
-    q, gate, kv = q_ref[0], gate_ref[0], kv_ref[0]
-    k = kv[:, :CH]
-    v1 = jnp.concatenate([kv[:, CH:], jnp.ones((4 * COLS, CH), BF)], axis=1)
-    row_tile = (pos_ref[5] + i) // TILE
     run = lax.broadcasted_iota(jnp.int32, (1, 4 * COLS), 1) // HALF
-    pen = jnp.zeros((1, 4 * COLS), F32)
-    for rel, shift in enumerate((0, 3, 1, 2)):
-        col = lax.rem(x + shift, 4) * COLS
-        for slot, start in ((2 * rel, 0), (2 * rel + 1, HALF), (8 + rel, LANES)):
-            keep = filt_ref[row_tile, (col + start) // TILE]
-            pen = jnp.where(run == slot, (keep.astype(F32) - 1.0) * 1000000000.0, pen)
     lane_head = lax.broadcasted_iota(jnp.int32, (COLS, CH), 1) // HD
-    att = jnp.zeros((COLS, CH), F32)
-    for h in range(HEADS):
-        mine = lane_head == h
-        qh = jnp.where(mine, q, jnp.zeros_like(q))
-        s = dot(qh, k, NT) + bias[h] + pen
-        p = jnp.exp2(s - jnp.max(s, axis=-1, keepdims=True)).astype(BF)
-        o = dot(p, v1, NN)
-        att = jnp.where(mine, o[:, :CH] / o[:, CH:], att)
-    gated = (gate * att).astype(BF)
-    out_ref[0] = dot(gated, wo_ref[...], NN).astype(BF)
+    for r in range(AT_ROWS):
+        q, k = q_ref[r], kv_ref[r, :, :CH]
+        v1 = jnp.concatenate([kv_ref[r, :, CH:], jnp.ones((4 * COLS, CH), BF)], axis=1)
+        row_tile = (pos_ref[5] + i * AT_ROWS + r) // TILE
+        pen = jnp.zeros((1, 4 * COLS), F32)
+        for rel, shift in enumerate((0, 3, 1, 2)):
+            col = lax.rem(x + shift, 4) * COLS
+            for slot, start in ((2 * rel, 0), (2 * rel + 1, HALF), (8 + rel, LANES)):
+                keep = filt_ref[row_tile, (col + start) // TILE]
+                pen = jnp.where(run == slot, (keep.astype(F32) - 1.0) * 1000000000.0, pen)
+        att = jnp.zeros((COLS, CH), F32)
+        for h in range(HEADS):
+            mine = lane_head == h
+            qh = jnp.where(mine, q, jnp.zeros_like(q))
+            s = dot(qh, k, NT) + bias[h] + pen
+            p = jnp.exp2(s - jnp.max(s, axis=-1, keepdims=True)).astype(BF)
+            o = dot(p, v1, NN)
+            att = jnp.where(mine, o[:, :CH] / o[:, CH:], att)
+        gated = (gate_ref[r] * att).astype(BF)
+        out_ref[r] = dot(gated, wo_ref[...], NN).astype(BF)
 
 
 def attend(pos, filt, q, gate, kv, pay0, pay1, wo):
-    row = pl.BlockSpec((1, COLS, CH), lambda i: (i, 0, 0))
+    row = pl.BlockSpec((AT_ROWS, COLS, CH), lambda i: (i, 0, 0))
+    keys = pl.BlockSpec((AT_ROWS, 4 * COLS, 2 * CH), lambda i: (i, 0, 0))
     return pl.pallas_call(
         attend_kernel,
-        grid=(ROWS,),
+        grid=(ROWS // AT_ROWS,),
         out_shape=jax.ShapeDtypeStruct((ROWS, COLS, CH), BF),
-        in_specs=[SMEM, SMEM, row, row, pl.BlockSpec((1, 4 * COLS, 2 * CH), lambda i: (i, 0, 0))] + [VMEM] * 3,
+        in_specs=[SMEM, SMEM, row, row, keys] + [VMEM] * 3,
         out_specs=row,
         scratch_shapes=[pltpu.VMEM((HEADS, COLS, 4 * COLS), F32)],
         compiler_params=PARAMS,
         cost_estimate=pl.CostEstimate(flops=8 * 10**9, bytes_accessed=10**7, transcendentals=7 * 10**6),
         name="attend",
     )(pos, filt, q, gate, kv, pay0, pay1, wo)
-
-
-def standardise_features(values):
-    widened = values.astype(F32)
-    centered = widened - jnp.mean(widened, axis=-1, keepdims=True)
-    spread = jnp.mean(centered * centered, axis=-1, keepdims=True)
-    return centered * lax.rsqrt(spread + 1e-05)
 
 
 ALL = ("zh", "zl", "y", "c", "x")
@@ -306,11 +338,7 @@
     pp = lax.ppermute
     zh, zl = lax.axis_index("zh"), lax.axis_index("zl")
     y, c, x = lax.axis_index("y"), lax.axis_index("c"), lax.axis_index("x")
-    normed = standardise_features(stack).astype(BF)
-    proj = jnp.einsum("sjc,cx->jxs", normed, entry, preferred_element_type=F32).astype(BF)
-    left = proj[:, :PF].reshape(BLK, MSA)
-    right = proj[:, PF:].transpose(1, 0, 2)
-    right = jnp.concatenate([right[:, :8].reshape(8 * PF, MSA), right[:, 8:].reshape(4 * PF, MSA)], axis=0)
+    left, right = msa_project(stack.transpose(1, 0, 2), entry.T)
     row0 = (zh * 16 + zl * 8 + y * 2 + c) * ROWS
     prepared = (
         final.reshape(PF, PF, CH).transpose(1, 0, 2),

time: 129 us -> 124 us (0.961)
  other arithmetic: 4.42 us -> 0.01 us
  waiting for transfers between devices: 17.5 us -> 21.2 us
  matrix products: 1.31 us -> 0 us
    reduce_sum x2 -> x0, other arithmetic: 4.37 us -> none  [the longest x1 2.37 us: standardise_features(): spread = jnp.mean(centered * centered, axis=-1, keepdims=True)]
    all_to_all x1, waiting for transfers between devices: 0.14 us -> 3.55 us  [body(): pay0 = lax.all_to_all(col, ('zl', 'y'), 0, 0, tiled=True)]
    dot_general x1 -> x0, matrix products: 1.31 us -> none  [body(): jnp.einsum('sjc,cx->jxs', normed, entry, preferred_element_type=F32)]
    pallas_call x2 -> x3, Pallas kernels: 28.7 us -> 28.2 us  [the longest x1 18.7 us: attend(): pl.pallas_call(attend_kernel, grid=(ROWS // AT_ROWS,), out_shape=jax.Shap...]
  transfers between devices with their start and end apart: 25 -> 25, of which waited for: 11 -> 11; matrix products, arithmetic and copies ran while one was open for 2% -> 2% of each run, Pallas kernels for 7% -> 5%
where the time goes in v3:
time: 124 us
  starting transfers between devices  59.8 us (48%)
  Pallas kernels  37.4 us (30%)
  waiting for transfers between devices  21.2 us (17%)
  local copies, waits for them, and re-layouts  4.61 us (4%)
    pallas_call x1, Pallas kernels, attend(): pl.pallas_call(attend_kernel, grid=(ROWS // AT_ROWS,), out_shape=jax.Shap...  18.7 us
    ppermute x3, starting transfers between devices, gather_bias_z(): lax.ppermute(own, 'zh', ring(4, k))  17.1 us
    ppermute x8, starting transfers between devices, gather_right(): return mine + [pp(m, 'c', ring(2, 1)) for m in mine]  14.6 us
    pallas_call x1, Pallas kernels, opm(): pl.pallas_call(opm_kernel, out_shape=(jax.ShapeDtypeStruct((ROWS, COLS, C...  9.21 us
    ppermute x1, starting transfers between devices, body(): pp(right, ALL, SPREAD)  7.74 us
    pallas_call x1, Pallas kernels, project(): pl.pallas_call(project_kernel, grid=(ROWS // PR_ROWS,), out_shape=(jax.Sh...  5.95 us
    ppermute x3, waiting for transfers between devices, body(): prev, nxt, far = [pp(norm, 'x', ring(4, k)) for k in (1, 3, 2)]  5.25 us
    all_to_all x1, starting transfers between devices, body(): pay0 = lax.all_to_all(col, ('zl', 'y'), 0, 0, tiled=True)  4.87 us
  transfers between devices with their start and end apart: 25, of which 11 were waited for; matrix products, arithmetic and copies ran while one was open for 2% of the time, Pallas kernels for 5%

profile of v3, /device:TPU:1, one launch (start us, length us, event | category | flops | bytes accessed | tf_op | source)
XLA Modules:
  0.0 123.9 jit_solution(15235487804792415518)
XLA Ops:
  0.7 3.5 %msa.1 = (bf16[384,256]{1,0:T(8,128)(2,1)}, bf16[384,256]{1,0:T(8,128)(2,1)}) custom-call(bf16[12,256,256]{2,1,0:T(8,128)(2,1)} %bitcast.17, bf16[64,256]{1,0:T(8,128)(2,1)} %bitcast.20), custom_call_target="tpu_custom_call" | custom-call | flops 100000000 | bytes 2000000 | tf_op jit(solution)/shard_map/msa/pallas_call | solution.py:58
  4.1 7.7 %collective-permute-start = (bf16[384,256]{1,0:T(8,128)(2,1)}, bf16[384,256]{1,0:T(8,128)(2,1)S(1)}, u32[]{:S(2)}, u32[]{:S(2)}) collective-permute-start(bf16[384,256]{1,0:T(8,128)(2,1)} %get-tuple-element.22), channel_id=1, source_target_pairs={{2,0},{1,64},{0,128},{3,192},{6,4},{5,68},{4,132},{7,196},{10,8},{... | collective-permute-start | bytes 589832 | tf_op jit(solution)/shard_map/ppermute | solution.py:348
  11.9 0.8 copy.12
  13.9 1.9 %collective-permute-done.refs_0_ = bf16[384,256]{1,0:T(8,128)(2,1)S(1)} collective-permute-done((bf16[384,256]{1,0:T(8,128)(2,1)}, bf16[384,256]{1,0:T(8,128)(2,1)S(1)}, u32[]{:S(2)}, u32[]{:S(2)}) %collective-permute-start) | collective-permute-done | bytes 196640 | tf_op jit(solution)/shard_map/ppermute | solution.py:348
  15.8 2.9 %collective-permute-start.4 = (bf16[384,256]{1,0:T(8,128)(2,1)S(1)}, bf16[384,256]{1,0:T(8,128)(2,1)S(1)}, u32[]{:S(2)}, u32[]{:S(2)}) collective-permute-start(bf16[384,256]{1,0:T(8,128)(2,1)S(1)} %collective-permute-done.refs_0_), channel_id=1, source_target_pairs={{0,16},{8,24},{16,0},{24,8},{1,17},{9,25},{17,1},{25,9},{2,18},{10... | collective-permute-start | bytes 589832 | tf_op jit(solution)/shard_map/ppermute | solution.py:325
  18.7 5.9 %collective-permute-start.8 = (bf16[384,256]{1,0:T(8,128)(2,1)S(1)}, bf16[384,256]{1,0:T(8,128)(2,1)S(1)}, u32[]{:S(2)}, u32[]{:S(2)}) collective-permute-start(bf16[384,256]{1,0:T(8,128)(2,1)S(1)} %collective-permute-done.refs_0_), channel_id=1, source_target_pairs={{0,4},{4,0},{1,5},{5,1},{2,6},{6,2},{3,7},{7,3},{8,12},{12,8},{9,1... | collective-permute-start | bytes 589832 | tf_op jit(solution)/shard_map/ppermute | solution.py:329
  24.6 0.8 collective-permute-start.3
  25.4 0.7 collective-permute-start.2
  26.1 2.6 %collective-permute-start.12 = (bf16[384,256]{1,0:T(8,128)(2,1)S(1)}, bf16[384,256]{1,0:T(8,128)(2,1)S(1)}, u32[]{:S(2)}, u32[]{:S(2)}) collective-permute-start(bf16[384,256]{1,0:T(8,128)(2,1)S(1)} %collective-permute-done.4.refs_4_), channel_id=1, source_target_pairs={{0,4},{4,0},{1,5},{5,1},{2,6},{6,2},{3,7},{7,3},{8,12},{12,8},{9,1... | collective-permute-start | bytes 589832 | tf_op jit(solution)/shard_map/ppermute | solution.py:329
  28.7 3.0 %collective-permute-done.3.refs_3_ = bf16[384,256]{1,0:T(8,128)(2,1)S(1)} collective-permute-done((bf16[384,256]{1,0:T(8,128)(2,1)S(1)}, bf16[384,256]{1,0:T(8,128)(2,1)S(1)}, u32[]{:S(2)}, u32[]{:S(2)}) %collective-permute-start.3) | collective-permute-done | bytes 196640 | tf_op jit(solution)/shard_map/ppermute | solution.py:325
  31.7 1.5 %collective-permute-start.11 = (bf16[384,256]{1,0:T(8,128)(2,1)S(1)}, bf16[384,256]{1,0:T(8,128)(2,1)S(1)}, u32[]{:S(2)}, u32[]{:S(2)}) collective-permute-start(bf16[384,256]{1,0:T(8,128)(2,1)S(1)} %collective-permute-done.3.refs_3_), channel_id=1, source_target_pairs={{0,4},{4,0},{1,5},{5,1},{2,6},{6,2},{3,7},{7,3},{8,12},{12,8},{9,1... | collective-permute-start | bytes 589832 | tf_op jit(solution)/shard_map/ppermute | solution.py:329
  33.2 2.5 %collective-permute-start.6 = (bf16[384,256]{1,0:T(8,128)(2,1)S(1)}, bf16[384,256]{1,0:T(8,128)(2,1)S(1)}, u32[]{:S(2)}, u32[]{:S(2)}) collective-permute-start(bf16[384,256]{1,0:T(8,128)(2,1)S(1)} %collective-permute-done.1.refs_1_), channel_id=1, source_target_pairs={{0,24},{8,0},{16,8},{24,16},{1,25},{9,1},{17,9},{25,17},{2,26},{10... | collective-permute-start | bytes 589832 | tf_op jit(solution)/shard_map/ppermute | solution.py:326
  36.2 2.4 %collective-permute-start.9 = (bf16[384,256]{1,0:T(8,128)(2,1)S(1)}, bf16[384,256]{1,0:T(8,128)(2,1)S(1)}, u32[]{:S(2)}, u32[]{:S(2)}) collective-permute-start(bf16[384,256]{1,0:T(8,128)(2,1)S(1)} %collective-permute-done.1.refs_1_), channel_id=1, source_target_pairs={{0,4},{4,0},{1,5},{5,1},{2,6},{6,2},{3,7},{7,3},{8,12},{12,8},{9,1... | collective-permute-start | bytes 589832 | tf_op jit(solution)/shard_map/ppermute | solution.py:329
  38.8 1.7 %collective-permute-done.5.refs_5_ = bf16[384,256]{1,0:T(8,128)(2,1)S(1)} collective-permute-done((bf16[384,256]{1,0:T(8,128)(2,1)S(1)}, bf16[384,256]{1,0:T(8,128)(2,1)S(1)}, u32[]{:S(2)}, u32[]{:S(2)}) %collective-permute-start.5) | collective-permute-done | bytes 196640 | tf_op jit(solution)/shard_map/ppermute | solution.py:327
  40.4 1.4 %collective-permute-start.13 = (bf16[384,256]{1,0:T(8,128)(2,1)S(1)}, bf16[384,256]{1,0:T(8,128)(2,1)S(1)}, u32[]{:S(2)}, u32[]{:S(2)}) collective-permute-start(bf16[384,256]{1,0:T(8,128)(2,1)S(1)} %collective-permute-done.5.refs_5_), channel_id=1, source_target_pairs={{0,4},{4,0},{1,5},{5,1},{2,6},{6,2},{3,7},{7,3},{8,12},{12,8},{9,1... | collective-permute-start | bytes 589832 | tf_op jit(solution)/shard_map/ppermute | solution.py:329
  42.2 0.7 collective-permute-done.13.refs_13_
  44.0 9.2 %opm.1 = (bf16[12,192,128]{2,1,0:T(8,128)(2,1)}, bf16[12,192,128]{2,1,0:T(8,128)(2,1)}, bf16[48,256]{1,0:T(8,128)(2,1)}) custom-call(s32[6]{0:T(128)} %stack.42.pos_ref, bf16[384,256]{1,0:T(8,128)(2,1)} %get-tuple-element.24.lt_ref, bf16[384,256]{1,0:T(8,128)(2,1)} %copy-done.7, bf16[384,256]{1,0:T(8,128)(2,1)} %copy-done.12, bf16[384,256]{1,0:T(8,128)(2,1)} %copy-done.11, ...), custom_call_target="tpu_custom_call" | custom-call | flops 6000000000 | bytes 10000000 | tf_op jit(solution)/shard_map/opm/pallas_call | solution.py:174
  53.3 3.2 %collective-permute-start.17 = (bf16[12,192,128]{2,1,0:T(8,128)(2,1)}, bf16[12,192,128]{2,1,0:T(8,128)(2,1)S(1)}, u32[]{:S(2)}, u32[]{:S(2)}) collective-permute-start(bf16[12,192,128]{2,1,0:T(8,128)(2,1)} %get-tuple-element.29.own_ref), channel_id=1, source_target_pairs={{0,3},{1,0},{2,1},{3,2},{4,7},{5,4},{6,5},{7,6},{8,11},{9,8},{10,9... | collective-permute-start | bytes 1769480 | tf_op jit(solution)/shard_map/ppermute | solution.py:351
  57.0 1.4 %collective-permute-start.19 = (bf16[48,256]{1,0:T(8,128)(2,1)}, bf16[48,256]{1,0:T(8,128)(2,1)S(1)}, u32[]{:S(2)}, u32[]{:S(2)}) collective-permute-start(bf16[48,256]{1,0:T(8,128)(2,1)} %get-tuple-element.30), channel_id=1, source_target_pairs={{0,0},{1,64},{2,128},{3,192},{4,4},{5,68},{6,132},{7,196},{8,8},{9... | collective-permute-start | bytes 73736 | tf_op jit(solution)/shard_map/ppermute | solution.py:352
  58.3 13.0 %collective-permute-start.22 = (bf16[48,256]{1,0:T(8,128)(2,1)S(1)}, bf16[48,256]{1,0:T(8,128)(2,1)S(1)}, u32[]{:S(2)}, u32[]{:S(2)}) collective-permute-start(bf16[48,256]{1,0:T(8,128)(2,1)S(1)} %collective-permute-done.19), channel_id=1, source_target_pairs={{0,192},{64,0},{128,64},{192,128},{1,193},{65,1},{129,65},{193,129... | collective-permute-start | bytes 73736 | tf_op jit(solution)/shard_map/ppermute | solution.py:333
  71.3 1.8 %collective-permute-start.21 = (bf16[48,256]{1,0:T(8,128)(2,1)S(1)}, bf16[48,256]{1,0:T(8,128)(2,1)S(1)}, u32[]{:S(2)}, u32[]{:S(2)}) collective-permute-start(bf16[48,256]{1,0:T(8,128)(2,1)S(1)} %collective-permute-done.19), channel_id=1, source_target_pairs={{0,128},{64,192},{128,0},{192,64},{1,129},{65,193},{129,1},{193,65... | collective-permute-start | bytes 73736 | tf_op jit(solution)/shard_map/ppermute | solution.py:333
  73.1 2.4 %collective-permute-start.20 = (bf16[48,256]{1,0:T(8,128)(2,1)S(1)}, bf16[48,256]{1,0:T(8,128)(2,1)S(1)}, u32[]{:S(2)}, u32[]{:S(2)}) collective-permute-start(bf16[48,256]{1,0:T(8,128)(2,1)S(1)} %collective-permute-done.19), channel_id=1, source_target_pairs={{0,64},{64,128},{128,192},{192,0},{1,65},{65,129},{129,193},{193,1... | collective-permute-start | bytes 73736 | tf_op jit(solution)/shard_map/ppermute | solution.py:333
  75.5 2.5 %collective-permute-done.21 = bf16[48,256]{1,0:T(8,128)(2,1)S(1)} collective-permute-done((bf16[48,256]{1,0:T(8,128)(2,1)S(1)}, bf16[48,256]{1,0:T(8,128)(2,1)S(1)}, u32[]{:S(2)}, u32[]{:S(2)}) %collective-permute-start.21) | collective-permute-done | bytes 24608 | tf_op jit(solution)/shard_map/ppermute | solution.py:333
  78.2 5.2 %collective-permute-done.17.next_ref = bf16[12,192,128]{2,1,0:T(8,128)(2,1)S(1)} collective-permute-done((bf16[12,192,128]{2,1,0:T(8,128)(2,1)}, bf16[12,192,128]{2,1,0:T(8,128)(2,1)S(1)}, u32[]{:S(2)}, u32[]{:S(2)}) %collective-permute-start.17) | collective-permute-done | bytes 589856 | tf_op jit(solution)/shard_map/ppermute | solution.py:351
  83.5 1.0 broadcast_in_dim.2
  84.5 4.9 %all-to-all-start = ((bf16[8,4,48,256]{3,2,1,0:T(8,128)(2,1)}), bf16[8,4,48,256]{3,2,1,0:T(8,128)(2,1)S(1)}, u32[]{:S(2)}, u32[]{:S(2)}) async-start(bf16[8,4,48,256]{3,2,1,0:T(8,128)(2,1)} %broadcast_in_dim.2), calls=%async_computation | async-start | bytes 1572864 | tf_op jit(solution)/shard_map/all_to_all | solution.py:355
  89.4 5.9 %project.1 = (bf16[12,192,128]{2,1,0:T(8,128)(2,1)}, f32[12,192,128]{2,1,0:T(8,128)}, bf16[12,768,256]{2,1,0:T(8,128)(2,1)}) custom-call(bf16[12,192,128]{2,1,0:T(8,128)(2,1)} %get-tuple-element.29.own_ref, bf16[12,192,128]{2,1,0:T(8,128)(2,1)} %copy-done.6, bf16[12,192,128]{2,1,0:T(8,128)(2,1)} %copy-done.5, bf16[12,192,128]{2,1,0:T(8,128)(2,1)} %copy-done.4, ...), custom_call_target="tpu_custom_call" | custom-call | flops 10000000000 | bytes 20000000 | tf_op jit(solution)/shard_map/project/pallas_call | solution.py:212
  95.3 3.5 %all-to-all-done.pay0_ref = bf16[8,4,48,256]{3,2,1,0:T(8,128)(2,1)S(1)} async-done(((bf16[8,4,48,256]{3,2,1,0:T(8,128)(2,1)}), bf16[8,4,48,256]{3,2,1,0:T(8,128)(2,1)S(1)}, u32[]{:S(2)}, u32[]{:S(2)}) %all-to-all-start) | async-done | bytes 786464 | tf_op jit(solution)/shard_map/all_to_all | solution.py:355
  98.9 3.4 %collective-permute-start.23 = (bf16[8,4,48,256]{3,2,1,0:T(8,128)(2,1)S(1)}, bf16[8,4,48,256]{3,2,1,0:T(8,128)(2,1)S(1)}, u32[]{:S(2)}, u32[]{:S(2)}) collective-permute-start(bf16[8,4,48,256]{3,2,1,0:T(8,128)(2,1)S(1)} %all-to-all-done.pay0_ref), channel_id=1, source_target_pairs={{0,4},{4,0},{1,5},{5,1},{2,6},{6,2},{3,7},{7,3},{8,12},{12,8},{9,1... | collective-permute-start | bytes 2359304 | tf_op jit(solution)/shard_map/ppermute | solution.py:357
  102.3 1.9 %collective-permute-done.23.pay1_ref = bf16[8,4,48,256]{3,2,1,0:T(8,128)(2,1)S(1)} collective-permute-done((bf16[8,4,48,256]{3,2,1,0:T(8,128)(2,1)S(1)}, bf16[8,4,48,256]{3,2,1,0:T(8,128)(2,1)S(1)}, u32[]{:S(2)}, u32[]{:S(2)}) %collective-permute-start.23) | collective-permute-done | bytes 786464 | tf_op jit(solution)/shard_map/ppermute | solution.py:357
  104.2 0.9 copy-done.3
  105.2 18.7 %attend.1 = bf16[12,192,128]{2,1,0:T(8,128)(2,1)} custom-call(s32[6]{0:T(128)} %stack.42.pos_ref, s32[6,6]{1,0:T(8,128)} %filt_ref.1, bf16[12,192,128]{2,1,0:T(8,128)(2,1)} %get-tuple-element.38.q_ref, f32[12,192,128]{2,1,0:T(8,128)} %get-tuple-element.39.gate_ref, bf16[12,768,256]{2,1,0:T(8,128)(2,1)} %get-tuple-element.40.kv_ref, ...), custom_call_target="tpu_custom_call" | custom-call | flops 8000000000 | bytes 10000000 | tf_op jit(solution)/shard_map/attend/pallas_call | solution.py:297
  (73 shorter events, 3.9 us)
Async XLA Ops:
  0.6 11.3 %copy-start.1 = (bf16[1024,128]{1,0:T(8,128)(2,1)S(1)}, bf16[1024,128]{1,0:T(8,128)(2,1)}, u32[]{:S(2)}) copy-start(bf16[1024,128]{1,0:T(8,128)(2,1)} %param.11) | copy-start | bytes 786436
  0.6 12.1 %copy-start.2 = (f32[128,4]{0,1:T(4,128)S(1)}, f32[128,4]{0,1:T(4,128)}, u32[]{:S(2)}) copy-start(f32[128,4]{0,1:T(4,128)} %param.13) | copy-start | bytes 6148
  4.1 11.6 %collective-permute-start = (bf16[384,256]{1,0:T(8,128)(2,1)}, bf16[384,256]{1,0:T(8,128)(2,1)S(1)}, u32[]{:S(2)}, u32[]{:S(2)}) collective-permute-start(bf16[384,256]{1,0:T(8,128)(2,1)} %get-tuple-element.22), channel_id=1, source_target_pairs={{2,0},{1,64},{0,128},{3,192},{6,4},{5,68},{4,132},{7,196},{10,8},{... | collective-permute-start | bytes 589832 | tf_op jit(solution)/shard_map/ppermute | solution.py:348
  15.8 27.5 %copy-start.7 = (bf16[384,256]{1,0:T(8,128)(2,1)}, bf16[384,256]{1,0:T(8,128)(2,1)S(1)}, u32[]{:S(2)}) copy-start(bf16[384,256]{1,0:T(8,128)(2,1)S(1)} %collective-permute-done.refs_0_) | copy-start | bytes 589828
  15.8 10.3 %collective-permute-start.4 = (bf16[384,256]{1,0:T(8,128)(2,1)S(1)}, bf16[384,256]{1,0:T(8,128)(2,1)S(1)}, u32[]{:S(2)}, u32[]{:S(2)}) collective-permute-start(bf16[384,256]{1,0:T(8,128)(2,1)S(1)} %collective-permute-done.refs_0_), channel_id=1, source_target_pairs={{0,16},{8,24},{16,0},{24,8},{1,17},{9,25},{17,1},{25,9},{2,18},{10... | collective-permute-start | bytes 589832 | tf_op jit(solution)/shard_map/ppermute | solution.py:325
  18.7 10.0 %collective-permute-start.8 = (bf16[384,256]{1,0:T(8,128)(2,1)S(1)}, bf16[384,256]{1,0:T(8,128)(2,1)S(1)}, u32[]{:S(2)}, u32[]{:S(2)}) collective-permute-start(bf16[384,256]{1,0:T(8,128)(2,1)S(1)} %collective-permute-done.refs_0_), channel_id=1, source_target_pairs={{0,4},{4,0},{1,5},{5,1},{2,6},{6,2},{3,7},{7,3},{8,12},{12,8},{9,1... | collective-permute-start | bytes 589832 | tf_op jit(solution)/shard_map/ppermute | solution.py:329
  24.6 7.1 %collective-permute-start.3 = (bf16[384,256]{1,0:T(8,128)(2,1)S(1)}, bf16[384,256]{1,0:T(8,128)(2,1)S(1)}, u32[]{:S(2)}, u32[]{:S(2)}) collective-permute-start(bf16[384,256]{1,0:T(8,128)(2,1)S(1)} %collective-permute-done.refs_0_), channel_id=1, source_target_pairs={{0,24},{8,0},{16,8},{24,16},{1,25},{9,1},{17,9},{25,17},{2,26},{10... | collective-permute-start | bytes 589832 | tf_op jit(solution)/shard_map/ppermute | solution.py:325
  25.4 7.8 %collective-permute-start.2 = (bf16[384,256]{1,0:T(8,128)(2,1)S(1)}, bf16[384,256]{1,0:T(8,128)(2,1)S(1)}, u32[]{:S(2)}, u32[]{:S(2)}) collective-permute-start(bf16[384,256]{1,0:T(8,128)(2,1)S(1)} %collective-permute-done.refs_0_), channel_id=1, source_target_pairs={{0,8},{8,16},{16,24},{24,0},{1,9},{9,17},{17,25},{25,1},{2,10},{10... | collective-permute-start | bytes 589832 | tf_op jit(solution)/shard_map/ppermute | solution.py:325
  26.1 7.1 %collective-permute-start.1 = (bf16[384,256]{1,0:T(8,128)(2,1)S(1)}, bf16[384,256]{1,0:T(8,128)(2,1)S(1)}, u32[]{:S(2)}, u32[]{:S(2)}) collective-permute-start(bf16[384,256]{1,0:T(8,128)(2,1)S(1)} %collective-permute-done.refs_0_), channel_id=1, source_target_pairs={{0,32},{32,0},{1,33},{33,1},{2,34},{34,2},{3,35},{35,3},{4,36},{36... | collective-permute-start | bytes 589832 | tf_op jit(solution)/shard_map/ppermute | solution.py:324
  26.1 17.2 %copy-start.8 = (bf16[384,256]{1,0:T(8,128)(2,1)}, bf16[384,256]{1,0:T(8,128)(2,1)S(1)}, u32[]{:S(2)}) copy-start(bf16[384,256]{1,0:T(8,128)(2,1)S(1)} %collective-permute-done.4.refs_4_) | copy-start | bytes 589828
  26.1 9.6 %collective-permute-start.12 = (bf16[384,256]{1,0:T(8,128)(2,1)S(1)}, bf16[384,256]{1,0:T(8,128)(2,1)S(1)}, u32[]{:S(2)}, u32[]{:S(2)}) collective-permute-start(bf16[384,256]{1,0:T(8,128)(2,1)S(1)} %collective-permute-done.4.refs_4_), channel_id=1, source_target_pairs={{0,4},{4,0},{1,5},{5,1},{2,6},{6,2},{3,7},{7,3},{8,12},{12,8},{9,1... | collective-permute-start | bytes 589832 | tf_op jit(solution)/shard_map/ppermute | solution.py:329
  28.7 14.6 %copy-start.9 = (bf16[384,256]{1,0:T(8,128)(2,1)}, bf16[384,256]{1,0:T(8,128)(2,1)S(1)}, u32[]{:S(2)}) copy-start(bf16[384,256]{1,0:T(8,128)(2,1)S(1)} %collective-permute-done.8.refs_8_) | copy-start | bytes 589828
  28.7 7.5 %collective-permute-start.7 = (bf16[384,256]{1,0:T(8,128)(2,1)S(1)}, bf16[384,256]{1,0:T(8,128)(2,1)S(1)}, u32[]{:S(2)}, u32[]{:S(2)}) collective-permute-start(bf16[384,256]{1,0:T(8,128)(2,1)S(1)} %collective-permute-done.4.refs_4_), channel_id=1, source_target_pairs={{0,32},{32,0},{1,33},{33,1},{2,34},{34,2},{3,35},{35,3},{4,36},{36... | collective-permute-start | bytes 589832 | tf_op jit(solution)/shard_map/ppermute | solution.py:327
  31.7 11.6 %copy-start.10 = (bf16[384,256]{1,0:T(8,128)(2,1)}, bf16[384,256]{1,0:T(8,128)(2,1)S(1)}, u32[]{:S(2)}) copy-start(bf16[384,256]{1,0:T(8,128)(2,1)S(1)} %collective-permute-done.3.refs_3_) | copy-start | bytes 589828
  31.7 6.9 %collective-permute-start.11 = (bf16[384,256]{1,0:T(8,128)(2,1)S(1)}, bf16[384,256]{1,0:T(8,128)(2,1)S(1)}, u32[]{:S(2)}, u32[]{:S(2)}) collective-permute-start(bf16[384,256]{1,0:T(8,128)(2,1)S(1)} %collective-permute-done.3.refs_3_), channel_id=1, source_target_pairs={{0,4},{4,0},{1,5},{5,1},{2,6},{6,2},{3,7},{7,3},{8,12},{12,8},{9,1... | collective-permute-start | bytes 589832 | tf_op jit(solution)/shard_map/ppermute | solution.py:329
  33.2 7.2 %collective-permute-start.5 = (bf16[384,256]{1,0:T(8,128)(2,1)S(1)}, bf16[384,256]{1,0:T(8,128)(2,1)S(1)}, u32[]{:S(2)}, u32[]{:S(2)}) collective-permute-start(bf16[384,256]{1,0:T(8,128)(2,1)S(1)} %collective-permute-done.2.refs_2_), channel_id=1, source_target_pairs={{0,32},{32,0},{1,33},{33,1},{2,34},{34,2},{3,35},{35,3},{4,36},{36... | collective-permute-start | bytes 589832 | tf_op jit(solution)/shard_map/ppermute | solution.py:327
  33.2 8.6 %collective-permute-start.6 = (bf16[384,256]{1,0:T(8,128)(2,1)S(1)}, bf16[384,256]{1,0:T(8,128)(2,1)S(1)}, u32[]{:S(2)}, u32[]{:S(2)}) collective-permute-start(bf16[384,256]{1,0:T(8,128)(2,1)S(1)} %collective-permute-done.1.refs_1_), channel_id=1, source_target_pairs={{0,24},{8,0},{16,8},{24,16},{1,25},{9,1},{17,9},{25,17},{2,26},{10... | collective-permute-start | bytes 589832 | tf_op jit(solution)/shard_map/ppermute | solution.py:326
  35.7 6.4 %collective-permute-start.10 = (bf16[384,256]{1,0:T(8,128)(2,1)S(1)}, bf16[384,256]{1,0:T(8,128)(2,1)S(1)}, u32[]{:S(2)}, u32[]{:S(2)}) collective-permute-start(bf16[384,256]{1,0:T(8,128)(2,1)S(1)} %collective-permute-done.2.refs_2_), channel_id=1, source_target_pairs={{0,4},{4,0},{1,5},{5,1},{2,6},{6,2},{3,7},{7,3},{8,12},{12,8},{9,1... | collective-permute-start | bytes 589832 | tf_op jit(solution)/shard_map/ppermute | solution.py:329
  36.2 5.9 %collective-permute-start.9 = (bf16[384,256]{1,0:T(8,128)(2,1)S(1)}, bf16[384,256]{1,0:T(8,128)(2,1)S(1)}, u32[]{:S(2)}, u32[]{:S(2)}) collective-permute-start(bf16[384,256]{1,0:T(8,128)(2,1)S(1)} %collective-permute-done.1.refs_1_), channel_id=1, source_target_pairs={{0,4},{4,0},{1,5},{5,1},{2,6},{6,2},{3,7},{7,3},{8,12},{12,8},{9,1... | collective-permute-start | bytes 589832 | tf_op jit(solution)/shard_map/ppermute | solution.py:329
  38.7 3.5 %collective-permute-start.15 = (bf16[384,256]{1,0:T(8,128)(2,1)S(1)}, bf16[384,256]{1,0:T(8,128)(2,1)S(1)}, u32[]{:S(2)}, u32[]{:S(2)}) collective-permute-start(bf16[384,256]{1,0:T(8,128)(2,1)S(1)} %collective-permute-done.7.refs_7_), channel_id=1, source_target_pairs={{0,4},{4,0},{1,5},{5,1},{2,6},{6,2},{3,7},{7,3},{8,12},{12,8},{9,1... | collective-permute-start | bytes 589832 | tf_op jit(solution)/shard_map/ppermute | solution.py:329
  40.4 2.5 %collective-permute-start.13 = (bf16[384,256]{1,0:T(8,128)(2,1)S(1)}, bf16[384,256]{1,0:T(8,128)(2,1)S(1)}, u32[]{:S(2)}, u32[]{:S(2)}) collective-permute-start(bf16[384,256]{1,0:T(8,128)(2,1)S(1)} %collective-permute-done.5.refs_5_), channel_id=1, source_target_pairs={{0,4},{4,0},{1,5},{5,1},{2,6},{6,2},{3,7},{7,3},{8,12},{12,8},{9,1... | collective-permute-start | bytes 589832 | tf_op jit(solution)/shard_map/ppermute | solution.py:329
  41.9 1.4 %collective-permute-start.14 = (bf16[384,256]{1,0:T(8,128)(2,1)S(1)}, bf16[384,256]{1,0:T(8,128)(2,1)S(1)}, u32[]{:S(2)}, u32[]{:S(2)}) collective-permute-start(bf16[384,256]{1,0:T(8,128)(2,1)S(1)} %collective-permute-done.6.refs_6_), channel_id=1, source_target_pairs={{0,4},{4,0},{1,5},{5,1},{2,6},{6,2},{3,7},{7,3},{8,12},{12,8},{9,1... | collective-permute-start | bytes 589832 | tf_op jit(solution)/shard_map/ppermute | solution.py:329
  53.2 25.0 %collective-permute-start.18 = (bf16[12,192,128]{2,1,0:T(8,128)(2,1)}, bf16[12,192,128]{2,1,0:T(8,128)(2,1)S(1)}, u32[]{:S(2)}, u32[]{:S(2)}) collective-permute-start(bf16[12,192,128]{2,1,0:T(8,128)(2,1)} %get-tuple-element.29.own_ref), channel_id=1, source_target_pairs={{0,2},{1,3},{2,0},{3,1},{4,6},{5,7},{6,4},{7,5},{8,10},{9,11},{10,... | collective-permute-start | bytes 1769480 | tf_op jit(solution)/shard_map/ppermute | solution.py:351
  53.3 30.2 %collective-permute-start.17 = (bf16[12,192,128]{2,1,0:T(8,128)(2,1)}, bf16[12,192,128]{2,1,0:T(8,128)(2,1)S(1)}, u32[]{:S(2)}, u32[]{:S(2)}) collective-permute-start(bf16[12,192,128]{2,1,0:T(8,128)(2,1)} %get-tuple-element.29.own_ref), channel_id=1, source_target_pairs={{0,3},{1,0},{2,1},{3,2},{4,7},{5,4},{6,5},{7,6},{8,11},{9,8},{10,9... | collective-permute-start | bytes 1769480 | tf_op jit(solution)/shard_map/ppermute | solution.py:351
  56.5 27.0 %collective-permute-start.16 = (bf16[12,192,128]{2,1,0:T(8,128)(2,1)}, bf16[12,192,128]{2,1,0:T(8,128)(2,1)S(1)}, u32[]{:S(2)}, u32[]{:S(2)}) collective-permute-start(bf16[12,192,128]{2,1,0:T(8,128)(2,1)} %get-tuple-element.29.own_ref), channel_id=1, source_target_pairs={{0,1},{1,2},{2,3},{3,0},{4,5},{5,6},{6,7},{7,4},{8,9},{9,10},{10,1... | collective-permute-start | bytes 1769480 | tf_op jit(solution)/shard_map/ppermute | solution.py:351
  57.0 1.4 %collective-permute-start.19 = (bf16[48,256]{1,0:T(8,128)(2,1)}, bf16[48,256]{1,0:T(8,128)(2,1)S(1)}, u32[]{:S(2)}, u32[]{:S(2)}) collective-permute-start(bf16[48,256]{1,0:T(8,128)(2,1)} %get-tuple-element.30), channel_id=1, source_target_pairs={{0,0},{1,64},{2,128},{3,192},{4,4},{5,68},{6,132},{7,196},{8,8},{9... | collective-permute-start | bytes 73736 | tf_op jit(solution)/shard_map/ppermute | solution.py:352
  58.3 14.8 %collective-permute-start.22 = (bf16[48,256]{1,0:T(8,128)(2,1)S(1)}, bf16[48,256]{1,0:T(8,128)(2,1)S(1)}, u32[]{:S(2)}, u32[]{:S(2)}) collective-permute-start(bf16[48,256]{1,0:T(8,128)(2,1)S(1)} %collective-permute-done.19), channel_id=1, source_target_pairs={{0,192},{64,0},{128,64},{192,128},{1,193},{65,1},{129,65},{193,129... | collective-permute-start | bytes 73736 | tf_op jit(solution)/shard_map/ppermute | solution.py:333
  71.3 6.7 %collective-permute-start.21 = (bf16[48,256]{1,0:T(8,128)(2,1)S(1)}, bf16[48,256]{1,0:T(8,128)(2,1)S(1)}, u32[]{:S(2)}, u32[]{:S(2)}) collective-permute-start(bf16[48,256]{1,0:T(8,128)(2,1)S(1)} %collective-permute-done.19), channel_id=1, source_target_pairs={{0,128},{64,192},{128,0},{192,64},{1,129},{65,193},{129,1},{193,65... | collective-permute-start | bytes 73736 | tf_op jit(solution)/shard_map/ppermute | solution.py:333
  73.1 5.1 %collective-permute-start.20 = (bf16[48,256]{1,0:T(8,128)(2,1)S(1)}, bf16[48,256]{1,0:T(8,128)(2,1)S(1)}, u32[]{:S(2)}, u32[]{:S(2)}) collective-permute-start(bf16[48,256]{1,0:T(8,128)(2,1)S(1)} %collective-permute-done.19), channel_id=1, source_target_pairs={{0,64},{64,128},{128,192},{192,0},{1,65},{65,129},{129,193},{193,1... | collective-permute-start | bytes 73736 | tf_op jit(solution)/shard_map/ppermute | solution.py:333
  78.2 11.1 %copy-start.4 = (bf16[12,192,128]{2,1,0:T(8,128)(2,1)}, bf16[12,192,128]{2,1,0:T(8,128)(2,1)S(1)}, u32[]{:S(2)}) copy-start(bf16[12,192,128]{2,1,0:T(8,128)(2,1)S(1)} %collective-permute-done.18.far_ref) | copy-start | bytes 1769476
  84.5 14.4 %all-to-all-start = ((bf16[8,4,48,256]{3,2,1,0:T(8,128)(2,1)}), bf16[8,4,48,256]{3,2,1,0:T(8,128)(2,1)S(1)}, u32[]{:S(2)}, u32[]{:S(2)}) async-start(bf16[8,4,48,256]{3,2,1,0:T(8,128)(2,1)} %broadcast_in_dim.2), calls=%async_computation | async-start | bytes 1572864 | tf_op jit(solution)/shard_map/all_to_all | solution.py:355
  98.9 5.3 %collective-permute-start.23 = (bf16[8,4,48,256]{3,2,1,0:T(8,128)(2,1)S(1)}, bf16[8,4,48,256]{3,2,1,0:T(8,128)(2,1)S(1)}, u32[]{:S(2)}, u32[]{:S(2)}) collective-permute-start(bf16[8,4,48,256]{3,2,1,0:T(8,128)(2,1)S(1)} %all-to-all-done.pay0_ref), channel_id=1, source_target_pairs={{0,4},{4,0},{1,5},{5,1},{2,6},{6,2},{3,7},{7,3},{8,12},{12,8},{9,1... | collective-permute-start | bytes 2359304 | tf_op jit(solution)/shard_map/ppermute | solution.py:357
  (16 other events, 67.4 us)

commit v4 on v3

--- a/solution.py
+++ b/solution.py
@@ -265,7 +265,7 @@
                     )
             return carry
 
-        lax.fori_loop(0, 8, place, 0)
+        lax.fori_loop(0, 8, place, 0, unroll=2)
 
     run = lax.broadcasted_iota(jnp.int32, (1, 4 * COLS), 1) // HALF
     lane_head = lax.broadcasted_iota(jnp.int32, (COLS, CH), 1) // HD
@@ -284,7 +284,7 @@
             mine = lane_head == h
             qh = jnp.where(mine, q, jnp.zeros_like(q))
             s = dot(qh, k, NT) + bias[h] + pen
-            p = jnp.exp2(s - jnp.max(s, axis=-1, keepdims=True)).astype(BF)
+            p = jnp.exp2((s - jnp.max(s, axis=-1, keepdims=True)).astype(BF))
             o = dot(p, v1, NN)
             att = jnp.where(mine, o[:, :CH] / o[:, CH:], att)
         gated = (gate_ref[r] * att).astype(BF)

time: 124 us -> 124 us (level)
  no operation moved by 1% of the time
where the time goes in v4:
time: 124 us
  starting transfers between devices  59.8 us (48%)
  Pallas kernels  37.1 us (30%)
  waiting for transfers between devices  21.2 us (17%)
  local copies, waits for them, and re-layouts  4.61 us (4%)
    pallas_call x1, Pallas kernels, attend(): pl.pallas_call(attend_kernel, grid=(ROWS // AT_ROWS,), out_shape=jax.Shap...  18.4 us
    ppermute x3, starting transfers between devices, gather_bias_z(): lax.ppermute(own, 'zh', ring(4, k))  17.1 us
    ppermute x8, starting transfers between devices, gather_right(): return mine + [pp(m, 'c', ring(2, 1)) for m in mine]  14.6 us
    pallas_call x1, Pallas kernels, opm(): pl.pallas_call(opm_kernel, out_shape=(jax.ShapeDtypeStruct((ROWS, COLS, C...  9.21 us
    ppermute x1, starting transfers between devices, body(): pp(right, ALL, SPREAD)  7.74 us
    pallas_call x1, Pallas kernels, project(): pl.pallas_call(project_kernel, grid=(ROWS // PR_ROWS,), out_shape=(jax.Sh...  5.95 us
    ppermute x3, waiting for transfers between devices, body(): prev, nxt, far = [pp(norm, 'x', ring(4, k)) for k in (1, 3, 2)]  5.25 us
    all_to_all x1, starting transfers between devices, body(): pay0 = lax.all_to_all(col, ('zl', 'y'), 0, 0, tiled=True)  4.87 us
  transfers between devices with their start and end apart: 25, of which 11 were waited for; matrix products, arithmetic and copies ran while one was open for 2% of the time, Pallas kernels for 5%

profile of v4, /device:TPU:1, one launch (start us, length us, event | category | flops | bytes accessed | tf_op | source)
XLA Modules:
  0.0 123.6 jit_solution(6521080387805725936)
XLA Ops:
  0.7 3.5 %msa.1 = (bf16[384,256]{1,0:T(8,128)(2,1)}, bf16[384,256]{1,0:T(8,128)(2,1)}) custom-call(bf16[12,256,256]{2,1,0:T(8,128)(2,1)} %bitcast.17, bf16[64,256]{1,0:T(8,128)(2,1)} %bitcast.20), custom_call_target="tpu_custom_call" | custom-call | flops 100000000 | bytes 2000000 | tf_op jit(solution)/shard_map/msa/pallas_call | solution.py:58
  4.1 7.7 %collective-permute-start = (bf16[384,256]{1,0:T(8,128)(2,1)}, bf16[384,256]{1,0:T(8,128)(2,1)S(1)}, u32[]{:S(2)}, u32[]{:S(2)}) collective-permute-start(bf16[384,256]{1,0:T(8,128)(2,1)} %get-tuple-element.22), channel_id=1, source_target_pairs={{2,0},{1,64},{0,128},{3,192},{6,4},{5,68},{4,132},{7,196},{10,8},{... | collective-permute-start | bytes 589832 | tf_op jit(solution)/shard_map/ppermute | solution.py:348
  11.9 0.8 copy.12
  13.9 1.9 %collective-permute-done.refs_0_ = bf16[384,256]{1,0:T(8,128)(2,1)S(1)} collective-permute-done((bf16[384,256]{1,0:T(8,128)(2,1)}, bf16[384,256]{1,0:T(8,128)(2,1)S(1)}, u32[]{:S(2)}, u32[]{:S(2)}) %collective-permute-start) | collective-permute-done | bytes 196640 | tf_op jit(solution)/shard_map/ppermute | solution.py:348
  15.8 2.9 %collective-permute-start.4 = (bf16[384,256]{1,0:T(8,128)(2,1)S(1)}, bf16[384,256]{1,0:T(8,128)(2,1)S(1)}, u32[]{:S(2)}, u32[]{:S(2)}) collective-permute-start(bf16[384,256]{1,0:T(8,128)(2,1)S(1)} %collective-permute-done.refs_0_), channel_id=1, source_target_pairs={{0,16},{8,24},{16,0},{24,8},{1,17},{9,25},{17,1},{25,9},{2,18},{10... | collective-permute-start | bytes 589832 | tf_op jit(solution)/shard_map/ppermute | solution.py:325
  18.7 5.9 %collective-permute-start.8 = (bf16[384,256]{1,0:T(8,128)(2,1)S(1)}, bf16[384,256]{1,0:T(8,128)(2,1)S(1)}, u32[]{:S(2)}, u32[]{:S(2)}) collective-permute-start(bf16[384,256]{1,0:T(8,128)(2,1)S(1)} %collective-permute-done.refs_0_), channel_id=1, source_target_pairs={{0,4},{4,0},{1,5},{5,1},{2,6},{6,2},{3,7},{7,3},{8,12},{12,8},{9,1... | collective-permute-start | bytes 589832 | tf_op jit(solution)/shard_map/ppermute | solution.py:329
  24.6 0.8 collective-permute-start.3
  25.4 0.7 collective-permute-start.2
  26.1 2.6 %collective-permute-start.12 = (bf16[384,256]{1,0:T(8,128)(2,1)S(1)}, bf16[384,256]{1,0:T(8,128)(2,1)S(1)}, u32[]{:S(2)}, u32[]{:S(2)}) collective-permute-start(bf16[384,256]{1,0:T(8,128)(2,1)S(1)} %collective-permute-done.4.refs_4_), channel_id=1, source_target_pairs={{0,4},{4,0},{1,5},{5,1},{2,6},{6,2},{3,7},{7,3},{8,12},{12,8},{9,1... | collective-permute-start | bytes 589832 | tf_op jit(solution)/shard_map/ppermute | solution.py:329
  28.7 3.0 %collective-permute-done.3.refs_3_ = bf16[384,256]{1,0:T(8,128)(2,1)S(1)} collective-permute-done((bf16[384,256]{1,0:T(8,128)(2,1)S(1)}, bf16[384,256]{1,0:T(8,128)(2,1)S(1)}, u32[]{:S(2)}, u32[]{:S(2)}) %collective-permute-start.3) | collective-permute-done | bytes 196640 | tf_op jit(solution)/shard_map/ppermute | solution.py:325
  31.7 1.5 %collective-permute-start.11 = (bf16[384,256]{1,0:T(8,128)(2,1)S(1)}, bf16[384,256]{1,0:T(8,128)(2,1)S(1)}, u32[]{:S(2)}, u32[]{:S(2)}) collective-permute-start(bf16[384,256]{1,0:T(8,128)(2,1)S(1)} %collective-permute-done.3.refs_3_), channel_id=1, source_target_pairs={{0,4},{4,0},{1,5},{5,1},{2,6},{6,2},{3,7},{7,3},{8,12},{12,8},{9,1... | collective-permute-start | bytes 589832 | tf_op jit(solution)/shard_map/ppermute | solution.py:329
  33.2 2.5 %collective-permute-start.6 = (bf16[384,256]{1,0:T(8,128)(2,1)S(1)}, bf16[384,256]{1,0:T(8,128)(2,1)S(1)}, u32[]{:S(2)}, u32[]{:S(2)}) collective-permute-start(bf16[384,256]{1,0:T(8,128)(2,1)S(1)} %collective-permute-done.1.refs_1_), channel_id=1, source_target_pairs={{0,24},{8,0},{16,8},{24,16},{1,25},{9,1},{17,9},{25,17},{2,26},{10... | collective-permute-start | bytes 589832 | tf_op jit(solution)/shard_map/ppermute | solution.py:326
  36.2 2.4 %collective-permute-start.9 = (bf16[384,256]{1,0:T(8,128)(2,1)S(1)}, bf16[384,256]{1,0:T(8,128)(2,1)S(1)}, u32[]{:S(2)}, u32[]{:S(2)}) collective-permute-start(bf16[384,256]{1,0:T(8,128)(2,1)S(1)} %collective-permute-done.1.refs_1_), channel_id=1, source_target_pairs={{0,4},{4,0},{1,5},{5,1},{2,6},{6,2},{3,7},{7,3},{8,12},{12,8},{9,1... | collective-permute-start | bytes 589832 | tf_op jit(solution)/shard_map/ppermute | solution.py:329
  38.8 1.7 %collective-permute-done.5.refs_5_ = bf16[384,256]{1,0:T(8,128)(2,1)S(1)} collective-permute-done((bf16[384,256]{1,0:T(8,128)(2,1)S(1)}, bf16[384,256]{1,0:T(8,128)(2,1)S(1)}, u32[]{:S(2)}, u32[]{:S(2)}) %collective-permute-start.5) | collective-permute-done | bytes 196640 | tf_op jit(solution)/shard_map/ppermute | solution.py:327
  40.4 1.4 %collective-permute-start.13 = (bf16[384,256]{1,0:T(8,128)(2,1)S(1)}, bf16[384,256]{1,0:T(8,128)(2,1)S(1)}, u32[]{:S(2)}, u32[]{:S(2)}) collective-permute-start(bf16[384,256]{1,0:T(8,128)(2,1)S(1)} %collective-permute-done.5.refs_5_), channel_id=1, source_target_pairs={{0,4},{4,0},{1,5},{5,1},{2,6},{6,2},{3,7},{7,3},{8,12},{12,8},{9,1... | collective-permute-start | bytes 589832 | tf_op jit(solution)/shard_map/ppermute | solution.py:329
  42.2 0.7 collective-permute-done.13.refs_13_
  44.0 9.2 %opm.1 = (bf16[12,192,128]{2,1,0:T(8,128)(2,1)}, bf16[12,192,128]{2,1,0:T(8,128)(2,1)}, bf16[48,256]{1,0:T(8,128)(2,1)}) custom-call(s32[6]{0:T(128)} %stack.42.pos_ref, bf16[384,256]{1,0:T(8,128)(2,1)} %get-tuple-element.24.lt_ref, bf16[384,256]{1,0:T(8,128)(2,1)} %copy-done.7, bf16[384,256]{1,0:T(8,128)(2,1)} %copy-done.12, bf16[384,256]{1,0:T(8,128)(2,1)} %copy-done.11, ...), custom_call_target="tpu_custom_call" | custom-call | flops 6000000000 | bytes 10000000 | tf_op jit(solution)/shard_map/opm/pallas_call | solution.py:174
  53.3 3.2 %collective-permute-start.17 = (bf16[12,192,128]{2,1,0:T(8,128)(2,1)}, bf16[12,192,128]{2,1,0:T(8,128)(2,1)S(1)}, u32[]{:S(2)}, u32[]{:S(2)}) collective-permute-start(bf16[12,192,128]{2,1,0:T(8,128)(2,1)} %get-tuple-element.29.own_ref), channel_id=1, source_target_pairs={{0,3},{1,0},{2,1},{3,2},{4,7},{5,4},{6,5},{7,6},{8,11},{9,8},{10,9... | collective-permute-start | bytes 1769480 | tf_op jit(solution)/shard_map/ppermute | solution.py:351
  57.0 1.4 %collective-permute-start.19 = (bf16[48,256]{1,0:T(8,128)(2,1)}, bf16[48,256]{1,0:T(8,128)(2,1)S(1)}, u32[]{:S(2)}, u32[]{:S(2)}) collective-permute-start(bf16[48,256]{1,0:T(8,128)(2,1)} %get-tuple-element.30), channel_id=1, source_target_pairs={{0,0},{1,64},{2,128},{3,192},{4,4},{5,68},{6,132},{7,196},{8,8},{9... | collective-permute-start | bytes 73736 | tf_op jit(solution)/shard_map/ppermute | solution.py:352
  58.3 13.0 %collective-permute-start.22 = (bf16[48,256]{1,0:T(8,128)(2,1)S(1)}, bf16[48,256]{1,0:T(8,128)(2,1)S(1)}, u32[]{:S(2)}, u32[]{:S(2)}) collective-permute-start(bf16[48,256]{1,0:T(8,128)(2,1)S(1)} %collective-permute-done.19), channel_id=1, source_target_pairs={{0,192},{64,0},{128,64},{192,128},{1,193},{65,1},{129,65},{193,129... | collective-permute-start | bytes 73736 | tf_op jit(solution)/shard_map/ppermute | solution.py:333
  71.3 1.8 %collective-permute-start.21 = (bf16[48,256]{1,0:T(8,128)(2,1)S(1)}, bf16[48,256]{1,0:T(8,128)(2,1)S(1)}, u32[]{:S(2)}, u32[]{:S(2)}) collective-permute-start(bf16[48,256]{1,0:T(8,128)(2,1)S(1)} %collective-permute-done.19), channel_id=1, source_target_pairs={{0,128},{64,192},{128,0},{192,64},{1,129},{65,193},{129,1},{193,65... | collective-permute-start | bytes 73736 | tf_op jit(solution)/shard_map/ppermute | solution.py:333
  73.1 2.4 %collective-permute-start.20 = (bf16[48,256]{1,0:T(8,128)(2,1)S(1)}, bf16[48,256]{1,0:T(8,128)(2,1)S(1)}, u32[]{:S(2)}, u32[]{:S(2)}) collective-permute-start(bf16[48,256]{1,0:T(8,128)(2,1)S(1)} %collective-permute-done.19), channel_id=1, source_target_pairs={{0,64},{64,128},{128,192},{192,0},{1,65},{65,129},{129,193},{193,1... | collective-permute-start | bytes 73736 | tf_op jit(solution)/shard_map/ppermute | solution.py:333
  75.5 2.5 %collective-permute-done.21 = bf16[48,256]{1,0:T(8,128)(2,1)S(1)} collective-permute-done((bf16[48,256]{1,0:T(8,128)(2,1)S(1)}, bf16[48,256]{1,0:T(8,128)(2,1)S(1)}, u32[]{:S(2)}, u32[]{:S(2)}) %collective-permute-start.21) | collective-permute-done | bytes 24608 | tf_op jit(solution)/shard_map/ppermute | solution.py:333
  78.2 5.2 %collective-permute-done.17.next_ref = bf16[12,192,128]{2,1,0:T(8,128)(2,1)S(1)} collective-permute-done((bf16[12,192,128]{2,1,0:T(8,128)(2,1)}, bf16[12,192,128]{2,1,0:T(8,128)(2,1)S(1)}, u32[]{:S(2)}, u32[]{:S(2)}) %collective-permute-start.17) | collective-permute-done | bytes 589856 | tf_op jit(solution)/shard_map/ppermute | solution.py:351
  83.5 1.0 broadcast_in_dim.2
  84.5 4.9 %all-to-all-start = ((bf16[8,4,48,256]{3,2,1,0:T(8,128)(2,1)}), bf16[8,4,48,256]{3,2,1,0:T(8,128)(2,1)S(1)}, u32[]{:S(2)}, u32[]{:S(2)}) async-start(bf16[8,4,48,256]{3,2,1,0:T(8,128)(2,1)} %broadcast_in_dim.2), calls=%async_computation | async-start | bytes 1572864 | tf_op jit(solution)/shard_map/all_to_all | solution.py:355
  89.4 5.9 %project.1 = (bf16[12,192,128]{2,1,0:T(8,128)(2,1)}, f32[12,192,128]{2,1,0:T(8,128)}, bf16[12,768,256]{2,1,0:T(8,128)(2,1)}) custom-call(bf16[12,192,128]{2,1,0:T(8,128)(2,1)} %get-tuple-element.29.own_ref, bf16[12,192,128]{2,1,0:T(8,128)(2,1)} %copy-done.6, bf16[12,192,128]{2,1,0:T(8,128)(2,1)} %copy-done.5, bf16[12,192,128]{2,1,0:T(8,128)(2,1)} %copy-done.4, ...), custom_call_target="tpu_custom_call" | custom-call | flops 10000000000 | bytes 20000000 | tf_op jit(solution)/shard_map/project/pallas_call | solution.py:212
  95.3 3.5 %all-to-all-done.pay0_ref = bf16[8,4,48,256]{3,2,1,0:T(8,128)(2,1)S(1)} async-done(((bf16[8,4,48,256]{3,2,1,0:T(8,128)(2,1)}), bf16[8,4,48,256]{3,2,1,0:T(8,128)(2,1)S(1)}, u32[]{:S(2)}, u32[]{:S(2)}) %all-to-all-start) | async-done | bytes 786464 | tf_op jit(solution)/shard_map/all_to_all | solution.py:355
  98.9 3.4 %collective-permute-start.23 = (bf16[8,4,48,256]{3,2,1,0:T(8,128)(2,1)S(1)}, bf16[8,4,48,256]{3,2,1,0:T(8,128)(2,1)S(1)}, u32[]{:S(2)}, u32[]{:S(2)}) collective-permute-start(bf16[8,4,48,256]{3,2,1,0:T(8,128)(2,1)S(1)} %all-to-all-done.pay0_ref), channel_id=1, source_target_pairs={{0,4},{4,0},{1,5},{5,1},{2,6},{6,2},{3,7},{7,3},{8,12},{12,8},{9,1... | collective-permute-start | bytes 2359304 | tf_op jit(solution)/shard_map/ppermute | solution.py:357
  102.3 1.9 %collective-permute-done.23.pay1_ref = bf16[8,4,48,256]{3,2,1,0:T(8,128)(2,1)S(1)} collective-permute-done((bf16[8,4,48,256]{3,2,1,0:T(8,128)(2,1)S(1)}, bf16[8,4,48,256]{3,2,1,0:T(8,128)(2,1)S(1)}, u32[]{:S(2)}, u32[]{:S(2)}) %collective-permute-start.23) | collective-permute-done | bytes 786464 | tf_op jit(solution)/shard_map/ppermute | solution.py:357
  104.2 0.9 copy-done.3
  105.2 18.4 %attend.1 = bf16[12,192,128]{2,1,0:T(8,128)(2,1)} custom-call(s32[6]{0:T(128)} %stack.42.pos_ref, s32[6,6]{1,0:T(8,128)} %filt_ref.1, bf16[12,192,128]{2,1,0:T(8,128)(2,1)} %get-tuple-element.38.q_ref, f32[12,192,128]{2,1,0:T(8,128)} %get-tuple-element.39.gate_ref, bf16[12,768,256]{2,1,0:T(8,128)(2,1)} %get-tuple-element.40.kv_ref, ...), custom_call_target="tpu_custom_call" | custom-call | flops 8000000000 | bytes 10000000 | tf_op jit(solution)/shard_map/attend/pallas_call | solution.py:297
  (73 shorter events, 3.9 us)
Async XLA Ops:
  0.6 11.3 %copy-start.1 = (bf16[1024,128]{1,0:T(8,128)(2,1)S(1)}, bf16[1024,128]{1,0:T(8,128)(2,1)}, u32[]{:S(2)}) copy-start(bf16[1024,128]{1,0:T(8,128)(2,1)} %param.11) | copy-start | bytes 786436
  0.6 12.1 %copy-start.2 = (f32[128,4]{0,1:T(4,128)S(1)}, f32[128,4]{0,1:T(4,128)}, u32[]{:S(2)}) copy-start(f32[128,4]{0,1:T(4,128)} %param.13) | copy-start | bytes 6148
  4.1 11.6 %collective-permute-start = (bf16[384,256]{1,0:T(8,128)(2,1)}, bf16[384,256]{1,0:T(8,128)(2,1)S(1)}, u32[]{:S(2)}, u32[]{:S(2)}) collective-permute-start(bf16[384,256]{1,0:T(8,128)(2,1)} %get-tuple-element.22), channel_id=1, source_target_pairs={{2,0},{1,64},{0,128},{3,192},{6,4},{5,68},{4,132},{7,196},{10,8},{... | collective-permute-start | bytes 589832 | tf_op jit(solution)/shard_map/ppermute | solution.py:348
  15.8 27.5 %copy-start.7 = (bf16[384,256]{1,0:T(8,128)(2,1)}, bf16[384,256]{1,0:T(8,128)(2,1)S(1)}, u32[]{:S(2)}) copy-start(bf16[384,256]{1,0:T(8,128)(2,1)S(1)} %collective-permute-done.refs_0_) | copy-start | bytes 589828
  15.8 10.3 %collective-permute-start.4 = (bf16[384,256]{1,0:T(8,128)(2,1)S(1)}, bf16[384,256]{1,0:T(8,128)(2,1)S(1)}, u32[]{:S(2)}, u32[]{:S(2)}) collective-permute-start(bf16[384,256]{1,0:T(8,128)(2,1)S(1)} %collective-permute-done.refs_0_), channel_id=1, source_target_pairs={{0,16},{8,24},{16,0},{24,8},{1,17},{9,25},{17,1},{25,9},{2,18},{10... | collective-permute-start | bytes 589832 | tf_op jit(solution)/shard_map/ppermute | solution.py:325
  18.7 10.0 %collective-permute-start.8 = (bf16[384,256]{1,0:T(8,128)(2,1)S(1)}, bf16[384,256]{1,0:T(8,128)(2,1)S(1)}, u32[]{:S(2)}, u32[]{:S(2)}) collective-permute-start(bf16[384,256]{1,0:T(8,128)(2,1)S(1)} %collective-permute-done.refs_0_), channel_id=1, source_target_pairs={{0,4},{4,0},{1,5},{5,1},{2,6},{6,2},{3,7},{7,3},{8,12},{12,8},{9,1... | collective-permute-start | bytes 589832 | tf_op jit(solution)/shard_map/ppermute | solution.py:329
  24.6 7.1 %collective-permute-start.3 = (bf16[384,256]{1,0:T(8,128)(2,1)S(1)}, bf16[384,256]{1,0:T(8,128)(2,1)S(1)}, u32[]{:S(2)}, u32[]{:S(2)}) collective-permute-start(bf16[384,256]{1,0:T(8,128)(2,1)S(1)} %collective-permute-done.refs_0_), channel_id=1, source_target_pairs={{0,24},{8,0},{16,8},{24,16},{1,25},{9,1},{17,9},{25,17},{2,26},{10... | collective-permute-start | bytes 589832 | tf_op jit(solution)/shard_map/ppermute | solution.py:325
  25.4 7.8 %collective-permute-start.2 = (bf16[384,256]{1,0:T(8,128)(2,1)S(1)}, bf16[384,256]{1,0:T(8,128)(2,1)S(1)}, u32[]{:S(2)}, u32[]{:S(2)}) collective-permute-start(bf16[384,256]{1,0:T(8,128)(2,1)S(1)} %collective-permute-done.refs_0_), channel_id=1, source_target_pairs={{0,8},{8,16},{16,24},{24,0},{1,9},{9,17},{17,25},{25,1},{2,10},{10... | collective-permute-start | bytes 589832 | tf_op jit(solution)/shard_map/ppermute | solution.py:325
  26.1 7.1 %collective-permute-start.1 = (bf16[384,256]{1,0:T(8,128)(2,1)S(1)}, bf16[384,256]{1,0:T(8,128)(2,1)S(1)}, u32[]{:S(2)}, u32[]{:S(2)}) collective-permute-start(bf16[384,256]{1,0:T(8,128)(2,1)S(1)} %collective-permute-done.refs_0_), channel_id=1, source_target_pairs={{0,32},{32,0},{1,33},{33,1},{2,34},{34,2},{3,35},{35,3},{4,36},{36... | collective-permute-start | bytes 589832 | tf_op jit(solution)/shard_map/ppermute | solution.py:324
  26.1 17.2 %copy-start.8 = (bf16[384,256]{1,0:T(8,128)(2,1)}, bf16[384,256]{1,0:T(8,128)(2,1)S(1)}, u32[]{:S(2)}) copy-start(bf16[384,256]{1,0:T(8,128)(2,1)S(1)} %collective-permute-done.4.refs_4_) | copy-start | bytes 589828
  26.1 9.6 %collective-permute-start.12 = (bf16[384,256]{1,0:T(8,128)(2,1)S(1)}, bf16[384,256]{1,0:T(8,128)(2,1)S(1)}, u32[]{:S(2)}, u32[]{:S(2)}) collective-permute-start(bf16[384,256]{1,0:T(8,128)(2,1)S(1)} %collective-permute-done.4.refs_4_), channel_id=1, source_target_pairs={{0,4},{4,0},{1,5},{5,1},{2,6},{6,2},{3,7},{7,3},{8,12},{12,8},{9,1... | collective-permute-start | bytes 589832 | tf_op jit(solution)/shard_map/ppermute | solution.py:329
  28.7 14.6 %copy-start.9 = (bf16[384,256]{1,0:T(8,128)(2,1)}, bf16[384,256]{1,0:T(8,128)(2,1)S(1)}, u32[]{:S(2)}) copy-start(bf16[384,256]{1,0:T(8,128)(2,1)S(1)} %collective-permute-done.8.refs_8_) | copy-start | bytes 589828
  28.7 7.5 %collective-permute-start.7 = (bf16[384,256]{1,0:T(8,128)(2,1)S(1)}, bf16[384,256]{1,0:T(8,128)(2,1)S(1)}, u32[]{:S(2)}, u32[]{:S(2)}) collective-permute-start(bf16[384,256]{1,0:T(8,128)(2,1)S(1)} %collective-permute-done.4.refs_4_), channel_id=1, source_target_pairs={{0,32},{32,0},{1,33},{33,1},{2,34},{34,2},{3,35},{35,3},{4,36},{36... | collective-permute-start | bytes 589832 | tf_op jit(solution)/shard_map/ppermute | solution.py:327
  31.7 11.6 %copy-start.10 = (bf16[384,256]{1,0:T(8,128)(2,1)}, bf16[384,256]{1,0:T(8,128)(2,1)S(1)}, u32[]{:S(2)}) copy-start(bf16[384,256]{1,0:T(8,128)(2,1)S(1)} %collective-permute-done.3.refs_3_) | copy-start | bytes 589828
  31.7 6.9 %collective-permute-start.11 = (bf16[384,256]{1,0:T(8,128)(2,1)S(1)}, bf16[384,256]{1,0:T(8,128)(2,1)S(1)}, u32[]{:S(2)}, u32[]{:S(2)}) collective-permute-start(bf16[384,256]{1,0:T(8,128)(2,1)S(1)} %collective-permute-done.3.refs_3_), channel_id=1, source_target_pairs={{0,4},{4,0},{1,5},{5,1},{2,6},{6,2},{3,7},{7,3},{8,12},{12,8},{9,1... | collective-permute-start | bytes 589832 | tf_op jit(solution)/shard_map/ppermute | solution.py:329
  33.2 7.2 %collective-permute-start.5 = (bf16[384,256]{1,0:T(8,128)(2,1)S(1)}, bf16[384,256]{1,0:T(8,128)(2,1)S(1)}, u32[]{:S(2)}, u32[]{:S(2)}) collective-permute-start(bf16[384,256]{1,0:T(8,128)(2,1)S(1)} %collective-permute-done.2.refs_2_), channel_id=1, source_target_pairs={{0,32},{32,0},{1,33},{33,1},{2,34},{34,2},{3,35},{35,3},{4,36},{36... | collective-permute-start | bytes 589832 | tf_op jit(solution)/shard_map/ppermute | solution.py:327
  33.2 8.6 %collective-permute-start.6 = (bf16[384,256]{1,0:T(8,128)(2,1)S(1)}, bf16[384,256]{1,0:T(8,128)(2,1)S(1)}, u32[]{:S(2)}, u32[]{:S(2)}) collective-permute-start(bf16[384,256]{1,0:T(8,128)(2,1)S(1)} %collective-permute-done.1.refs_1_), channel_id=1, source_target_pairs={{0,24},{8,0},{16,8},{24,16},{1,25},{9,1},{17,9},{25,17},{2,26},{10... | collective-permute-start | bytes 589832 | tf_op jit(solution)/shard_map/ppermute | solution.py:326
  35.7 6.4 %collective-permute-start.10 = (bf16[384,256]{1,0:T(8,128)(2,1)S(1)}, bf16[384,256]{1,0:T(8,128)(2,1)S(1)}, u32[]{:S(2)}, u32[]{:S(2)}) collective-permute-start(bf16[384,256]{1,0:T(8,128)(2,1)S(1)} %collective-permute-done.2.refs_2_), channel_id=1, source_target_pairs={{0,4},{4,0},{1,5},{5,1},{2,6},{6,2},{3,7},{7,3},{8,12},{12,8},{9,1... | collective-permute-start | bytes 589832 | tf_op jit(solution)/shard_map/ppermute | solution.py:329
  36.2 5.9 %collective-permute-start.9 = (bf16[384,256]{1,0:T(8,128)(2,1)S(1)}, bf16[384,256]{1,0:T(8,128)(2,1)S(1)}, u32[]{:S(2)}, u32[]{:S(2)}) collective-permute-start(bf16[384,256]{1,0:T(8,128)(2,1)S(1)} %collective-permute-done.1.refs_1_), channel_id=1, source_target_pairs={{0,4},{4,0},{1,5},{5,1},{2,6},{6,2},{3,7},{7,3},{8,12},{12,8},{9,1... | collective-permute-start | bytes 589832 | tf_op jit(solution)/shard_map/ppermute | solution.py:329
  38.7 3.5 %collective-permute-start.15 = (bf16[384,256]{1,0:T(8,128)(2,1)S(1)}, bf16[384,256]{1,0:T(8,128)(2,1)S(1)}, u32[]{:S(2)}, u32[]{:S(2)}) collective-permute-start(bf16[384,256]{1,0:T(8,128)(2,1)S(1)} %collective-permute-done.7.refs_7_), channel_id=1, source_target_pairs={{0,4},{4,0},{1,5},{5,1},{2,6},{6,2},{3,7},{7,3},{8,12},{12,8},{9,1... | collective-permute-start | bytes 589832 | tf_op jit(solution)/shard_map/ppermute | solution.py:329
  40.4 2.5 %collective-permute-start.13 = (bf16[384,256]{1,0:T(8,128)(2,1)S(1)}, bf16[384,256]{1,0:T(8,128)(2,1)S(1)}, u32[]{:S(2)}, u32[]{:S(2)}) collective-permute-start(bf16[384,256]{1,0:T(8,128)(2,1)S(1)} %collective-permute-done.5.refs_5_), channel_id=1, source_target_pairs={{0,4},{4,0},{1,5},{5,1},{2,6},{6,2},{3,7},{7,3},{8,12},{12,8},{9,1... | collective-permute-start | bytes 589832 | tf_op jit(solution)/shard_map/ppermute | solution.py:329
  41.9 1.4 %collective-permute-start.14 = (bf16[384,256]{1,0:T(8,128)(2,1)S(1)}, bf16[384,256]{1,0:T(8,128)(2,1)S(1)}, u32[]{:S(2)}, u32[]{:S(2)}) collective-permute-start(bf16[384,256]{1,0:T(8,128)(2,1)S(1)} %collective-permute-done.6.refs_6_), channel_id=1, source_target_pairs={{0,4},{4,0},{1,5},{5,1},{2,6},{6,2},{3,7},{7,3},{8,12},{12,8},{9,1... | collective-permute-start | bytes 589832 | tf_op jit(solution)/shard_map/ppermute | solution.py:329
  53.2 25.0 %collective-permute-start.18 = (bf16[12,192,128]{2,1,0:T(8,128)(2,1)}, bf16[12,192,128]{2,1,0:T(8,128)(2,1)S(1)}, u32[]{:S(2)}, u32[]{:S(2)}) collective-permute-start(bf16[12,192,128]{2,1,0:T(8,128)(2,1)} %get-tuple-element.29.own_ref), channel_id=1, source_target_pairs={{0,2},{1,3},{2,0},{3,1},{4,6},{5,7},{6,4},{7,5},{8,10},{9,11},{10,... | collective-permute-start | bytes 1769480 | tf_op jit(solution)/shard_map/ppermute | solution.py:351
  53.3 30.2 %collective-permute-start.17 = (bf16[12,192,128]{2,1,0:T(8,128)(2,1)}, bf16[12,192,128]{2,1,0:T(8,128)(2,1)S(1)}, u32[]{:S(2)}, u32[]{:S(2)}) collective-permute-start(bf16[12,192,128]{2,1,0:T(8,128)(2,1)} %get-tuple-element.29.own_ref), channel_id=1, source_target_pairs={{0,3},{1,0},{2,1},{3,2},{4,7},{5,4},{6,5},{7,6},{8,11},{9,8},{10,9... | collective-permute-start | bytes 1769480 | tf_op jit(solution)/shard_map/ppermute | solution.py:351
  56.5 27.0 %collective-permute-start.16 = (bf16[12,192,128]{2,1,0:T(8,128)(2,1)}, bf16[12,192,128]{2,1,0:T(8,128)(2,1)S(1)}, u32[]{:S(2)}, u32[]{:S(2)}) collective-permute-start(bf16[12,192,128]{2,1,0:T(8,128)(2,1)} %get-tuple-element.29.own_ref), channel_id=1, source_target_pairs={{0,1},{1,2},{2,3},{3,0},{4,5},{5,6},{6,7},{7,4},{8,9},{9,10},{10,1... | collective-permute-start | bytes 1769480 | tf_op jit(solution)/shard_map/ppermute | solution.py:351
  57.0 1.4 %collective-permute-start.19 = (bf16[48,256]{1,0:T(8,128)(2,1)}, bf16[48,256]{1,0:T(8,128)(2,1)S(1)}, u32[]{:S(2)}, u32[]{:S(2)}) collective-permute-start(bf16[48,256]{1,0:T(8,128)(2,1)} %get-tuple-element.30), channel_id=1, source_target_pairs={{0,0},{1,64},{2,128},{3,192},{4,4},{5,68},{6,132},{7,196},{8,8},{9... | collective-permute-start | bytes 73736 | tf_op jit(solution)/shard_map/ppermute | solution.py:352
  58.3 14.8 %collective-permute-start.22 = (bf16[48,256]{1,0:T(8,128)(2,1)S(1)}, bf16[48,256]{1,0:T(8,128)(2,1)S(1)}, u32[]{:S(2)}, u32[]{:S(2)}) collective-permute-start(bf16[48,256]{1,0:T(8,128)(2,1)S(1)} %collective-permute-done.19), channel_id=1, source_target_pairs={{0,192},{64,0},{128,64},{192,128},{1,193},{65,1},{129,65},{193,129... | collective-permute-start | bytes 73736 | tf_op jit(solution)/shard_map/ppermute | solution.py:333
  71.3 6.7 %collective-permute-start.21 = (bf16[48,256]{1,0:T(8,128)(2,1)S(1)}, bf16[48,256]{1,0:T(8,128)(2,1)S(1)}, u32[]{:S(2)}, u32[]{:S(2)}) collective-permute-start(bf16[48,256]{1,0:T(8,128)(2,1)S(1)} %collective-permute-done.19), channel_id=1, source_target_pairs={{0,128},{64,192},{128,0},{192,64},{1,129},{65,193},{129,1},{193,65... | collective-permute-start | bytes 73736 | tf_op jit(solution)/shard_map/ppermute | solution.py:333
  73.1 5.1 %collective-permute-start.20 = (bf16[48,256]{1,0:T(8,128)(2,1)S(1)}, bf16[48,256]{1,0:T(8,128)(2,1)S(1)}, u32[]{:S(2)}, u32[]{:S(2)}) collective-permute-start(bf16[48,256]{1,0:T(8,128)(2,1)S(1)} %collective-permute-done.19), channel_id=1, source_target_pairs={{0,64},{64,128},{128,192},{192,0},{1,65},{65,129},{129,193},{193,1... | collective-permute-start | bytes 73736 | tf_op jit(solution)/shard_map/ppermute | solution.py:333
  78.2 11.1 %copy-start.4 = (bf16[12,192,128]{2,1,0:T(8,128)(2,1)}, bf16[12,192,128]{2,1,0:T(8,128)(2,1)S(1)}, u32[]{:S(2)}) copy-start(bf16[12,192,128]{2,1,0:T(8,128)(2,1)S(1)} %collective-permute-done.18.far_ref) | copy-start | bytes 1769476
  84.5 14.4 %all-to-all-start = ((bf16[8,4,48,256]{3,2,1,0:T(8,128)(2,1)}), bf16[8,4,48,256]{3,2,1,0:T(8,128)(2,1)S(1)}, u32[]{:S(2)}, u32[]{:S(2)}) async-start(bf16[8,4,48,256]{3,2,1,0:T(8,128)(2,1)} %broadcast_in_dim.2), calls=%async_computation | async-start | bytes 1572864 | tf_op jit(solution)/shard_map/all_to_all | solution.py:355
  98.9 5.3 %collective-permute-start.23 = (bf16[8,4,48,256]{3,2,1,0:T(8,128)(2,1)S(1)}, bf16[8,4,48,256]{3,2,1,0:T(8,128)(2,1)S(1)}, u32[]{:S(2)}, u32[]{:S(2)}) collective-permute-start(bf16[8,4,48,256]{3,2,1,0:T(8,128)(2,1)S(1)} %all-to-all-done.pay0_ref), channel_id=1, source_target_pairs={{0,4},{4,0},{1,5},{5,1},{2,6},{6,2},{3,7},{7,3},{8,12},{12,8},{9,1... | collective-permute-start | bytes 2359304 | tf_op jit(solution)/shard_map/ppermute | solution.py:357
  (16 other events, 67.4 us)

commit v5 on v4

--- a/solution.py
+++ b/solution.py
@@ -348,8 +348,10 @@
     right, w, off, pos = lax.optimization_barrier((pp(right, ALL, SPREAD), *prepared))
     mid, norm, bias = opm(pos, left, gather_right(right), w, emb, off)
 
-    prev, nxt, far = [pp(norm, "x", ring(4, k)) for k in (1, 3, 2)]
-    col = gather_bias_z(pp(bias, ALL, SWAP))
+    prev, nxt = pp(norm, "x", ring(4, 1)), pp(norm, "x", ring(4, 3))
+    bias, own = lax.optimization_barrier((pp(bias, ALL, SWAP), norm))
+    far = pp(own, "x", ring(4, 2))
+    col = gather_bias_z(bias)
     prev, nxt, far, col = lax.optimization_barrier((prev, nxt, far, col))
     q, gate, kv = project(norm, prev, nxt, far, qkg)
     pay0 = lax.all_to_all(col, ("zl", "y"), 0, 0, tiled=True)

time: 124 us -> 131 us (1.056)
  waiting for transfers between devices: 21.2 us -> 30 us
  starting transfers between devices: 59.8 us -> 58 us
    ppermute x4, waiting for transfers between devices: 5.25 us -> 15.3 us  [the longest x2 12.7 us: body(): prev, nxt = (pp(norm, 'x', ring(4, 1)), pp(norm, 'x', ring(4, 3)))]
    ppermute x3, starting transfers between devices: 17.1 us -> 7.45 us  [gather_bias_z(): lax.ppermute(own, 'zh', ring(4, k))]
    ppermute x4, starting transfers between devices: 5.15 us -> 12.2 us  [the longest x2 8.52 us: body(): prev, nxt = (pp(norm, 'x', ring(4, 1)), pp(norm, 'x', ring(4, 3)))]
    ppermute x1, starting transfers between devices: 3.42 us -> 4.94 us  [body(): pay1 = pp(pay0, 'c', ring(2, 1))]
  transfers between devices with their start and end apart: 25 -> 25, of which waited for: 11 -> 12; matrix products, arithmetic and copies ran while one was open for 2% -> 2% of each run, Pallas kernels for 5% -> 5%
where the time goes in v5:
time: 131 us
  starting transfers between devices  58 us (44%)
  Pallas kernels  37.1 us (28%)
  waiting for transfers between devices  30 us (23%)
  local copies, waits for them, and re-layouts  4.61 us (4%)
    pallas_call x1, Pallas kernels, attend(): pl.pallas_call(attend_kernel, grid=(ROWS // AT_ROWS,), out_shape=jax.Shap...  18.4 us
    ppermute x8, starting transfers between devices, gather_right(): return mine + [pp(m, 'c', ring(2, 1)) for m in mine]  14.6 us
    ppermute x2, waiting for transfers between devices, body(): prev, nxt = (pp(norm, 'x', ring(4, 1)), pp(norm, 'x', ring(4, 3)))  12.7 us
    pallas_call x1, Pallas kernels, opm(): pl.pallas_call(opm_kernel, out_shape=(jax.ShapeDtypeStruct((ROWS, COLS, C...  9.21 us
    ppermute x2, starting transfers between devices, body(): prev, nxt = (pp(norm, 'x', ring(4, 1)), pp(norm, 'x', ring(4, 3)))  8.52 us
    ppermute x1, starting transfers between devices, body(): pp(right, ALL, SPREAD)  7.74 us
    ppermute x3, starting transfers between devices, gather_bias_z(): lax.ppermute(own, 'zh', ring(4, k))  7.45 us
    pallas_call x1, Pallas kernels, project(): pl.pallas_call(project_kernel, grid=(ROWS // PR_ROWS,), out_shape=(jax.Sh...  5.95 us
  transfers between devices with their start and end apart: 25, of which 12 were waited for; matrix products, arithmetic and copies ran while one was open for 2% of the time, Pallas kernels for 5%

profile of v5, /device:TPU:1, one launch (start us, length us, event | category | flops | bytes accessed | tf_op | source)
XLA Modules:
  0.0 130.6 jit_solution(18416192455770723684)
XLA Ops:
  0.7 3.5 %msa.1 = (bf16[384,256]{1,0:T(8,128)(2,1)}, bf16[384,256]{1,0:T(8,128)(2,1)}) custom-call(bf16[12,256,256]{2,1,0:T(8,128)(2,1)} %bitcast.17, bf16[64,256]{1,0:T(8,128)(2,1)} %bitcast.20), custom_call_target="tpu_custom_call" | custom-call | flops 100000000 | bytes 2000000 | tf_op jit(solution)/shard_map/msa/pallas_call | solution.py:58
  4.1 7.7 %collective-permute-start = (bf16[384,256]{1,0:T(8,128)(2,1)}, bf16[384,256]{1,0:T(8,128)(2,1)S(1)}, u32[]{:S(2)}, u32[]{:S(2)}) collective-permute-start(bf16[384,256]{1,0:T(8,128)(2,1)} %get-tuple-element.24), channel_id=1, source_target_pairs={{2,0},{1,64},{0,128},{3,192},{6,4},{5,68},{4,132},{7,196},{10,8},{... | collective-permute-start | bytes 589832 | tf_op jit(solution)/shard_map/ppermute | solution.py:348
  11.9 0.8 copy.12
  13.9 1.9 %collective-permute-done.refs_0_ = bf16[384,256]{1,0:T(8,128)(2,1)S(1)} collective-permute-done((bf16[384,256]{1,0:T(8,128)(2,1)}, bf16[384,256]{1,0:T(8,128)(2,1)S(1)}, u32[]{:S(2)}, u32[]{:S(2)}) %collective-permute-start) | collective-permute-done | bytes 196640 | tf_op jit(solution)/shard_map/ppermute | solution.py:348
  15.8 2.9 %collective-permute-start.4 = (bf16[384,256]{1,0:T(8,128)(2,1)S(1)}, bf16[384,256]{1,0:T(8,128)(2,1)S(1)}, u32[]{:S(2)}, u32[]{:S(2)}) collective-permute-start(bf16[384,256]{1,0:T(8,128)(2,1)S(1)} %collective-permute-done.refs_0_), channel_id=1, source_target_pairs={{0,16},{8,24},{16,0},{24,8},{1,17},{9,25},{17,1},{25,9},{2,18},{10... | collective-permute-start | bytes 589832 | tf_op jit(solution)/shard_map/ppermute | solution.py:325
  18.7 5.9 %collective-permute-start.8 = (bf16[384,256]{1,0:T(8,128)(2,1)S(1)}, bf16[384,256]{1,0:T(8,128)(2,1)S(1)}, u32[]{:S(2)}, u32[]{:S(2)}) collective-permute-start(bf16[384,256]{1,0:T(8,128)(2,1)S(1)} %collective-permute-done.refs_0_), channel_id=1, source_target_pairs={{0,4},{4,0},{1,5},{5,1},{2,6},{6,2},{3,7},{7,3},{8,12},{12,8},{9,1... | collective-permute-start | bytes 589832 | tf_op jit(solution)/shard_map/ppermute | solution.py:329
  26.1 2.6 %collective-permute-start.12 = (bf16[384,256]{1,0:T(8,128)(2,1)S(1)}, bf16[384,256]{1,0:T(8,128)(2,1)S(1)}, u32[]{:S(2)}, u32[]{:S(2)}) collective-permute-start(bf16[384,256]{1,0:T(8,128)(2,1)S(1)} %collective-permute-done.4.refs_4_), channel_id=1, source_target_pairs={{0,4},{4,0},{1,5},{5,1},{2,6},{6,2},{3,7},{7,3},{8,12},{12,8},{9,1... | collective-permute-start | bytes 589832 | tf_op jit(solution)/shard_map/ppermute | solution.py:329
  28.7 3.0 %collective-permute-done.3.refs_3_ = bf16[384,256]{1,0:T(8,128)(2,1)S(1)} collective-permute-done((bf16[384,256]{1,0:T(8,128)(2,1)S(1)}, bf16[384,256]{1,0:T(8,128)(2,1)S(1)}, u32[]{:S(2)}, u32[]{:S(2)}) %collective-permute-start.3) | collective-permute-done | bytes 196640 | tf_op jit(solution)/shard_map/ppermute | solution.py:325
  31.7 1.5 %collective-permute-start.11 = (bf16[384,256]{1,0:T(8,128)(2,1)S(1)}, bf16[384,256]{1,0:T(8,128)(2,1)S(1)}, u32[]{:S(2)}, u32[]{:S(2)}) collective-permute-start(bf16[384,256]{1,0:T(8,128)(2,1)S(1)} %collective-permute-done.3.refs_3_), channel_id=1, source_target_pairs={{0,4},{4,0},{1,5},{5,1},{2,6},{6,2},{3,7},{7,3},{8,12},{12,8},{9,1... | collective-permute-start | bytes 589832 | tf_op jit(solution)/shard_map/ppermute | solution.py:329
  33.2 2.5 %collective-permute-start.6 = (bf16[384,256]{1,0:T(8,128)(2,1)S(1)}, bf16[384,256]{1,0:T(8,128)(2,1)S(1)}, u32[]{:S(2)}, u32[]{:S(2)}) collective-permute-start(bf16[384,256]{1,0:T(8,128)(2,1)S(1)} %collective-permute-done.1.refs_1_), channel_id=1, source_target_pairs={{0,24},{8,0},{16,8},{24,16},{1,25},{9,1},{17,9},{25,17},{2,26},{10... | collective-permute-start | bytes 589832 | tf_op jit(solution)/shard_map/ppermute | solution.py:326
  36.2 2.4 %collective-permute-start.9 = (bf16[384,256]{1,0:T(8,128)(2,1)S(1)}, bf16[384,256]{1,0:T(8,128)(2,1)S(1)}, u32[]{:S(2)}, u32[]{:S(2)}) collective-permute-start(bf16[384,256]{1,0:T(8,128)(2,1)S(1)} %collective-permute-done.1.refs_1_), channel_id=1, source_target_pairs={{0,4},{4,0},{1,5},{5,1},{2,6},{6,2},{3,7},{7,3},{8,12},{12,8},{9,1... | collective-permute-start | bytes 589832 | tf_op jit(solution)/shard_map/ppermute | solution.py:329
  38.8 1.7 %collective-permute-done.5.refs_5_ = bf16[384,256]{1,0:T(8,128)(2,1)S(1)} collective-permute-done((bf16[384,256]{1,0:T(8,128)(2,1)S(1)}, bf16[384,256]{1,0:T(8,128)(2,1)S(1)}, u32[]{:S(2)}, u32[]{:S(2)}) %collective-permute-start.5) | collective-permute-done | bytes 196640 | tf_op jit(solution)/shard_map/ppermute | solution.py:327
  40.4 1.4 %collective-permute-start.13 = (bf16[384,256]{1,0:T(8,128)(2,1)S(1)}, bf16[384,256]{1,0:T(8,128)(2,1)S(1)}, u32[]{:S(2)}, u32[]{:S(2)}) collective-permute-start(bf16[384,256]{1,0:T(8,128)(2,1)S(1)} %collective-permute-done.5.refs_5_), channel_id=1, source_target_pairs={{0,4},{4,0},{1,5},{5,1},{2,6},{6,2},{3,7},{7,3},{8,12},{12,8},{9,1... | collective-permute-start | bytes 589832 | tf_op jit(solution)/shard_map/ppermute | solution.py:329
  44.0 9.2 %opm.1 = (bf16[12,192,128]{2,1,0:T(8,128)(2,1)}, bf16[12,192,128]{2,1,0:T(8,128)(2,1)}, bf16[48,256]{1,0:T(8,128)(2,1)}) custom-call(s32[6]{0:T(128)} %stack.42.pos_ref, bf16[384,256]{1,0:T(8,128)(2,1)} %get-tuple-element.26.lt_ref, bf16[384,256]{1,0:T(8,128)(2,1)} %copy-done.7, bf16[384,256]{1,0:T(8,128)(2,1)} %copy-done.12, bf16[384,256]{1,0:T(8,128)(2,1)} %copy-done.11, ...), custom_call_target="tpu_custom_call" | custom-call | flops 6000000000 | bytes 10000000 | tf_op jit(solution)/shard_map/opm/pallas_call | solution.py:174
  53.2 1.4 %collective-permute-start.18 = (bf16[48,256]{1,0:T(8,128)(2,1)}, bf16[48,256]{1,0:T(8,128)(2,1)S(1)}, u32[]{:S(2)}, u32[]{:S(2)}) collective-permute-start(bf16[48,256]{1,0:T(8,128)(2,1)} %get-tuple-element.32), channel_id=1, source_target_pairs={{0,0},{1,64},{2,128},{3,192},{4,4},{5,68},{6,132},{7,196},{8,8},{9... | collective-permute-start | bytes 73736 | tf_op jit(solution)/shard_map/ppermute | solution.py:352
  54.6 8.5 %collective-permute-start.17 = (bf16[12,192,128]{2,1,0:T(8,128)(2,1)}, bf16[12,192,128]{2,1,0:T(8,128)(2,1)S(1)}, u32[]{:S(2)}, u32[]{:S(2)}) collective-permute-start(bf16[12,192,128]{2,1,0:T(8,128)(2,1)} %get-tuple-element.33.own_ref), channel_id=1, source_target_pairs={{0,3},{1,0},{2,1},{3,2},{4,7},{5,4},{6,5},{7,6},{8,11},{9,8},{10,9... | collective-permute-start | bytes 1769480 | tf_op jit(solution)/shard_map/ppermute | solution.py:351
  63.1 2.2 %collective-permute-start.19 = (bf16[12,192,128]{2,1,0:T(8,128)(2,1)}, bf16[12,192,128]{2,1,0:T(8,128)(2,1)S(1)}, u32[]{:S(2)}, u32[]{:S(2)}) collective-permute-start(bf16[12,192,128]{2,1,0:T(8,128)(2,1)} %get-tuple-element.33.own_ref), channel_id=1, source_target_pairs={{0,2},{1,3},{2,0},{3,1},{4,6},{5,7},{6,4},{7,5},{8,10},{9,11},{10,... | collective-permute-start | bytes 1769480 | tf_op jit(solution)/shard_map/ppermute | solution.py:353
  65.3 2.5 %collective-permute-start.22 = (bf16[48,256]{1,0:T(8,128)(2,1)S(1)}, bf16[48,256]{1,0:T(8,128)(2,1)S(1)}, u32[]{:S(2)}, u32[]{:S(2)}) collective-permute-start(bf16[48,256]{1,0:T(8,128)(2,1)S(1)} %collective-permute-done.18), channel_id=1, source_target_pairs={{0,192},{64,0},{128,64},{192,128},{1,193},{65,1},{129,65},{193,129... | collective-permute-start | bytes 73736 | tf_op jit(solution)/shard_map/ppermute | solution.py:333
  67.8 2.6 %collective-permute-start.21 = (bf16[48,256]{1,0:T(8,128)(2,1)S(1)}, bf16[48,256]{1,0:T(8,128)(2,1)S(1)}, u32[]{:S(2)}, u32[]{:S(2)}) collective-permute-start(bf16[48,256]{1,0:T(8,128)(2,1)S(1)} %collective-permute-done.18), channel_id=1, source_target_pairs={{0,128},{64,192},{128,0},{192,64},{1,129},{65,193},{129,1},{193,65... | collective-permute-start | bytes 73736 | tf_op jit(solution)/shard_map/ppermute | solution.py:333
  70.4 2.4 %collective-permute-start.20 = (bf16[48,256]{1,0:T(8,128)(2,1)S(1)}, bf16[48,256]{1,0:T(8,128)(2,1)S(1)}, u32[]{:S(2)}, u32[]{:S(2)}) collective-permute-start(bf16[48,256]{1,0:T(8,128)(2,1)S(1)} %collective-permute-done.18), channel_id=1, source_target_pairs={{0,64},{64,128},{128,192},{192,0},{1,65},{65,129},{129,193},{193,1... | collective-permute-start | bytes 73736 | tf_op jit(solution)/shard_map/ppermute | solution.py:333
  72.8 1.7 %collective-permute-done.21 = bf16[48,256]{1,0:T(8,128)(2,1)S(1)} collective-permute-done((bf16[48,256]{1,0:T(8,128)(2,1)S(1)}, bf16[48,256]{1,0:T(8,128)(2,1)S(1)}, u32[]{:S(2)}, u32[]{:S(2)}) %collective-permute-start.21) | collective-permute-done | bytes 24608 | tf_op jit(solution)/shard_map/ppermute | solution.py:333
  74.5 1.0 collective-permute-done.20
  75.5 12.7 %collective-permute-done.17.next_ref = bf16[12,192,128]{2,1,0:T(8,128)(2,1)S(1)} collective-permute-done((bf16[12,192,128]{2,1,0:T(8,128)(2,1)}, bf16[12,192,128]{2,1,0:T(8,128)(2,1)S(1)}, u32[]{:S(2)}, u32[]{:S(2)}) %collective-permute-start.17) | collective-permute-done | bytes 589856 | tf_op jit(solution)/shard_map/ppermute | solution.py:351
  88.2 2.6 %collective-permute-done.19.far_ref = bf16[12,192,128]{2,1,0:T(8,128)(2,1)S(1)} collective-permute-done((bf16[12,192,128]{2,1,0:T(8,128)(2,1)}, bf16[12,192,128]{2,1,0:T(8,128)(2,1)S(1)}, u32[]{:S(2)}, u32[]{:S(2)}) %collective-permute-start.19) | collective-permute-done | bytes 589856 | tf_op jit(solution)/shard_map/ppermute | solution.py:353
  90.8 1.0 broadcast_in_dim.2
  91.8 4.3 %all-to-all-start = ((bf16[8,4,48,256]{3,2,1,0:T(8,128)(2,1)}), bf16[8,4,48,256]{3,2,1,0:T(8,128)(2,1)S(1)}, u32[]{:S(2)}, u32[]{:S(2)}) async-start(bf16[8,4,48,256]{3,2,1,0:T(8,128)(2,1)} %broadcast_in_dim.2), calls=%async_computation | async-start | bytes 1572864 | tf_op jit(solution)/shard_map/all_to_all | solution.py:357
  96.1 5.9 %project.1 = (bf16[12,192,128]{2,1,0:T(8,128)(2,1)}, f32[12,192,128]{2,1,0:T(8,128)}, bf16[12,768,256]{2,1,0:T(8,128)(2,1)}) custom-call(bf16[12,192,128]{2,1,0:T(8,128)(2,1)} %get-tuple-element.33.own_ref, bf16[12,192,128]{2,1,0:T(8,128)(2,1)} %copy-done.5, bf16[12,192,128]{2,1,0:T(8,128)(2,1)} %copy-done.4, bf16[12,192,128]{2,1,0:T(8,128)(2,1)} %copy-done.6, ...), custom_call_target="tpu_custom_call" | custom-call | flops 10000000000 | bytes 20000000 | tf_op jit(solution)/shard_map/project/pallas_call | solution.py:212
  102.0 2.4 %all-to-all-done.pay0_ref = bf16[8,4,48,256]{3,2,1,0:T(8,128)(2,1)S(1)} async-done(((bf16[8,4,48,256]{3,2,1,0:T(8,128)(2,1)}), bf16[8,4,48,256]{3,2,1,0:T(8,128)(2,1)S(1)}, u32[]{:S(2)}, u32[]{:S(2)}) %all-to-all-start) | async-done | bytes 786464 | tf_op jit(solution)/shard_map/all_to_all | solution.py:357
  104.4 4.9 %collective-permute-start.23 = (bf16[8,4,48,256]{3,2,1,0:T(8,128)(2,1)S(1)}, bf16[8,4,48,256]{3,2,1,0:T(8,128)(2,1)S(1)}, u32[]{:S(2)}, u32[]{:S(2)}) collective-permute-start(bf16[8,4,48,256]{3,2,1,0:T(8,128)(2,1)S(1)} %all-to-all-done.pay0_ref), channel_id=1, source_target_pairs={{0,4},{4,0},{1,5},{5,1},{2,6},{6,2},{3,7},{7,3},{8,12},{12,8},{9,1... | collective-permute-start | bytes 2359304 | tf_op jit(solution)/shard_map/ppermute | solution.py:359
  109.3 1.9 %collective-permute-done.23.pay1_ref = bf16[8,4,48,256]{3,2,1,0:T(8,128)(2,1)S(1)} collective-permute-done((bf16[8,4,48,256]{3,2,1,0:T(8,128)(2,1)S(1)}, bf16[8,4,48,256]{3,2,1,0:T(8,128)(2,1)S(1)}, u32[]{:S(2)}, u32[]{:S(2)}) %collective-permute-start.23) | collective-permute-done | bytes 786464 | tf_op jit(solution)/shard_map/ppermute | solution.py:359
  111.3 0.9 copy-done.3
  112.2 18.4 %attend.1 = bf16[12,192,128]{2,1,0:T(8,128)(2,1)} custom-call(s32[6]{0:T(128)} %stack.42.pos_ref, s32[6,6]{1,0:T(8,128)} %filt_ref.1, bf16[12,192,128]{2,1,0:T(8,128)(2,1)} %get-tuple-element.42.q_ref, f32[12,192,128]{2,1,0:T(8,128)} %get-tuple-element.43.gate_ref, bf16[12,768,256]{2,1,0:T(8,128)(2,1)} %get-tuple-element.44.kv_ref, ...), custom_call_target="tpu_custom_call" | custom-call | flops 8000000000 | bytes 10000000 | tf_op jit(solution)/shard_map/attend/pallas_call | solution.py:297
  (73 shorter events, 5.4 us)
Async XLA Ops:
  0.6 11.3 %copy-start.1 = (bf16[1024,128]{1,0:T(8,128)(2,1)S(1)}, bf16[1024,128]{1,0:T(8,128)(2,1)}, u32[]{:S(2)}) copy-start(bf16[1024,128]{1,0:T(8,128)(2,1)} %param.11) | copy-start | bytes 786436
  0.6 12.1 %copy-start.2 = (f32[128,4]{0,1:T(4,128)S(1)}, f32[128,4]{0,1:T(4,128)}, u32[]{:S(2)}) copy-start(f32[128,4]{0,1:T(4,128)} %param.13) | copy-start | bytes 6148
  4.1 11.6 %collective-permute-start = (bf16[384,256]{1,0:T(8,128)(2,1)}, bf16[384,256]{1,0:T(8,128)(2,1)S(1)}, u32[]{:S(2)}, u32[]{:S(2)}) collective-permute-start(bf16[384,256]{1,0:T(8,128)(2,1)} %get-tuple-element.24), channel_id=1, source_target_pairs={{2,0},{1,64},{0,128},{3,192},{6,4},{5,68},{4,132},{7,196},{10,8},{... | collective-permute-start | bytes 589832 | tf_op jit(solution)/shard_map/ppermute | solution.py:348
  15.8 27.5 %copy-start.7 = (bf16[384,256]{1,0:T(8,128)(2,1)}, bf16[384,256]{1,0:T(8,128)(2,1)S(1)}, u32[]{:S(2)}) copy-start(bf16[384,256]{1,0:T(8,128)(2,1)S(1)} %collective-permute-done.refs_0_) | copy-start | bytes 589828
  15.8 10.3 %collective-permute-start.4 = (bf16[384,256]{1,0:T(8,128)(2,1)S(1)}, bf16[384,256]{1,0:T(8,128)(2,1)S(1)}, u32[]{:S(2)}, u32[]{:S(2)}) collective-permute-start(bf16[384,256]{1,0:T(8,128)(2,1)S(1)} %collective-permute-done.refs_0_), channel_id=1, source_target_pairs={{0,16},{8,24},{16,0},{24,8},{1,17},{9,25},{17,1},{25,9},{2,18},{10... | collective-permute-start | bytes 589832 | tf_op jit(solution)/shard_map/ppermute | solution.py:325
  18.7 10.0 %collective-permute-start.8 = (bf16[384,256]{1,0:T(8,128)(2,1)S(1)}, bf16[384,256]{1,0:T(8,128)(2,1)S(1)}, u32[]{:S(2)}, u32[]{:S(2)}) collective-permute-start(bf16[384,256]{1,0:T(8,128)(2,1)S(1)} %collective-permute-done.refs_0_), channel_id=1, source_target_pairs={{0,4},{4,0},{1,5},{5,1},{2,6},{6,2},{3,7},{7,3},{8,12},{12,8},{9,1... | collective-permute-start | bytes 589832 | tf_op jit(solution)/shard_map/ppermute | solution.py:329
  24.6 7.1 %collective-permute-start.3 = (bf16[384,256]{1,0:T(8,128)(2,1)S(1)}, bf16[384,256]{1,0:T(8,128)(2,1)S(1)}, u32[]{:S(2)}, u32[]{:S(2)}) collective-permute-start(bf16[384,256]{1,0:T(8,128)(2,1)S(1)} %collective-permute-done.refs_0_), channel_id=1, source_target_pairs={{0,24},{8,0},{16,8},{24,16},{1,25},{9,1},{17,9},{25,17},{2,26},{10... | collective-permute-start | bytes 589832 | tf_op jit(solution)/shard_map/ppermute | solution.py:325
  25.4 7.8 %collective-permute-start.2 = (bf16[384,256]{1,0:T(8,128)(2,1)S(1)}, bf16[384,256]{1,0:T(8,128)(2,1)S(1)}, u32[]{:S(2)}, u32[]{:S(2)}) collective-permute-start(bf16[384,256]{1,0:T(8,128)(2,1)S(1)} %collective-permute-done.refs_0_), channel_id=1, source_target_pairs={{0,8},{8,16},{16,24},{24,0},{1,9},{9,17},{17,25},{25,1},{2,10},{10... | collective-permute-start | bytes 589832 | tf_op jit(solution)/shard_map/ppermute | solution.py:325
  26.1 7.1 %collective-permute-start.1 = (bf16[384,256]{1,0:T(8,128)(2,1)S(1)}, bf16[384,256]{1,0:T(8,128)(2,1)S(1)}, u32[]{:S(2)}, u32[]{:S(2)}) collective-permute-start(bf16[384,256]{1,0:T(8,128)(2,1)S(1)} %collective-permute-done.refs_0_), channel_id=1, source_target_pairs={{0,32},{32,0},{1,33},{33,1},{2,34},{34,2},{3,35},{35,3},{4,36},{36... | collective-permute-start | bytes 589832 | tf_op jit(solution)/shard_map/ppermute | solution.py:324
  26.1 17.2 %copy-start.8 = (bf16[384,256]{1,0:T(8,128)(2,1)}, bf16[384,256]{1,0:T(8,128)(2,1)S(1)}, u32[]{:S(2)}) copy-start(bf16[384,256]{1,0:T(8,128)(2,1)S(1)} %collective-permute-done.4.refs_4_) | copy-start | bytes 589828
  26.1 9.6 %collective-permute-start.12 = (bf16[384,256]{1,0:T(8,128)(2,1)S(1)}, bf16[384,256]{1,0:T(8,128)(2,1)S(1)}, u32[]{:S(2)}, u32[]{:S(2)}) collective-permute-start(bf16[384,256]{1,0:T(8,128)(2,1)S(1)} %collective-permute-done.4.refs_4_), channel_id=1, source_target_pairs={{0,4},{4,0},{1,5},{5,1},{2,6},{6,2},{3,7},{7,3},{8,12},{12,8},{9,1... | collective-permute-start | bytes 589832 | tf_op jit(solution)/shard_map/ppermute | solution.py:329
  28.7 14.6 %copy-start.9 = (bf16[384,256]{1,0:T(8,128)(2,1)}, bf16[384,256]{1,0:T(8,128)(2,1)S(1)}, u32[]{:S(2)}) copy-start(bf16[384,256]{1,0:T(8,128)(2,1)S(1)} %collective-permute-done.8.refs_8_) | copy-start | bytes 589828
  28.7 7.5 %collective-permute-start.7 = (bf16[384,256]{1,0:T(8,128)(2,1)S(1)}, bf16[384,256]{1,0:T(8,128)(2,1)S(1)}, u32[]{:S(2)}, u32[]{:S(2)}) collective-permute-start(bf16[384,256]{1,0:T(8,128)(2,1)S(1)} %collective-permute-done.4.refs_4_), channel_id=1, source_target_pairs={{0,32},{32,0},{1,33},{33,1},{2,34},{34,2},{3,35},{35,3},{4,36},{36... | collective-permute-start | bytes 589832 | tf_op jit(solution)/shard_map/ppermute | solution.py:327
  31.7 11.6 %copy-start.10 = (bf16[384,256]{1,0:T(8,128)(2,1)}, bf16[384,256]{1,0:T(8,128)(2,1)S(1)}, u32[]{:S(2)}) copy-start(bf16[384,256]{1,0:T(8,128)(2,1)S(1)} %collective-permute-done.3.refs_3_) | copy-start | bytes 589828
  31.7 6.9 %collective-permute-start.11 = (bf16[384,256]{1,0:T(8,128)(2,1)S(1)}, bf16[384,256]{1,0:T(8,128)(2,1)S(1)}, u32[]{:S(2)}, u32[]{:S(2)}) collective-permute-start(bf16[384,256]{1,0:T(8,128)(2,1)S(1)} %collective-permute-done.3.refs_3_), channel_id=1, source_target_pairs={{0,4},{4,0},{1,5},{5,1},{2,6},{6,2},{3,7},{7,3},{8,12},{12,8},{9,1... | collective-permute-start | bytes 589832 | tf_op jit(solution)/shard_map/ppermute | solution.py:329
  33.2 10.1 %copy-start.11 = (bf16[384,256]{1,0:T(8,128)(2,1)}, bf16[384,256]{1,0:T(8,128)(2,1)S(1)}, u32[]{:S(2)}) copy-start(bf16[384,256]{1,0:T(8,128)(2,1)S(1)} %collective-permute-done.2.refs_2_) | copy-start | bytes 589828
  33.2 7.2 %collective-permute-start.5 = (bf16[384,256]{1,0:T(8,128)(2,1)S(1)}, bf16[384,256]{1,0:T(8,128)(2,1)S(1)}, u32[]{:S(2)}, u32[]{:S(2)}) collective-permute-start(bf16[384,256]{1,0:T(8,128)(2,1)S(1)} %collective-permute-done.2.refs_2_), channel_id=1, source_target_pairs={{0,32},{32,0},{1,33},{33,1},{2,34},{34,2},{3,35},{35,3},{4,36},{36... | collective-permute-start | bytes 589832 | tf_op jit(solution)/shard_map/ppermute | solution.py:327
  33.2 8.6 %collective-permute-start.6 = (bf16[384,256]{1,0:T(8,128)(2,1)S(1)}, bf16[384,256]{1,0:T(8,128)(2,1)S(1)}, u32[]{:S(2)}, u32[]{:S(2)}) collective-permute-start(bf16[384,256]{1,0:T(8,128)(2,1)S(1)} %collective-permute-done.1.refs_1_), channel_id=1, source_target_pairs={{0,24},{8,0},{16,8},{24,16},{1,25},{9,1},{17,9},{25,17},{2,26},{10... | collective-permute-start | bytes 589832 | tf_op jit(solution)/shard_map/ppermute | solution.py:326
  35.7 6.4 %collective-permute-start.10 = (bf16[384,256]{1,0:T(8,128)(2,1)S(1)}, bf16[384,256]{1,0:T(8,128)(2,1)S(1)}, u32[]{:S(2)}, u32[]{:S(2)}) collective-permute-start(bf16[384,256]{1,0:T(8,128)(2,1)S(1)} %collective-permute-done.2.refs_2_), channel_id=1, source_target_pairs={{0,4},{4,0},{1,5},{5,1},{2,6},{6,2},{3,7},{7,3},{8,12},{12,8},{9,1... | collective-permute-start | bytes 589832 | tf_op jit(solution)/shard_map/ppermute | solution.py:329
  36.2 5.9 %collective-permute-start.9 = (bf16[384,256]{1,0:T(8,128)(2,1)S(1)}, bf16[384,256]{1,0:T(8,128)(2,1)S(1)}, u32[]{:S(2)}, u32[]{:S(2)}) collective-permute-start(bf16[384,256]{1,0:T(8,128)(2,1)S(1)} %collective-permute-done.1.refs_1_), channel_id=1, source_target_pairs={{0,4},{4,0},{1,5},{5,1},{2,6},{6,2},{3,7},{7,3},{8,12},{12,8},{9,1... | collective-permute-start | bytes 589832 | tf_op jit(solution)/shard_map/ppermute | solution.py:329
  38.7 3.5 %collective-permute-start.15 = (bf16[384,256]{1,0:T(8,128)(2,1)S(1)}, bf16[384,256]{1,0:T(8,128)(2,1)S(1)}, u32[]{:S(2)}, u32[]{:S(2)}) collective-permute-start(bf16[384,256]{1,0:T(8,128)(2,1)S(1)} %collective-permute-done.7.refs_7_), channel_id=1, source_target_pairs={{0,4},{4,0},{1,5},{5,1},{2,6},{6,2},{3,7},{7,3},{8,12},{12,8},{9,1... | collective-permute-start | bytes 589832 | tf_op jit(solution)/shard_map/ppermute | solution.py:329
  40.4 2.5 %collective-permute-start.13 = (bf16[384,256]{1,0:T(8,128)(2,1)S(1)}, bf16[384,256]{1,0:T(8,128)(2,1)S(1)}, u32[]{:S(2)}, u32[]{:S(2)}) collective-permute-start(bf16[384,256]{1,0:T(8,128)(2,1)S(1)} %collective-permute-done.5.refs_5_), channel_id=1, source_target_pairs={{0,4},{4,0},{1,5},{5,1},{2,6},{6,2},{3,7},{7,3},{8,12},{12,8},{9,1... | collective-permute-start | bytes 589832 | tf_op jit(solution)/shard_map/ppermute | solution.py:329
  41.9 1.4 %collective-permute-start.14 = (bf16[384,256]{1,0:T(8,128)(2,1)S(1)}, bf16[384,256]{1,0:T(8,128)(2,1)S(1)}, u32[]{:S(2)}, u32[]{:S(2)}) collective-permute-start(bf16[384,256]{1,0:T(8,128)(2,1)S(1)} %collective-permute-done.6.refs_6_), channel_id=1, source_target_pairs={{0,4},{4,0},{1,5},{5,1},{2,6},{6,2},{3,7},{7,3},{8,12},{12,8},{9,1... | collective-permute-start | bytes 589832 | tf_op jit(solution)/shard_map/ppermute | solution.py:329
  53.2 9.9 %collective-permute-start.18 = (bf16[48,256]{1,0:T(8,128)(2,1)}, bf16[48,256]{1,0:T(8,128)(2,1)S(1)}, u32[]{:S(2)}, u32[]{:S(2)}) collective-permute-start(bf16[48,256]{1,0:T(8,128)(2,1)} %get-tuple-element.32), channel_id=1, source_target_pairs={{0,0},{1,64},{2,128},{3,192},{4,4},{5,68},{6,132},{7,196},{8,8},{9... | collective-permute-start | bytes 73736 | tf_op jit(solution)/shard_map/ppermute | solution.py:352
  54.6 33.6 %collective-permute-start.17 = (bf16[12,192,128]{2,1,0:T(8,128)(2,1)}, bf16[12,192,128]{2,1,0:T(8,128)(2,1)S(1)}, u32[]{:S(2)}, u32[]{:S(2)}) collective-permute-start(bf16[12,192,128]{2,1,0:T(8,128)(2,1)} %get-tuple-element.33.own_ref), channel_id=1, source_target_pairs={{0,3},{1,0},{2,1},{3,2},{4,7},{5,4},{6,5},{7,6},{8,11},{9,8},{10,9... | collective-permute-start | bytes 1769480 | tf_op jit(solution)/shard_map/ppermute | solution.py:351
  63.1 25.1 %collective-permute-start.16 = (bf16[12,192,128]{2,1,0:T(8,128)(2,1)}, bf16[12,192,128]{2,1,0:T(8,128)(2,1)S(1)}, u32[]{:S(2)}, u32[]{:S(2)}) collective-permute-start(bf16[12,192,128]{2,1,0:T(8,128)(2,1)} %get-tuple-element.33.own_ref), channel_id=1, source_target_pairs={{0,1},{1,2},{2,3},{3,0},{4,5},{5,6},{6,7},{7,4},{8,9},{9,10},{10,1... | collective-permute-start | bytes 1769480 | tf_op jit(solution)/shard_map/ppermute | solution.py:351
  63.1 27.7 %collective-permute-start.19 = (bf16[12,192,128]{2,1,0:T(8,128)(2,1)}, bf16[12,192,128]{2,1,0:T(8,128)(2,1)S(1)}, u32[]{:S(2)}, u32[]{:S(2)}) collective-permute-start(bf16[12,192,128]{2,1,0:T(8,128)(2,1)} %get-tuple-element.33.own_ref), channel_id=1, source_target_pairs={{0,2},{1,3},{2,0},{3,1},{4,6},{5,7},{6,4},{7,5},{8,10},{9,11},{10,... | collective-permute-start | bytes 1769480 | tf_op jit(solution)/shard_map/ppermute | solution.py:353
  65.3 5.1 %collective-permute-start.22 = (bf16[48,256]{1,0:T(8,128)(2,1)S(1)}, bf16[48,256]{1,0:T(8,128)(2,1)S(1)}, u32[]{:S(2)}, u32[]{:S(2)}) collective-permute-start(bf16[48,256]{1,0:T(8,128)(2,1)S(1)} %collective-permute-done.18), channel_id=1, source_target_pairs={{0,192},{64,0},{128,64},{192,128},{1,193},{65,1},{129,65},{193,129... | collective-permute-start | bytes 73736 | tf_op jit(solution)/shard_map/ppermute | solution.py:333
  67.8 6.7 %collective-permute-start.21 = (bf16[48,256]{1,0:T(8,128)(2,1)S(1)}, bf16[48,256]{1,0:T(8,128)(2,1)S(1)}, u32[]{:S(2)}, u32[]{:S(2)}) collective-permute-start(bf16[48,256]{1,0:T(8,128)(2,1)S(1)} %collective-permute-done.18), channel_id=1, source_target_pairs={{0,128},{64,192},{128,0},{192,64},{1,129},{65,193},{129,1},{193,65... | collective-permute-start | bytes 73736 | tf_op jit(solution)/shard_map/ppermute | solution.py:333
  70.4 5.1 %collective-permute-start.20 = (bf16[48,256]{1,0:T(8,128)(2,1)S(1)}, bf16[48,256]{1,0:T(8,128)(2,1)S(1)}, u32[]{:S(2)}, u32[]{:S(2)}) collective-permute-start(bf16[48,256]{1,0:T(8,128)(2,1)S(1)} %collective-permute-done.18), channel_id=1, source_target_pairs={{0,64},{64,128},{128,192},{192,0},{1,65},{65,129},{129,193},{193,1... | collective-permute-start | bytes 73736 | tf_op jit(solution)/shard_map/ppermute | solution.py:333
  91.8 12.6 %all-to-all-start = ((bf16[8,4,48,256]{3,2,1,0:T(8,128)(2,1)}), bf16[8,4,48,256]{3,2,1,0:T(8,128)(2,1)S(1)}, u32[]{:S(2)}, u32[]{:S(2)}) async-start(bf16[8,4,48,256]{3,2,1,0:T(8,128)(2,1)} %broadcast_in_dim.2), calls=%async_computation | async-start | bytes 1572864 | tf_op jit(solution)/shard_map/all_to_all | solution.py:357
  104.4 6.9 %collective-permute-start.23 = (bf16[8,4,48,256]{3,2,1,0:T(8,128)(2,1)S(1)}, bf16[8,4,48,256]{3,2,1,0:T(8,128)(2,1)S(1)}, u32[]{:S(2)}, u32[]{:S(2)}) collective-permute-start(bf16[8,4,48,256]{3,2,1,0:T(8,128)(2,1)S(1)} %all-to-all-done.pay0_ref), channel_id=1, source_target_pairs={{0,4},{4,0},{1,5},{5,1},{2,6},{6,2},{3,7},{7,3},{8,12},{12,8},{9,1... | collective-permute-start | bytes 2359304 | tf_op jit(solution)/shard_map/ppermute | solution.py:359
  (16 other events, 68.1 us)
